TPU v7x, 128 devices: a whole 4x4x4 slice. The times are simulated.
128 devices in a mesh: gx: 8 (over y, core), gy: 16 (over z, x).
Axes of the slice: x: 4, y: 4, z: 4, core: 2. Of those that a mesh axis runs over, the one named last changes fastest.
Arguments:
- atmosphere_surface_fields: float32 [20, 2097152], P(None, ('gx', 'gy')), may hold values from -6 to 6
- ocean_surface_fields: float32 [20, 2097152], P(None, ('gx', 'gy')), may hold values from -6 to 6
- atm_area: float32 [2097152], P(('gx', 'gy')), may hold values from 1 to 4
- ocn_area: float32 [2097152], P(('gx', 'gy')), may hold values from 1 to 4
- send_atm: int32 [128, 9, 24], P(('gx', 'gy')), may hold values from -1 to 127, as said below
- send_ocn: int32 [128, 9, 24], P(('gx', 'gy')), may hold values from -1 to 127, as said below
- atm_ref: int32 [8388608], P(('gx', 'gy')), may hold values from 0 to 27647, as said below
- ocn_ref: int32 [8388608], P(('gx', 'gy')), may hold values from 0 to 27647, as said below
- cell_area: float32 [8388608], P(('gx', 'gy')), may hold values from 0.1 to 1
- cell_mask: int32 [8388608], P(('gx', 'gy')), may hold values 0 or 1
- cell_count: int32 [128], P(('gx', 'gy')), may hold values from 8192 to 65536, as said below
Outputs:
- atm_flux: float32 [18, 2097152], P(None, ('gx', 'gy'))
- ocn_flux: float32 [18, 2097152], P(None, ('gx', 'gy'))
Inputs may be any that keep to these rules, and one draw needn't show every extreme that they name: `send_atm`: in each row [s, n] the first one to 24 entries are distinct blocks of device s and the rest are -1; rows [s, 4] and [s, 8] are full, and some owner receives full rows from all its neighbours. `send_ocn`: in each row [s, n] the first one to 24 entries are distinct blocks of device s and the rest are -1; rows [s, 4] and [s, 8] are full, and some owner receives full rows from all its neighbours. `atm_ref`: every cell, live or not, names a slot whose entry in send_atm is not -1; the 32 cells of each aligned group of 32 cells name the same slot. `ocn_ref`: every cell, live or not, names a slot whose entry in send_ocn is not -1; the 32 cells of each aligned group of 32 cells name the same slot. `cell_count`: some owner has all 65536 cells live.
All inputs are finite; a program needn't handle non-finite values. No bound on the sum of `cell_mask` on one device may be relied on, other than what follows from the above.
Results may differ from a plain program's by a relative error of at most 0.0003.
Values sent between devices are 32-bit elements; how exact they have to be, the bound alone decides.
No kernel may reach another device: no remote copies, remote signals or barrier semaphores. Data moves between devices by JAX's collectives and lax.ppermute only.
A program may use at most 192 MiB of HBM per device.

v0:
```python
import math

import jax
import jax.numpy as jnp
from jax import lax
from jax.sharding import PartitionSpec as P

GRP = 32
ITERS = 6


KAPPA = 0.4
GRAVITY = 9.8
FLUX_SCALE = 25.0
HIGHEST = lax.Precision.HIGHEST


def from_behind(value, axis, steps):
    count = lax.axis_size(axis)
    pairs = [(source, (source + steps) % count) for source in range(count)]
    return lax.ppermute(value, axis, pairs)


def surface_flux(atmos, ocean):
    shear_x = 6.0 * atmos[0] - 0.3 * ocean[0]
    shear_y = 6.0 * atmos[1] - 0.3 * ocean[1]
    wind_speed = jnp.sqrt(shear_x * shear_x + shear_y * shear_y + 0.25 + 0.1 * atmos[5] * atmos[5])
    temp_diff = 3.0 * (atmos[2] - ocean[2])
    humid_diff = 0.002 * (atmos[3] - ocean[3])
    height = 10.0 * jnp.exp(0.3 * atmos[4])
    log_moment = jnp.log(height * 10000.0) - 0.5 * ocean[4]
    log_heat = jnp.log(height * 10000.0) - 0.5 * ocean[5]
    root_moment = KAPPA / log_moment
    root_heat = KAPPA / log_heat
    for sweep in range(ITERS):
        friction = root_moment * wind_speed
        buoyancy = root_heat * (temp_diff / 290.0 + 0.61 * humid_diff)
        stability = jnp.clip(
            KAPPA * GRAVITY * height * buoyancy / (friction * friction), -10.0, 3.0
        )
        unstable = jnp.sqrt(jnp.sqrt(1.0 - 16.0 * jnp.minimum(stability, 0.0)))
        psi_moment = jnp.where(
            stability > 0.0,
            -5.0 * stability,
            2.0 * jnp.log((1.0 + unstable) / 2.0)
            + jnp.log((1.0 + unstable * unstable) / 2.0)
            - 2.0 * jnp.arctan(unstable)
            + jnp.pi / 2.0,
        )
        psi_heat = jnp.where(
            stability > 0.0, -5.0 * stability, 2.0 * jnp.log((1.0 + unstable * unstable) / 2.0)
        )
        root_moment = 0.5 * root_moment + 0.5 * KAPPA / (log_moment - psi_moment)
        root_heat = 0.5 * root_heat + 0.5 * KAPPA / (log_heat - psi_heat)
    drag = FLUX_SCALE * root_moment * root_moment * wind_speed
    transfer = FLUX_SCALE * root_moment * root_heat * wind_speed
    leading = jnp.stack(
        [drag * shear_x, drag * shear_y, transfer * temp_diff, 500.0 * transfer * humid_diff]
    )
    tracer = transfer[None, :] * (atmos[6:] - ocean[6:])
    return jnp.concatenate([leading, tracer], axis=0)


def pack_blocks(fields, block_ids):
    nblocks = fields.shape[1] // 128
    blocks = fields.reshape(fields.shape[0], nblocks, 128)
    flat_ids = block_ids.reshape(-1)
    picked = jnp.take(blocks, jnp.maximum(flat_ids, 0), axis=1)
    picked = jnp.where((flat_ids >= 0)[None, :, None], picked, 0.0)
    return picked.reshape(fields.shape[0], 3, 3, block_ids.shape[1], 128)


def unpack_blocks(returned, block_ids, nblocks):
    flat_ids = block_ids.reshape(-1)
    selector = (flat_ids[None, :] == jnp.arange(nblocks, dtype=jnp.int32)[:, None]).astype(
        jnp.float32
    )
    summed = jnp.einsum("bs,fsl->fbl", selector, returned, precision=HIGHEST)
    return summed.reshape(returned.shape[0], nblocks * 128)


def group_tables(refs):
    grouped = refs.reshape(-1, GRP)
    return (grouped[:, 0] // 128, grouped % 128)


def blocked_groups(ngroups):
    return math.gcd(ngroups, 256)


def gather_cell_rows(slabs, group_slot_index, group_lane_index):
    field_count = slabs.shape[0]
    ngroups = group_slot_index.shape[0]
    step_size = blocked_groups(ngroups)
    blocks = jnp.take(slabs, group_slot_index, axis=1)
    blocks = blocks.reshape(field_count, ngroups // step_size, step_size, 128).transpose(1, 0, 2, 3)
    lanes = group_lane_index.reshape(ngroups // step_size, step_size, GRP)
    lane_ids = jnp.arange(128, dtype=jnp.int32)

    def select(item):
        block_part, lane_part = item
        onehot = (lane_part[:, :, None] == lane_ids[None, None, :]).astype(jnp.float32)
        return jnp.einsum("fgl,gcl->fgc", block_part, onehot, precision=HIGHEST)

    cells = lax.map(select, (blocks, lanes))
    return cells.transpose(1, 0, 2, 3).reshape(field_count, ngroups * GRP)


def scatter_cell_rows(area_weighted_flux, group_slot_index, group_lane_index, slot_count):
    flux_count = area_weighted_flux.shape[0]
    ngroups = group_slot_index.shape[0]
    step_size = blocked_groups(ngroups)
    values = area_weighted_flux.reshape(flux_count, ngroups // step_size, step_size, GRP).transpose(
        1, 0, 2, 3
    )
    lanes = group_lane_index.reshape(ngroups // step_size, step_size, GRP)
    lane_ids = jnp.arange(128, dtype=jnp.int32)

    def spread(item):
        value_part, lane_part = item
        onehot = (lane_part[:, :, None] == lane_ids[None, None, :]).astype(jnp.float32)
        return jnp.einsum("fgc,gcl->fgl", value_part, onehot, precision=HIGHEST)

    per_group = (
        lax.map(spread, (values, lanes)).transpose(1, 0, 2, 3).reshape(flux_count, ngroups, 128)
    )
    slot_lookup_table = (
        group_slot_index[None, :] == jnp.arange(slot_count, dtype=jnp.int32)[:, None]
    ).astype(jnp.float32)
    return jnp.einsum("sg,fgl->fsl", slot_lookup_table, per_group, precision=HIGHEST)


def route_slots(atmos_part, ocean_part, direction):
    atmos_slabs = []
    ocean_slabs = []
    for neighbor in range(9):
        offset_x = neighbor // 3 - 1
        offset_y = neighbor % 3 - 1
        slab_pair = (
            atmos_part[:, offset_x + 1, offset_y + 1],
            ocean_part[:, offset_x + 1, offset_y + 1],
        )
        if offset_x != 0:
            slab_pair = from_behind((slab_pair[0], slab_pair[1]), "gx", direction * offset_x)
        if offset_y != 0:
            slab_pair = from_behind((slab_pair[0], slab_pair[1]), "gy", direction * offset_y)
        atmos_slabs.append(slab_pair[0])
        ocean_slabs.append(slab_pair[1])
    atmos_shape = (atmos_part.shape[0], 3, 3) + atmos_part.shape[3:]
    ocean_shape = (ocean_part.shape[0], 3, 3) + ocean_part.shape[3:]
    return (
        jnp.stack(atmos_slabs, axis=1).reshape(atmos_shape),
        jnp.stack(ocean_slabs, axis=1).reshape(ocean_shape),
    )


def shards(
    atmosphere_surface_fields,
    ocean_surface_fields,
    atm_area,
    ocn_area,
    send_atm,
    send_ocn,
    atm_ref,
    ocn_ref,
    cell_area,
    cell_mask,
    cell_count,
):
    field_count = atmosphere_surface_fields.shape[0]
    atmosphere_index_list = send_atm[0]
    ocean_index_list = send_ocn[0]
    lane_width = atmosphere_index_list.shape[1]
    slot_count = 9 * lane_width
    atm_out = pack_blocks(atmosphere_surface_fields, atmosphere_index_list)
    ocn_out = pack_blocks(ocean_surface_fields, ocean_index_list)
    atmosphere_input, ocean_input = route_slots(atm_out, ocn_out, 1)
    atmosphere_slot_index, atmosphere_lane_index = group_tables(atm_ref)
    ocean_slot_index, ocean_lane_index = group_tables(ocn_ref)
    atmosphere_cell_rows = gather_cell_rows(
        atmosphere_input.reshape(field_count, slot_count, 128),
        atmosphere_slot_index,
        atmosphere_lane_index,
    )
    ocean_cell_rows = gather_cell_rows(
        ocean_input.reshape(field_count, slot_count, 128), ocean_slot_index, ocean_lane_index
    )
    fluxes = surface_flux(atmosphere_cell_rows, ocean_cell_rows)
    local_index = jnp.arange(atm_ref.shape[0], dtype=jnp.int32)
    weight = jnp.where((local_index < cell_count[0]) & (cell_mask == 1), cell_area, 0.0)
    area_weighted_flux = fluxes * weight[None, :]
    flux_count = fluxes.shape[0]
    atmosphere_returned_rows = scatter_cell_rows(
        area_weighted_flux, atmosphere_slot_index, atmosphere_lane_index, slot_count
    )
    ocean_returned_rows = scatter_cell_rows(
        area_weighted_flux, ocean_slot_index, ocean_lane_index, slot_count
    )
    back_shape = (flux_count, 3, 3, lane_width, 128)
    atmosphere_return_rows, ocean_return_rows = route_slots(
        atmosphere_returned_rows.reshape(back_shape), ocean_returned_rows.reshape(back_shape), -1
    )
    atm_sum = unpack_blocks(
        atmosphere_return_rows.reshape(flux_count, slot_count, 128),
        atmosphere_index_list,
        atmosphere_surface_fields.shape[1] // 128,
    )
    ocn_sum = unpack_blocks(
        ocean_return_rows.reshape(flux_count, slot_count, 128),
        ocean_index_list,
        ocean_surface_fields.shape[1] // 128,
    )
    return (atm_sum / atm_area[None, :], ocn_sum / ocn_area[None, :])


def solution(mesh):
    in_specs = (
        P(None, ("gx", "gy")),
        P(None, ("gx", "gy")),
        P(("gx", "gy")),
        P(("gx", "gy")),
        P(("gx", "gy"), None, None),
        P(("gx", "gy"), None, None),
        P(("gx", "gy")),
        P(("gx", "gy")),
        P(("gx", "gy")),
        P(("gx", "gy")),
        P(("gx", "gy")),
    )
    out_specs = (P(None, ("gx", "gy")), P(None, ("gx", "gy")))
    return jax.shard_map(shards, mesh=mesh, in_specs=in_specs, out_specs=out_specs, check_vma=False)
```

profile of v0, /device:TPU:1, one launch (start us, length us, event | category | flops | bytes accessed | tf_op | source)
XLA Modules:
  0.0 670.3 jit_solution(15433128049054620024)
XLA Ops:
  18.5 6.0 collective-permute-start.5
  63.7 8.8 %collective-permute-done.4 = f32[20,24,128]{2,1,0:T(8,128)S(1)} collective-permute-done((f32[20,24,128]{2,1,0:T(8,128)}, f32[20,24,128]{2,1,0:T(8,128)S(1)}, u32[]{:S(2)}, u32[]{:S(2)}) %collective-permute-start.4) | collective-permute-done | bytes 245792 | tf_op jit(solution)/shard_map/ppermute | solution.py:21
  88.8 23.8 %gather_fusion.1 = f32[2048,20,128]{2,1,0:T(8,128)} fusion(f32[20,216,128]{2,0,1:T(8,128)S(1)} %copy.193, s32[2048]{0:T(1024)S(1)} %get-tuple-element.246), kind=kCustom, calls=%fused_computation.1.clone | custom fusion | bytes 41951232 | tf_op jit(solution)/shard_map/jit(_take)/gather | solution.py:95
  112.7 19.2 %broadcast_select_fusion.1 = f32[2048,20,128]{2,1,0:T(8,128)} fusion(f32[2048,20,128]{2,1,0:T(8,128)} %gather_fusion.1, pred[2048]{0:T(1024)(128)(4,1)S(1)} %get-tuple-element.206), kind=kLoop, calls=%fused_computation.47 | loop fusion | flops 5242880 | bytes 41945088 | tf_op jit(solution)/shard_map/jit(_take)/select_n | solution.py:95
  134.8 81.1 %while.44 = (s32[]{:T(128)}, f32[8,20,256,32]{2,3,0,1:T(8,128)}, s32[8,256,32]{2,1,0:T(8,128)}, f32[8,20,256,128]{3,1,2,0:T(8,128)}, s32[]{:T(128)}) while((s32[]{:T(128)}, f32[8,20,256,32]{2,3,0,1:T(8,128)}, s32[8,256,32]{2,1,0:T(8,128)}, f32[8,20,256,128]{3,1,2,0:T(8,128)}, s32[]{:T(128)}) %tuple.132), condition=%wide.region_1.4_spmd.clone, body=%wide.region_0.3_spmd.clone.sunk | while | flops 252706816 | bytes 6521921 | solution.py:105
  135.7 5.4 fusion.141
  145.9 5.4 fusion.141
  156.0 5.4 fusion.141
  166.2 5.4 fusion.141
  176.3 5.4 fusion.141
  186.5 5.4 fusion.141
  196.6 5.4 fusion.141
  237.9 23.8 %gather_fusion.3 = f32[2048,20,128]{2,1,0:T(8,128)} fusion(f32[20,216,128]{2,0,1:T(8,128)S(1)} %copy.205, s32[2048]{0:T(1024)S(1)} %get-tuple-element.247), kind=kCustom, calls=%fused_computation.3.clone | custom fusion | bytes 41951232 | tf_op jit(solution)/shard_map/jit(_take)/gather | solution.py:95
  261.8 19.2 %broadcast_select_fusion = f32[2048,20,128]{2,1,0:T(8,128)} fusion(f32[2048,20,128]{2,1,0:T(8,128)} %gather_fusion.3, pred[2048]{0:T(1024)(128)(4,1)S(1)} %get-tuple-element.204), kind=kLoop, calls=%fused_computation.46 | loop fusion | flops 5242880 | bytes 41945088 | tf_op jit(solution)/shard_map/jit(_take)/select_n | solution.py:95
  284.1 80.9 %while.45 = (s32[]{:T(128)}, f32[8,20,256,32]{2,3,0,1:T(8,128)}, s32[8,256,32]{2,1,0:T(8,128)}, f32[8,20,256,128]{3,1,2,0:T(8,128)}, s32[]{:T(128)}) while((s32[]{:T(128)}, f32[8,20,256,32]{2,3,0,1:T(8,128)}, s32[8,256,32]{2,1,0:T(8,128)}, f32[8,20,256,128]{3,1,2,0:T(8,128)}, s32[]{:T(128)}) %tuple.133), condition=%wide.region_3.6_spmd.clone, body=%wide.region_2.5_spmd.clone.sunk | while | flops 252706816 | bytes 6521921 | solution.py:105
  285.0 5.4 fusion.143
  295.1 5.4 fusion.143
  315.3 5.4 fusion.143
  325.4 5.4 fusion.143
  355.8 5.4 fusion.143
  365.0 7.1 %fusion.94 = (f32[8,256,32]{1,2,0:T(8,128)S(1)}, f32[1,8,256,32]{2,3,1,0:T(8,128)S(1)}, f32[1,8,256,32]{2,3,1,0:T(8,128)S(1)}, f32[1,8,256,32]{2,3,1,0:T(8,128)S(1)}) fusion(f32[20,8,256,32]{2,3,1,0:T(8,128)} %bitcast.510, f32[20,8,256,32]{2,3,1,0:T(8,128)} %bitcast.518), kind=kLoop, calls=%fused_computation.142 | loop fusion | flops 14548992 | bytes 4194304 | tf_op jit(solution)/shard_map/mul | solution.py:56
  372.1 6.8 %multiply_dynamic-update-slice_fusion.3 = (f32[18,8,256,32]{2,3,1,0:T(8,128)S(1)}, f32[1,8,256,32]{2,3,1,0:T(8,128)S(1)}, f32[1,8,256,32]{2,3,1,0:T(8,128)S(1)}, f32[1,8,256,32]{2,3,1,0:T(8,128)S(1)}) fusion(f32[20,8,256,32]{2,3,1,0:T(8,128)} %bitcast.519, f32[20,8,256,32]{2,3,1,0:T(8,128)} %bitcast.511, f32[1,8,256,32]{2,3,1,0:T(8,128)S(1)} %get-tuple-element.199, ...), kind=kLoop, calls=%fused_computation.177 | loop fusion | flops 13565951 | bytes 3407872
  389.9 15.3 %copy.208 = f32[8,18,256,32]{3,1,2,0:T(8,128)} copy(f32[8,18,256,32]{2,3,0,1:T(8,128)} %multiply_bitcast_fusion) | data formatting | bytes 9437184
  405.2 10.4 %broadcast.2525.clone.1 = f32[8,18,256,128]{3,1,2,0:T(8,128)} broadcast(f32[]{:T(128)} %constant.143.clone.1), dimensions={} | broadcast | bytes 18874372 | tf_op jit(solution)/shard_map/broadcast.21
  415.5 56.4 %while.47 = (s32[]{:T(128)}, f32[8,18,256,128]{3,1,2,0:T(8,128)}, s32[8,256,32]{2,1,0:T(8,128)}, f32[8,18,256,32]{3,1,2,0:T(8,128)}, s32[]{:T(128)}) while((s32[]{:T(128)}, f32[8,18,256,128]{3,1,2,0:T(8,128)}, s32[8,256,32]{2,1,0:T(8,128)}, f32[8,18,256,32]{3,1,2,0:T(8,128)}, s32[]{:T(128)}) %tuple.128), condition=%wide.region_7.10_spmd.clone, body=%wide.region_6.9_spmd.clone.sunk | while | flops 227540992 | bytes 6390849 | solution.py:125
  416.5 6.1 bitcast_dynamic-update-slice_fusion.37
  423.5 6.1 bitcast_dynamic-update-slice_fusion.37
  430.5 6.1 bitcast_dynamic-update-slice_fusion.37
  437.6 6.1 bitcast_dynamic-update-slice_fusion.37
  444.6 6.2 bitcast_dynamic-update-slice_fusion.37
  451.7 6.1 bitcast_dynamic-update-slice_fusion.37
  458.7 6.1 bitcast_dynamic-update-slice_fusion.37
  465.8 6.1 bitcast_dynamic-update-slice_fusion.37
  471.9 18.1 %fusion.38 = f32[18,128,216]{1,2,0:T(8,128)S(1)} fusion(f32[18,2048,128]{2,0,1:T(8,128)} %bitcast.506, s32[2048]{0:T(1024)S(1)} %get-tuple-element.205), kind=kOutput, calls=%fused_computation.42 | convolution fusion | flops 12231032832 | bytes 20873216 | tf_op jit(solution)/shard_map/sg,fgl->fsl/dot_general | solution.py:130
  501.8 10.4 %broadcast.2525.clone = f32[8,18,256,128]{3,1,2,0:T(8,128)} broadcast(f32[]{:T(128)} %constant.143.clone.1), dimensions={} | broadcast | bytes 18874372 | tf_op jit(solution)/shard_map/broadcast.21
  512.2 56.5 %while.46 = (s32[]{:T(128)}, f32[8,18,256,128]{3,1,2,0:T(8,128)}, s32[8,256,32]{2,1,0:T(8,128)}, f32[8,18,256,32]{3,1,2,0:T(8,128)}, s32[]{:T(128)}) while((s32[]{:T(128)}, f32[8,18,256,128]{3,1,2,0:T(8,128)}, s32[8,256,32]{2,1,0:T(8,128)}, f32[8,18,256,32]{3,1,2,0:T(8,128)}, s32[]{:T(128)}) %tuple.131), condition=%wide.region_5.8_spmd.clone, body=%wide.region_4.7_spmd.clone.sunk | while | flops 227540992 | bytes 6390849 | solution.py:125
  513.3 6.1 bitcast_dynamic-update-slice_fusion.36
  520.3 6.1 bitcast_dynamic-update-slice_fusion.36
  527.4 6.1 bitcast_dynamic-update-slice_fusion.36
  534.4 6.1 bitcast_dynamic-update-slice_fusion.36
  541.5 6.2 bitcast_dynamic-update-slice_fusion.36
  548.6 6.1 bitcast_dynamic-update-slice_fusion.36
  555.6 6.1 bitcast_dynamic-update-slice_fusion.36
  562.6 6.1 bitcast_dynamic-update-slice_fusion.36
  568.8 17.1 %fusion.40 = f32[18,128,216]{1,2,0:T(8,128)S(1)} fusion(f32[18,2048,128]{2,0,1:T(8,128)} %bitcast.507, s32[2048]{0:T(1024)S(1)} %copy-done.23), kind=kOutput, calls=%fused_computation.44 | convolution fusion | flops 12231032832 | bytes 20873216 | tf_op jit(solution)/shard_map/sg,fgl->fsl/dot_general | solution.py:130
  587.1 8.3 %collective-permute-done.37 = f32[18,24,128]{2,1,0:T(8,128)S(1)} collective-permute-done((f32[18,24,128]{2,1,0:T(8,128)}, f32[18,24,128]{2,1,0:T(8,128)S(1)}, u32[]{:S(2)}, u32[]{:S(2)}) %collective-permute-start.37) | collective-permute-done | bytes 221216 | tf_op jit(solution)/shard_map/ppermute | solution.py:21
  601.0 5.4 collective-permute-done.40
  611.2 8.9 %collective-permute-done.44 = f32[18,24,128]{2,1,0:T(8,128)S(1)} collective-permute-done((f32[18,24,128]{2,1,0:T(8,128)S(1)}, f32[18,24,128]{2,1,0:T(8,128)S(1)}, u32[]{:S(2)}, u32[]{:S(2)}) %collective-permute-start.44) | collective-permute-done | bytes 221216 | tf_op jit(solution)/shard_map/ppermute | solution.py:21
  (334 shorter events, 295.7 us)
Async XLA Ops:
  11.6 30.8 %collective-permute-start = (f32[20,24,128]{2,1,0:T(8,128)}, f32[20,24,128]{2,1,0:T(8,128)}, u32[]{:S(2)}, u32[]{:S(2)}) collective-permute-start(f32[20,24,128]{2,1,0:T(8,128)} %bitcast.480), channel_id=1, source_target_pairs={{0,112},{16,0},{32,16},{48,32},{64,48},{80,64},{96,80},{112,96},{1... | collective-permute-start | bytes 737288 | tf_op jit(solution)/shard_map/ppermute | solution.py:21
  13.8 48.9 %collective-permute-start.2 = (f32[20,24,128]{2,1,0:T(8,128)}, f32[20,24,128]{2,1,0:T(8,128)}, u32[]{:S(2)}, u32[]{:S(2)}) collective-permute-start(f32[20,24,128]{2,1,0:T(8,128)} %bitcast.479), channel_id=1, source_target_pairs={{0,112},{16,0},{32,16},{48,32},{64,48},{80,64},{96,80},{112,96},{1... | collective-permute-start | bytes 737288 | tf_op jit(solution)/shard_map/ppermute | solution.py:21
  17.0 42.7 %collective-permute-start.3 = (f32[20,24,128]{2,1,0:T(8,128)}, f32[20,24,128]{2,1,0:T(8,128)}, u32[]{:S(2)}, u32[]{:S(2)}) collective-permute-start(f32[20,24,128]{2,1,0:T(8,128)} %bitcast.478), channel_id=1, source_target_pairs={{0,112},{16,0},{32,16},{48,32},{64,48},{80,64},{96,80},{112,96},{1... | collective-permute-start | bytes 737288 | tf_op jit(solution)/shard_map/ppermute | solution.py:21
  18.5 54.1 %collective-permute-start.5 = (f32[20,24,128]{2,1,0:T(8,128)}, f32[20,24,128]{2,1,0:T(8,128)}, u32[]{:S(2)}, u32[]{:S(2)}) collective-permute-start(f32[20,24,128]{2,1,0:T(8,128)} %bitcast.477), channel_id=1, source_target_pairs={{0,15},{1,0},{2,1},{3,2},{4,3},{5,4},{6,5},{7,6},{8,7},{9,8},{10,9... | collective-permute-start | bytes 737288 | tf_op jit(solution)/shard_map/ppermute | solution.py:21
  25.1 49.0 %collective-permute-start.6 = (f32[20,24,128]{2,1,0:T(8,128)}, f32[20,24,128]{2,1,0:T(8,128)}, u32[]{:S(2)}, u32[]{:S(2)}) collective-permute-start(f32[20,24,128]{2,1,0:T(8,128)} %bitcast.476), channel_id=1, source_target_pairs={{0,1},{1,2},{2,3},{3,4},{4,5},{5,6},{6,7},{7,8},{8,9},{9,10},{10,1... | collective-permute-start | bytes 737288 | tf_op jit(solution)/shard_map/ppermute | solution.py:21
  42.4 19.3 %collective-permute-start.1 = (f32[20,24,128]{2,1,0:T(8,128)}, f32[20,24,128]{2,1,0:T(8,128)}, u32[]{:S(2)}, u32[]{:S(2)}) collective-permute-start(f32[20,24,128]{2,1,0:T(8,128)} %collective-permute-done), channel_id=1, source_target_pairs={{0,15},{1,0},{2,1},{3,2},{4,3},{5,4},{6,5},{7,6},{8,7},{9,8},{10,9... | collective-permute-start | bytes 737288 | tf_op jit(solution)/shard_map/ppermute | solution.py:21
  59.8 13.4 %collective-permute-start.7 = (f32[20,24,128]{2,1,0:T(8,128)}, f32[20,24,128]{2,1,0:T(8,128)S(1)}, u32[]{:S(2)}, u32[]{:S(2)}) collective-permute-start(f32[20,24,128]{2,1,0:T(8,128)} %bitcast.475), channel_id=1, source_target_pairs={{0,16},{16,32},{32,48},{48,64},{64,80},{80,96},{96,112},{112,0},{1... | collective-permute-start | bytes 737288 | tf_op jit(solution)/shard_map/ppermute | solution.py:21
  61.7 10.9 %collective-permute-start.4 = (f32[20,24,128]{2,1,0:T(8,128)}, f32[20,24,128]{2,1,0:T(8,128)S(1)}, u32[]{:S(2)}, u32[]{:S(2)}) collective-permute-start(f32[20,24,128]{2,1,0:T(8,128)} %collective-permute-done.3), channel_id=1, source_target_pairs={{0,1},{1,2},{2,3},{3,4},{4,5},{5,6},{6,7},{7,8},{8,9},{9,10},{10,1... | collective-permute-start | bytes 737288 | tf_op jit(solution)/shard_map/ppermute | solution.py:21
  62.7 17.2 %collective-permute-start.9 = (f32[20,24,128]{2,1,0:T(8,128)S(1)}, f32[20,24,128]{2,1,0:T(8,128)S(1)}, u32[]{:S(2)}, u32[]{:S(2)}) collective-permute-start(f32[20,24,128]{2,1,0:T(8,128)S(1)} %bitcast.546), channel_id=1, source_target_pairs={{0,16},{16,32},{32,48},{48,64},{64,80},{80,96},{96,112},{112,0},{1... | collective-permute-start | bytes 737288 | tf_op jit(solution)/shard_map/ppermute | solution.py:21
  72.6 5.4 collective-permute-start.10
  72.6 12.1 %collective-permute-start.12 = (f32[20,24,128]{2,1,0:T(8,128)S(1)}, f32[20,24,128]{2,1,0:T(8,128)}, u32[]{:S(2)}, u32[]{:S(2)}) collective-permute-start(f32[20,24,128]{2,1,0:T(8,128)S(1)} %bitcast.545), channel_id=1, source_target_pairs={{0,112},{16,0},{32,16},{48,32},{64,48},{80,64},{96,80},{112,96},{1... | collective-permute-start | bytes 737288 | tf_op jit(solution)/shard_map/ppermute | solution.py:21
  73.1 6.7 collective-permute-start.8
  74.2 146.6 %collective-permute-start.14 = (f32[20,24,128]{2,1,0:T(8,128)}, f32[20,24,128]{2,1,0:T(8,128)}, u32[]{:S(2)}, u32[]{:S(2)}) collective-permute-start(f32[20,24,128]{2,1,0:T(8,128)} %bitcast.471), channel_id=1, source_target_pairs={{0,112},{16,0},{32,16},{48,32},{64,48},{80,64},{96,80},{112,96},{1... | collective-permute-start | bytes 737288 | tf_op jit(solution)/shard_map/ppermute | solution.py:21
  78.0 138.0 %collective-permute-start.15 = (f32[20,24,128]{2,1,0:T(8,128)}, f32[20,24,128]{2,1,0:T(8,128)}, u32[]{:S(2)}, u32[]{:S(2)}) collective-permute-start(f32[20,24,128]{2,1,0:T(8,128)} %bitcast.470), channel_id=1, source_target_pairs={{0,112},{16,0},{32,16},{48,32},{64,48},{80,64},{96,80},{112,96},{1... | collective-permute-start | bytes 737288 | tf_op jit(solution)/shard_map/ppermute | solution.py:21
  79.8 8.4 %collective-permute-start.11 = (f32[20,24,128]{2,1,0:T(8,128)S(1)}, f32[20,24,128]{2,1,0:T(8,128)S(1)}, u32[]{:S(2)}, u32[]{:S(2)}) collective-permute-start(f32[20,24,128]{2,1,0:T(8,128)S(1)} %collective-permute-done.10), channel_id=1, source_target_pairs={{0,1},{1,2},{2,3},{3,4},{4,5},{5,6},{6,7},{7,8},{8,9},{9,10},{10,1... | collective-permute-start | bytes 737288 | tf_op jit(solution)/shard_map/ppermute | solution.py:21
  79.9 148.5 %collective-permute-start.17 = (f32[20,24,128]{2,1,0:T(8,128)}, f32[20,24,128]{2,1,0:T(8,128)}, u32[]{:S(2)}, u32[]{:S(2)}) collective-permute-start(f32[20,24,128]{2,1,0:T(8,128)} %bitcast.469), channel_id=1, source_target_pairs={{0,15},{1,0},{2,1},{3,2},{4,3},{5,4},{6,5},{7,6},{8,7},{9,8},{10,9... | collective-permute-start | bytes 737288 | tf_op jit(solution)/shard_map/ppermute | solution.py:21
  84.7 137.1 %collective-permute-start.19 = (f32[20,24,128]{2,1,0:T(8,128)}, f32[20,24,128]{2,1,0:T(8,128)}, u32[]{:S(2)}, u32[]{:S(2)}) collective-permute-start(f32[20,24,128]{2,1,0:T(8,128)} %bitcast.467), channel_id=1, source_target_pairs={{0,16},{16,32},{32,48},{48,64},{64,80},{80,96},{96,112},{112,0},{1... | collective-permute-start | bytes 737288 | tf_op jit(solution)/shard_map/ppermute | solution.py:21
  88.2 130.2 %collective-permute-start.13 = (f32[20,24,128]{2,1,0:T(8,128)}, f32[20,24,128]{2,1,0:T(8,128)}, u32[]{:S(2)}, u32[]{:S(2)}) collective-permute-start(f32[20,24,128]{2,1,0:T(8,128)} %collective-permute-done.12), channel_id=1, source_target_pairs={{0,15},{1,0},{2,1},{3,2},{4,3},{5,4},{6,5},{7,6},{8,7},{9,8},{10,9... | collective-permute-start | bytes 737288 | tf_op jit(solution)/shard_map/ppermute | solution.py:21
  216.0 6.2 collective-permute-start.22
  218.4 9.8 %collective-permute-start.16 = (f32[20,24,128]{2,1,0:T(8,128)}, f32[20,24,128]{2,1,0:T(8,128)S(1)}, u32[]{:S(2)}, u32[]{:S(2)}) collective-permute-start(f32[20,24,128]{2,1,0:T(8,128)} %collective-permute-done.15), channel_id=1, source_target_pairs={{0,1},{1,2},{2,3},{3,4},{4,5},{5,6},{6,7},{7,8},{8,9},{9,10},{10,1... | collective-permute-start | bytes 737288 | tf_op jit(solution)/shard_map/ppermute | solution.py:21
  220.8 12.6 %collective-permute-start.18 = (f32[20,24,128]{2,1,0:T(8,128)}, f32[20,24,128]{2,1,0:T(8,128)S(1)}, u32[]{:S(2)}, u32[]{:S(2)}) collective-permute-start(f32[20,24,128]{2,1,0:T(8,128)} %bitcast.543), channel_id=1, source_target_pairs={{0,1},{1,2},{2,3},{3,4},{4,5},{5,6},{6,7},{7,8},{8,9},{9,10},{10,1... | collective-permute-start | bytes 737288 | tf_op jit(solution)/shard_map/ppermute | solution.py:21
  221.8 11.6 %collective-permute-start.21 = (f32[20,24,128]{2,1,0:T(8,128)}, f32[20,24,128]{2,1,0:T(8,128)S(1)}, u32[]{:S(2)}, u32[]{:S(2)}) collective-permute-start(f32[20,24,128]{2,1,0:T(8,128)} %bitcast.542), channel_id=1, source_target_pairs={{0,16},{16,32},{32,48},{48,64},{64,80},{80,96},{96,112},{112,0},{1... | collective-permute-start | bytes 737288 | tf_op jit(solution)/shard_map/ppermute | solution.py:21
  222.2 11.2 %collective-permute-start.20 = (f32[20,24,128]{2,1,0:T(8,128)}, f32[20,24,128]{2,1,0:T(8,128)S(1)}, u32[]{:S(2)}, u32[]{:S(2)}) collective-permute-start(f32[20,24,128]{2,1,0:T(8,128)} %collective-permute-done.19), channel_id=1, source_target_pairs={{0,15},{1,0},{2,1},{3,2},{4,3},{5,4},{6,5},{7,6},{8,7},{9,8},{10,9... | collective-permute-start | bytes 737288 | tf_op jit(solution)/shard_map/ppermute | solution.py:21
  228.1 9.3 %collective-permute-start.23 = (f32[20,24,128]{2,1,0:T(8,128)S(1)}, f32[20,24,128]{2,1,0:T(8,128)S(1)}, u32[]{:S(2)}, u32[]{:S(2)}) collective-permute-start(f32[20,24,128]{2,1,0:T(8,128)S(1)} %collective-permute-done.22), channel_id=1, source_target_pairs={{0,1},{1,2},{2,3},{3,4},{4,5},{5,6},{6,7},{7,8},{8,9},{9,10},{10,1... | collective-permute-start | bytes 737288 | tf_op jit(solution)/shard_map/ppermute | solution.py:21
  492.2 93.7 %collective-permute-start.36 = (f32[18,24,128]{2,1,0:T(8,128)S(1)}, f32[18,24,128]{2,1,0:T(8,128)}, u32[]{:S(2)}, u32[]{:S(2)}) collective-permute-start(f32[18,24,128]{2,1,0:T(8,128)S(1)} %get-tuple-element.232), channel_id=1, source_target_pairs={{0,16},{16,32},{32,48},{48,64},{64,80},{80,96},{96,112},{112,0},{1... | collective-permute-start | bytes 663560 | tf_op jit(solution)/shard_map/ppermute | solution.py:21
  497.0 100.4 %collective-permute-start.38 = (f32[18,24,128]{2,1,0:T(8,128)}, f32[18,24,128]{2,1,0:T(8,128)}, u32[]{:S(2)}, u32[]{:S(2)}) collective-permute-start(f32[18,24,128]{2,1,0:T(8,128)} %get-tuple-element.231), channel_id=1, source_target_pairs={{0,16},{16,32},{32,48},{48,64},{64,80},{80,96},{96,112},{112,0},{1... | collective-permute-start | bytes 663560 | tf_op jit(solution)/shard_map/ppermute | solution.py:21
  497.0 103.0 %collective-permute-start.39 = (f32[18,24,128]{2,1,0:T(8,128)}, f32[18,24,128]{2,1,0:T(8,128)}, u32[]{:S(2)}, u32[]{:S(2)}) collective-permute-start(f32[18,24,128]{2,1,0:T(8,128)} %get-tuple-element.230), channel_id=1, source_target_pairs={{0,16},{16,32},{32,48},{48,64},{64,80},{80,96},{96,112},{112,0},{1... | collective-permute-start | bytes 663560 | tf_op jit(solution)/shard_map/ppermute | solution.py:21
  497.1 111.0 %collective-permute-start.41 = (f32[18,24,128]{2,1,0:T(8,128)S(1)}, f32[18,24,128]{2,1,0:T(8,128)}, u32[]{:S(2)}, u32[]{:S(2)}) collective-permute-start(f32[18,24,128]{2,1,0:T(8,128)S(1)} %get-tuple-element.229), channel_id=1, source_target_pairs={{0,1},{1,2},{2,3},{3,4},{4,5},{5,6},{6,7},{7,8},{8,9},{9,10},{10,1... | collective-permute-start | bytes 663560 | tf_op jit(solution)/shard_map/ppermute | solution.py:21
  497.1 113.0 %collective-permute-start.42 = (f32[18,24,128]{2,1,0:T(8,128)S(1)}, f32[18,24,128]{2,1,0:T(8,128)}, u32[]{:S(2)}, u32[]{:S(2)}) collective-permute-start(f32[18,24,128]{2,1,0:T(8,128)S(1)} %get-tuple-element.228), channel_id=1, source_target_pairs={{0,15},{1,0},{2,1},{3,2},{4,3},{5,4},{6,5},{7,6},{8,7},{9,8},{10,9... | collective-permute-start | bytes 663560 | tf_op jit(solution)/shard_map/ppermute | solution.py:21
  585.9 9.5 %collective-permute-start.37 = (f32[18,24,128]{2,1,0:T(8,128)}, f32[18,24,128]{2,1,0:T(8,128)S(1)}, u32[]{:S(2)}, u32[]{:S(2)}) collective-permute-start(f32[18,24,128]{2,1,0:T(8,128)} %collective-permute-done.36), channel_id=1, source_target_pairs={{0,1},{1,2},{2,3},{3,4},{4,5},{5,6},{6,7},{7,8},{8,9},{9,10},{10,1... | collective-permute-start | bytes 663560 | tf_op jit(solution)/shard_map/ppermute | solution.py:21
  595.4 14.8 %collective-permute-start.43 = (f32[18,24,128]{2,1,0:T(8,128)S(1)}, f32[18,24,128]{2,1,0:T(8,128)S(1)}, u32[]{:S(2)}, u32[]{:S(2)}) collective-permute-start(f32[18,24,128]{2,1,0:T(8,128)S(1)} %get-tuple-element.227), channel_id=1, source_target_pairs={{0,112},{16,0},{32,16},{48,32},{64,48},{80,64},{96,80},{112,96},{1... | collective-permute-start | bytes 663560 | tf_op jit(solution)/shard_map/ppermute | solution.py:21
  597.4 24.8 %collective-permute-start.45 = (f32[18,24,128]{2,1,0:T(8,128)S(1)}, f32[18,24,128]{2,1,0:T(8,128)S(1)}, u32[]{:S(2)}, u32[]{:S(2)}) collective-permute-start(f32[18,24,128]{2,1,0:T(8,128)S(1)} %get-tuple-element.233), channel_id=1, source_target_pairs={{0,112},{16,0},{32,16},{48,32},{64,48},{80,64},{96,80},{112,96},{1... | collective-permute-start | bytes 663560 | tf_op jit(solution)/shard_map/ppermute | solution.py:21
  600.0 6.4 collective-permute-start.40
  606.4 15.9 %collective-permute-start.46 = (f32[18,24,128]{2,1,0:T(8,128)S(1)}, f32[18,24,128]{2,1,0:T(8,128)S(1)}, u32[]{:S(2)}, u32[]{:S(2)}) collective-permute-start(f32[18,24,128]{2,1,0:T(8,128)S(1)} %get-tuple-element.226), channel_id=1, source_target_pairs={{0,112},{16,0},{32,16},{48,32},{64,48},{80,64},{96,80},{112,96},{1... | collective-permute-start | bytes 663560 | tf_op jit(solution)/shard_map/ppermute | solution.py:21
  608.1 18.9 %collective-permute-start.24 = (f32[18,24,128]{2,1,0:T(8,128)S(1)}, f32[18,24,128]{2,1,0:T(8,128)}, u32[]{:S(2)}, u32[]{:S(2)}) collective-permute-start(f32[18,24,128]{2,1,0:T(8,128)S(1)} %get-tuple-element.240), channel_id=1, source_target_pairs={{0,16},{16,32},{32,48},{48,64},{64,80},{80,96},{96,112},{112,0},{1... | collective-permute-start | bytes 663560 | tf_op jit(solution)/shard_map/ppermute | solution.py:21
  610.1 35.6 %collective-permute-start.26 = (f32[18,24,128]{2,1,0:T(8,128)}, f32[18,24,128]{2,1,0:T(8,128)}, u32[]{:S(2)}, u32[]{:S(2)}) collective-permute-start(f32[18,24,128]{2,1,0:T(8,128)} %get-tuple-element.239), channel_id=1, source_target_pairs={{0,16},{16,32},{32,48},{48,64},{64,80},{80,96},{96,112},{112,0},{1... | collective-permute-start | bytes 663560 | tf_op jit(solution)/shard_map/ppermute | solution.py:21
  610.1 10.0 %collective-permute-start.44 = (f32[18,24,128]{2,1,0:T(8,128)S(1)}, f32[18,24,128]{2,1,0:T(8,128)S(1)}, u32[]{:S(2)}, u32[]{:S(2)}) collective-permute-start(f32[18,24,128]{2,1,0:T(8,128)S(1)} %collective-permute-done.43), channel_id=1, source_target_pairs={{0,1},{1,2},{2,3},{3,4},{4,5},{5,6},{6,7},{7,8},{8,9},{9,10},{10,1... | collective-permute-start | bytes 663560 | tf_op jit(solution)/shard_map/ppermute | solution.py:21
  620.1 25.7 %collective-permute-start.27 = (f32[18,24,128]{2,1,0:T(8,128)}, f32[18,24,128]{2,1,0:T(8,128)}, u32[]{:S(2)}, u32[]{:S(2)}) collective-permute-start(f32[18,24,128]{2,1,0:T(8,128)} %get-tuple-element.238), channel_id=1, source_target_pairs={{0,16},{16,32},{32,48},{48,64},{64,80},{80,96},{96,112},{112,0},{1... | collective-permute-start | bytes 663560 | tf_op jit(solution)/shard_map/ppermute | solution.py:21
  622.2 34.7 %collective-permute-start.29 = (f32[18,24,128]{2,1,0:T(8,128)}, f32[18,24,128]{2,1,0:T(8,128)}, u32[]{:S(2)}, u32[]{:S(2)}) collective-permute-start(f32[18,24,128]{2,1,0:T(8,128)} %get-tuple-element.237), channel_id=1, source_target_pairs={{0,1},{1,2},{2,3},{3,4},{4,5},{5,6},{6,7},{7,8},{8,9},{9,10},{10,1... | collective-permute-start | bytes 663560 | tf_op jit(solution)/shard_map/ppermute | solution.py:21
  622.3 10.0 %collective-permute-start.47 = (f32[18,24,128]{2,1,0:T(8,128)S(1)}, f32[18,24,128]{2,1,0:T(8,128)S(1)}, u32[]{:S(2)}, u32[]{:S(2)}) collective-permute-start(f32[18,24,128]{2,1,0:T(8,128)S(1)} %collective-permute-done.46), channel_id=1, source_target_pairs={{0,15},{1,0},{2,1},{3,2},{4,3},{5,4},{6,5},{7,6},{8,7},{9,8},{10,9... | collective-permute-start | bytes 663560 | tf_op jit(solution)/shard_map/ppermute | solution.py:21
  627.1 30.8 %collective-permute-start.30 = (f32[18,24,128]{2,1,0:T(8,128)}, f32[18,24,128]{2,1,0:T(8,128)}, u32[]{:S(2)}, u32[]{:S(2)}) collective-permute-start(f32[18,24,128]{2,1,0:T(8,128)} %get-tuple-element.236), channel_id=1, source_target_pairs={{0,15},{1,0},{2,1},{3,2},{4,3},{5,4},{6,5},{7,6},{8,7},{9,8},{10,9... | collective-permute-start | bytes 663560 | tf_op jit(solution)/shard_map/ppermute | solution.py:21
  632.3 11.7 %collective-permute-start.25 = (f32[18,24,128]{2,1,0:T(8,128)}, f32[18,24,128]{2,1,0:T(8,128)}, u32[]{:S(2)}, u32[]{:S(2)}) collective-permute-start(f32[18,24,128]{2,1,0:T(8,128)} %collective-permute-done.24), channel_id=1, source_target_pairs={{0,1},{1,2},{2,3},{3,4},{4,5},{5,6},{6,7},{7,8},{8,9},{9,10},{10,1... | collective-permute-start | bytes 663560 | tf_op jit(solution)/shard_map/ppermute | solution.py:21
  644.0 5.4 collective-permute-start.31
  645.8 6.3 collective-permute-start.34
  645.8 6.2 collective-permute-start.28
  649.4 13.4 %collective-permute-start.33 = (f32[18,24,128]{2,1,0:T(8,128)S(1)}, f32[18,24,128]{2,1,0:T(8,128)S(1)}, u32[]{:S(2)}, u32[]{:S(2)}) collective-permute-start(f32[18,24,128]{2,1,0:T(8,128)S(1)} %get-tuple-element.241), channel_id=1, source_target_pairs={{0,112},{16,0},{32,16},{48,32},{64,48},{80,64},{96,80},{112,96},{1... | collective-permute-start | bytes 663560 | tf_op jit(solution)/shard_map/ppermute | solution.py:21
  652.0 10.7 %collective-permute-start.32 = (f32[18,24,128]{2,1,0:T(8,128)S(1)}, f32[18,24,128]{2,1,0:T(8,128)S(1)}, u32[]{:S(2)}, u32[]{:S(2)}) collective-permute-start(f32[18,24,128]{2,1,0:T(8,128)S(1)} %collective-permute-done.31), channel_id=1, source_target_pairs={{0,1},{1,2},{2,3},{3,4},{4,5},{5,6},{6,7},{7,8},{8,9},{9,10},{10,1... | collective-permute-start | bytes 663560 | tf_op jit(solution)/shard_map/ppermute | solution.py:21
  652.0 10.8 %collective-permute-start.35 = (f32[18,24,128]{2,1,0:T(8,128)S(1)}, f32[18,24,128]{2,1,0:T(8,128)S(1)}, u32[]{:S(2)}, u32[]{:S(2)}) collective-permute-start(f32[18,24,128]{2,1,0:T(8,128)S(1)} %collective-permute-done.34), channel_id=1, source_target_pairs={{0,15},{1,0},{2,1},{3,2},{4,3},{5,4},{6,5},{7,6},{8,7},{9,8},{10,9... | collective-permute-start | bytes 663560 | tf_op jit(solution)/shard_map/ppermute | solution.py:21
  (32 other events, 311.4 us)
where the time goes:
time: 683 us; the launch traced here: 670 us
  local copies, waits for them, and re-layouts  239 us (35%)
  matrix products  224 us (33%)
  other arithmetic  75.6 us (11%)
  starting transfers between devices  71 us (10%)
  waiting for transfers between devices  57.7 us (8%)
    dot_general x16, matrix products, spread(): return jnp.einsum('fgc,gcl->fgl', value_part, onehot, precision=HIGHEST)  98.1 us
    dot_general x16, matrix products, select(): return jnp.einsum('fgl,gcl->fgc', block_part, onehot, precision=HIGHEST)  86.5 us
    ppermute x48, starting transfers between devices, from_behind(): return lax.ppermute(value, axis, pairs)  71 us
    dynamic_update_slice x32, local copies, waits for them, and re-layouts, gather_cell_rows(): cells = lax.map(select, (blocks, lanes))  60.7 us
    ppermute x48, waiting for transfers between devices, from_behind(): return lax.ppermute(value, axis, pairs)  57.7 us
    unnamed x119, local copies, waits for them, and re-layouts  54.3 us
    gather x2, local copies, waits for them, and re-layouts, gather_cell_rows(): blocks = jnp.take(slabs, group_slot_index, axis=1)  47.7 us
    select_n x2, other arithmetic, gather_cell_rows(): blocks = jnp.take(slabs, group_slot_index, axis=1)  38.4 us
  transfers between devices with their start and end apart: 48, of which 13 were waited for; matrix products, arithmetic and copies ran while one was open for 40% of the time, Pallas kernels for 0%

commit v1 on v0

v1 whole, which is shorter than its diff:
```python
import functools

import jax
import jax.numpy as jnp
import numpy as np
from jax import lax
from jax.experimental import pallas as pl
from jax.experimental.pallas import tpu as pltpu
from jax.sharding import PartitionSpec as P

ITERS = 6
GRP = 32
LANES = 128
CAP = 24
SLOTS = 9 * CAP
FIELDS = (6, 7, 7)
SUMS = (4, 7, 7)

VMEM = pl.BlockSpec(memory_space=pltpu.VMEM)
SMEM = pl.BlockSpec(memory_space=pltpu.SMEM)
F32 = jnp.float32
BF16 = jnp.bfloat16


def call(body, name, out_shape, in_specs, scratch=(), us=10):
    return pl.pallas_call(
        body,
        name=name,
        out_shape=out_shape,
        in_specs=in_specs,
        out_specs=jax.tree.map(lambda _: VMEM, out_shape),
        scratch_shapes=list(scratch),
        compiler_params=pltpu.CompilerParams(vmem_limit_bytes=40 * 1024 * 1024),
        cost_estimate=pl.CostEstimate(flops=0, bytes_accessed=int(us * 3.3e6), transcendentals=0),
    )


def shape(*dims):
    return jax.ShapeDtypeStruct(dims, F32)


def pack_body(ids_a, ids_o, fields_a, fields_o, *outs):
    for n in range(9):
        p, q = n // 3, n % 3

        def step(c, _):
            for comp, (ids, fields) in enumerate(((ids_a, fields_a), (ids_o, fields_o))):
                col = pl.ds(pl.multiple_of(jnp.maximum(ids[n * CAP + c], 0) * LANES, LANES), LANES)
                top, mid, low = fields[0:8, col], fields[8:16, col], fields[16:20, col]
                block = (p * 2 + comp) * CAP + c
                outs[q][pl.ds(block * 6, 6), :] = top[:6]
                outs[3 + q][pl.ds(block * 7, 2), :] = top[6:]
                outs[3 + q][pl.ds(block * 7 + 2, 5), :] = mid[:5]
                outs[6 + q][pl.ds(block * 7, 3), :] = mid[5:]
                outs[6 + q][pl.ds(block * 7 + 3, 4), :] = low
            return 0

        lax.fori_loop(0, CAP, step, 0, unroll=8)


def pack(ids_a, ids_o, fields_a, fields_o):
    outs = tuple(shape(3 * 2 * CAP * f, LANES) for f in FIELDS for _ in range(3))
    return call(pack_body, "pack", outs, [SMEM, SMEM, VMEM, VMEM], us=4)(ids_a, ids_o, fields_a, fields_o)


def hop(value, axis, steps):
    count = lax.axis_size(axis)
    return lax.ppermute(value, axis, [(s, (s + steps) % count) for s in range(count)])


def third(value, k):
    size = value.shape[0] // 3
    return value[k * size : (k + 1) * size]


def to_owners(parts):
    came = [hop(parts[0], "gy", -1), parts[1], hop(parts[2], "gy", 1)]
    ahead = hop(jnp.concatenate([third(v, 2) for v in came]), "gx", 1)
    behind = hop(jnp.concatenate([third(v, 0) for v in came]), "gx", -1)
    return behind, ahead, came


def to_sources(parts):
    came = [hop(parts[0], "gx", 1), parts[1], hop(parts[2], "gx", -1)]
    up = hop(jnp.concatenate([third(v, 2) for v in came]), "gy", -1)
    down = hop(jnp.concatenate([third(v, 0) for v in came]), "gy", 1)
    return down, up, came


def join_slabs(pieces, slabs, rows):
    behind, ahead, *came = pieces
    for p in range(3):
        for q in range(3):
            for comp in range(2):
                if p == 1:
                    source, at = came[q], (2 + comp) * rows
                else:
                    source, at = (behind, None, ahead)[p], (q * 2 + comp) * rows
                slabs[comp][pl.ds((p * 3 + q) * rows, rows), :] = source[pl.ds(at, rows), :]


def take_lanes(v, index):
    dims = lax.GatherDimensionNumbers(
        offset_dims=(),
        collapsed_slice_dims=(1,),
        start_index_map=(1,),
        operand_batching_dims=(0,),
        start_indices_batching_dims=(0,),
    )
    return lax.gather(v, index[..., None], dims, (1, 1), mode=lax.GatherScatterMode.PROMISE_IN_BOUNDS)


def gather_row(slab, slots, r, stride, lanes, quarter):
    out = None
    index = jnp.broadcast_to(lanes, (8, LANES))
    for j in range(4):
        v = take_lanes(slab[pl.ds(slots[4 * r + j] * stride, 8), :], index)
        out = v if out is None else jnp.where(quarter >= j, v, out)
    return out


def odd_arctan_coefficients():
    z_top = 0.325
    nodes = (np.cos((np.arange(400) + 0.5) * np.pi / 400) + 1) / 2 * z_top
    t = np.sqrt(nodes)
    fit = np.polynomial.chebyshev.Chebyshev.fit(nodes, np.arctan(t) / t, 7, domain=[0, z_top])
    return [float(c) for c in fit.convert(kind=np.polynomial.Polynomial).coef]


ARCTAN = odd_arctan_coefficients()


def small_arctan(t):
    z = t * t
    total = jnp.full_like(t, ARCTAN[-1])
    for c in ARCTAN[-2::-1]:
        total = total * z + c
    return t * total


def bulk(a, o):
    shear_x = 6.0 * a[0] - 0.3 * o[0]
    shear_y = 6.0 * a[1] - 0.3 * o[1]
    speed2 = shear_x * shear_x + shear_y * shear_y + 0.25 + 0.1 * a[5] * a[5]
    speed = jnp.sqrt(speed2)
    dtemp = 3.0 * (a[2] - o[2])
    dhum = 0.002 * (a[3] - o[3])
    height = 10.0 * jnp.exp(0.3 * a[4])
    log_height = jnp.log(height * 10000.0)
    log_m = log_height - 0.5 * o[4]
    log_h = log_height - 0.5 * o[5]
    rm = 0.4 / log_m
    rh = 0.4 / log_h
    base = (0.4 * 9.8) * height * (dtemp / 290.0 + 0.61 * dhum) / speed2
    for _ in range(ITERS):
        zeta = jnp.clip(base * rh / (rm * rm), -10.0, 3.0)
        u2 = jnp.sqrt(1.0 - 16.0 * jnp.minimum(zeta, 0.0))
        u = jnp.sqrt(u2)
        one_u = 1.0 + u
        one_u2 = 1.0 + u2
        stable = -5.0 * zeta
        psi_m = jnp.where(
            zeta > 0.0,
            stable,
            jnp.log(one_u * one_u * one_u2 * 0.125) - 2.0 * small_arctan((u - 1.0) / one_u),
        )
        psi_h = jnp.where(zeta > 0.0, stable, 2.0 * jnp.log(one_u2 * 0.5))
        rm = 0.5 * rm + 0.2 / (log_m - psi_m)
        rh = 0.5 * rh + 0.2 / (log_h - psi_h)
    drag = 25.0 * rm * rm * speed
    transfer = 25.0 * rm * rh * speed
    return (drag * shear_x, drag * shear_y, transfer * dtemp, 500.0 * transfer * dhum), transfer


def onehots(lanes_a, lanes_o, column):
    one, zero = jnp.ones((), BF16), jnp.zeros((), BF16)
    a = jnp.where(column == lanes_a.astype(BF16), one, zero)
    o = jnp.where(column == lanes_o.astype(BF16), one, zero)
    return jnp.concatenate([a, o], axis=0)


def two_pieces(v):
    high = v.astype(BF16).astype(F32)
    return high, v - high


def scatter_row(v, lanes_a, lanes_o, column, quarter):
    parts = [jnp.where(quarter == j, x, 0.0) for j in range(4) for x in two_pieces(v)]
    left = jnp.concatenate(parts, axis=0).astype(BF16)
    right = onehots(lanes_a, lanes_o, column)
    sums = lax.dot_general(left, right, (((1,), (1,)), ((), ())), preferred_element_type=F32)
    return [sums[16 * j : 16 * j + 8] + sums[16 * j + 8 : 16 * j + 16] for j in range(4)]


def add_groups(sums, slots_a, slots_o, r, acc_a, acc_o):
    for j in range(4):
        at_a = pl.ds(pl.multiple_of(slots_a[4 * r + j] * 8, 8), 8)
        at_o = pl.ds(pl.multiple_of(slots_o[4 * r + j] * 8, 8), 8)
        acc_a[at_a, :] += sums[j][:, :LANES]
        acc_o[at_o, :] += sums[j][:, LANES:]


def split_sums(accs, outs, rows):
    for p in range(3):
        for q in range(3):

            def step(c, _):
                for comp in range(2):
                    at = pl.multiple_of(((p * 3 + q) * CAP + c) * 8, 8)
                    outs[p][pl.ds(((q * 2 + comp) * CAP + c) * rows, rows), :] = accs[comp][pl.ds(at, 8), :][:rows]
                return 0

            lax.fori_loop(0, CAP, step, 0, unroll=8)


def iota_quarter():
    return lax.broadcasted_iota(jnp.int32, (8, LANES), 1) // GRP


def iota_column():
    return lax.broadcasted_iota(jnp.int32, (LANES, LANES), 0).astype(BF16)


def first_body(nrows, count, slots_a, slots_o, ref_a, ref_o, area, mask, *rest):
    pieces, (weight, lead, slab_a, slab_o, cells_a, cells_o) = rest[:5], rest[5:]
    join_slabs(pieces, (slab_a, slab_o), CAP * 6)
    quarter = iota_quarter()

    def gather(r, _):
        for ref, slab, slots, cells in ((ref_a, slab_a, slots_a, cells_a), (ref_o, slab_o, slots_o, cells_o)):
            lanes = ref[pl.ds(r, 1), :] & (LANES - 1)
            cells[pl.ds(r, 8, stride=nrows), :] = gather_row(slab, slots, r, 6, lanes, quarter)
        return 0

    lax.fori_loop(0, nrows, gather, 0, unroll=32)
    live = count[0]
    depth = 64

    def iterate(i, _):
        row = pl.multiple_of(i * depth, depth)
        a = [cells_a[pl.ds(pl.multiple_of(f * nrows + row, depth), depth), :] for f in range(6)]
        o = [cells_o[pl.ds(pl.multiple_of(f * nrows + row, depth), depth), :] for f in range(6)]
        here = pl.ds(row, depth)
        place = (row + lax.broadcasted_iota(jnp.int32, (depth, LANES), 0)) * LANES
        place = place + lax.broadcasted_iota(jnp.int32, (depth, LANES), 1)
        w = jnp.where((place < live) & (mask[here, :] == 1), area[here, :], 0.0)
        fluxes, transfer = bulk(a, o)
        weight[here, :] = transfer * w
        for k, flux in enumerate(fluxes):
            lead[pl.ds(row * 4 + k, depth, stride=4), :] = flux * w
        return 0

    lax.fori_loop(0, nrows // depth, iterate, 0)


def first(count, slots, refs, area, mask, pieces):
    nrows = area.shape[0]
    return call(
        functools.partial(first_body, nrows),
        "bulk",
        (shape(nrows, LANES), shape(nrows * 4 + 8, LANES)),
        [SMEM] * 3 + [VMEM] * 9,
        [pltpu.VMEM((SLOTS * 6 + 8, LANES), F32)] * 2 + [pltpu.VMEM((8 * nrows, LANES), F32)] * 2,
        us=20,
    )(count, *slots, *refs, area, mask, *pieces)


def lead_body(nrows, slots_a, slots_o, ref_a, ref_o, lead, *rest):
    outs, accs = rest[:3], rest[3:]
    for acc in accs:
        acc[...] = jnp.zeros_like(acc)
    quarter, column = iota_quarter(), iota_column()

    def step(r, _):
        lanes_a, lanes_o = ref_a[pl.ds(r, 1), :] & (LANES - 1), ref_o[pl.ds(r, 1), :] & (LANES - 1)
        v = lead[pl.ds(r * 4, 8), :]
        add_groups(scatter_row(v, lanes_a, lanes_o, column, quarter), slots_a, slots_o, r, *accs)
        return 0

    lax.fori_loop(0, nrows, step, 0, unroll=32)
    split_sums(accs, outs, 4)


def lead_sums(slots, refs, lead):
    nrows = refs[0].shape[0]
    return call(
        functools.partial(lead_body, nrows),
        "lead",
        tuple(shape(3 * 2 * CAP * 4, LANES) for _ in range(3)),
        [SMEM] * 2 + [VMEM] * 3,
        [pltpu.VMEM((SLOTS * 8, LANES), F32)] * 2,
        us=12,
    )(*slots, *refs, lead)


def tracer_body(nrows, slots_a, slots_o, ref_a, ref_o, weight, *rest):
    pieces, outs, slabs, accs = rest[:5], rest[5:8], rest[8:10], rest[10:]
    join_slabs(pieces, slabs, CAP * 7)
    for acc in accs:
        acc[...] = jnp.zeros_like(acc)
    quarter, column = iota_quarter(), iota_column()

    def step(r, _):
        lanes_a, lanes_o = ref_a[pl.ds(r, 1), :] & (LANES - 1), ref_o[pl.ds(r, 1), :] & (LANES - 1)
        a = gather_row(slabs[0], slots_a, r, 7, lanes_a, quarter)
        o = gather_row(slabs[1], slots_o, r, 7, lanes_o, quarter)
        v = (a - o) * jnp.broadcast_to(weight[pl.ds(r, 1), :], (8, LANES))
        add_groups(scatter_row(v, lanes_a, lanes_o, column, quarter), slots_a, slots_o, r, *accs)
        return 0

    lax.fori_loop(0, nrows, step, 0, unroll=32)
    split_sums(accs, outs, 7)


def tracers(slots, refs, weight, pieces):
    nrows = weight.shape[0]
    return call(
        functools.partial(tracer_body, nrows),
        "tracers",
        tuple(shape(3 * 2 * CAP * 7, LANES) for _ in range(3)),
        [SMEM] * 2 + [VMEM] * 8,
        [pltpu.VMEM((SLOTS * 7 + 8, LANES), F32)] * 2 + [pltpu.VMEM((SLOTS * 8, LANES), F32)] * 2,
        us=18,
    )(*slots, *refs, weight, *pieces)


def unpack_body(nblocks, ids_a, ids_o, area_a, area_o, *rest):
    parts = [rest[5 * k : 5 * k + 5] for k in range(3)]
    outs, accs = rest[15:17], rest[17:]
    for acc in accs:
        acc[...] = jnp.zeros_like(acc)
    for n in range(9):
        p, q = n // 3, n % 3

        def step(c, _):
            for comp, ids in enumerate((ids_a, ids_o)):
                at = pl.ds(pl.multiple_of(jnp.maximum(ids[n * CAP + c], 0) * 8, 8), 8)
                for k, rows in enumerate(SUMS):
                    down, up, *came = parts[k]
                    if q == 1:
                        source, base = came[p], (2 + comp) * CAP
                    else:
                        source, base = (down, None, up)[q], (p * 2 + comp) * CAP
                    acc = accs[comp * 3 + k]
                    acc[pl.ds(at.start, rows), :] += source[pl.ds((base + c) * rows, rows), :]
            return 0

        lax.fori_loop(0, CAP, step, 0, unroll=8)

    def finish(b, _):
        col = pl.ds(pl.multiple_of(b * LANES, LANES), LANES)
        for comp, area in enumerate((area_a, area_o)):
            row = 0
            for k, rows in enumerate(SUMS):
                v = accs[comp * 3 + k][pl.ds(pl.multiple_of(b * 8, 8), 8), :] / area[pl.ds(b, 1), :]
                outs[comp][row : row + rows, col] = v[:rows]
                row += rows
        return 0

    lax.fori_loop(0, nblocks, finish, 0, unroll=8)


def unpack(ids_a, ids_o, area_a, area_o, parts):
    nblocks = area_a.shape[0]
    flat = [x for part in parts for x in part]
    return call(
        functools.partial(unpack_body, nblocks),
        "unpack",
        (shape(sum(SUMS), nblocks * LANES),) * 2,
        [SMEM] * 2 + [VMEM] * 17,
        [pltpu.VMEM((nblocks * 8, LANES), F32)] * 6,
        us=6,
    )(ids_a, ids_o, area_a, area_o, *flat)


def shards(fields_a, fields_o, area_a, area_o, send_a, send_o, atm_ref, ocn_ref, cell_area, cell_mask, cell_count):
    ids_a, ids_o = send_a.reshape(-1), send_o.reshape(-1)
    packed = pack(ids_a, ids_o, fields_a, fields_o)
    refs = (atm_ref.reshape(-1, LANES), ocn_ref.reshape(-1, LANES))
    slots = tuple(ref[:, ::GRP].reshape(-1) // LANES for ref in refs)
    came = []
    for k in range(3):
        behind, ahead, rest = to_owners(packed[3 * k : 3 * k + 3])
        came.append((behind, ahead, *rest))
    weight, lead = first(
        cell_count, slots, refs, cell_area.reshape(-1, LANES), cell_mask.reshape(-1, LANES), came[0]
    )
    sums = [lead_sums(slots, refs, lead)] + [tracers(slots, refs, weight, came[k]) for k in (1, 2)]
    back = []
    for part in sums:
        down, up, rest = to_sources(part)
        back.append((down, up, *rest))
    return unpack(ids_a, ids_o, area_a.reshape(-1, LANES), area_o.reshape(-1, LANES), back)


def solution(mesh):
    both = ("gx", "gy")
    in_specs = (P(None, both), P(None, both), P(both), P(both), P(both, None, None), P(both, None, None)) + (P(both),) * 5
    return jax.shard_map(shards, mesh=mesh, in_specs=in_specs, out_specs=(P(None, both),) * 2, check_vma=False)
```

time: 683 us -> 163 us (0.24); the launches traced: 670 us -> 160 us
  local copies, waits for them, and re-layouts: 239 us -> 14.4 us
  matrix products: 224 us -> 0 us
  other arithmetic: 75.6 us -> 1.82 us
  Pallas kernels: 0 us -> 69.5 us
  waiting for transfers between devices: 57.7 us -> 26.7 us
  starting transfers between devices: 71 us -> 45.7 us
    dot_general x36 -> x0, matrix products: 224 us -> none  [the longest x16 98.1 us: spread(): return jnp.einsum('fgc,gcl->fgl', value_part, onehot, precision=HIGHEST)]
    pallas_call x0 -> x6, Pallas kernels: none -> 69.5 us  [the longest x2 30.1 us: tracers(): call(functools.partial(tracer_body, nrows), 'tracers', tuple((shape(3 * 2...]
    dynamic_update_slice x32 -> x0, local copies, waits for them, and re-layouts: 60.7 us -> none  [gather_cell_rows(): cells = lax.map(select, (blocks, lanes))]
    gather x4 -> x0, local copies, waits for them, and re-layouts: 52.5 us -> none  [the longest x2 47.7 us: gather_cell_rows(): blocks = jnp.take(slabs, group_slot_index, axis=1)]
    unnamed x119 -> x24, local copies, waits for them, and re-layouts: 54.3 us -> 4.59 us
    select_n x7 -> x1, other arithmetic: 46.8 us -> 0.01 us  [shards(): slots = tuple((ref[:, ::GRP].reshape(-1) // LANES for ref in refs))]
    ppermute x48 -> x24, waiting for transfers between devices: 57.7 us -> 26.7 us  [hop(): lax.ppermute(value, axis, [(s, (s + steps) % count) for s in range(count)])]
    eq x32 -> x0, local copies, waits for them, and re-layouts: 29.2 us -> none  [the longest x16 14.6 us: spread(): lane_part[:, :, None] == lane_ids[None, None, :]]
  transfers between devices with their start and end apart: 48 -> 24, of which waited for: 13 -> 6; matrix products, arithmetic and copies ran while one was open for 40% -> 6% of each run, Pallas kernels for 0% -> 39%
where the time goes in v1:
time: 163 us; the launch traced here: 160 us
  Pallas kernels  69.5 us (43%)
  starting transfers between devices  45.7 us (28%)
  waiting for transfers between devices  26.7 us (16%)
  local copies, waits for them, and re-layouts  14.4 us (9%)
  other arithmetic  1.82 us (1%)
  between operations  1.69 us (1%)
    ppermute x24, starting transfers between devices, hop(): lax.ppermute(value, axis, [(s, (s + steps) % count) for s in range(count)])  45.7 us
    pallas_call x2, Pallas kernels, tracers(): call(functools.partial(tracer_body, nrows), 'tracers', tuple((shape(3 * 2...  30.1 us
    ppermute x24, waiting for transfers between devices, hop(): lax.ppermute(value, axis, [(s, (s + steps) % count) for s in range(count)])  26.7 us
    pallas_call x1, Pallas kernels, first(): call(functools.partial(first_body, nrows), 'bulk', (shape(nrows, LANES),...  16.1 us
    pallas_call x1, Pallas kernels, lead_sums(): call(functools.partial(lead_body, nrows), 'lead', tuple((shape(3 * 2 * CA...  15.5 us
    unnamed x24, local copies, waits for them, and re-layouts  4.59 us
    pallas_call x1, Pallas kernels, unpack(): call(functools.partial(unpack_body, nblocks), 'unpack', (shape(sum(SUMS),...  4.39 us
    slice x2, local copies, waits for them, and re-layouts, shards(): slots = tuple((ref[:, ::GRP].reshape(-1) // LANES for ref in refs))  3.85 us
  transfers between devices with their start and end apart: 24, of which 6 were waited for; matrix products, arithmetic and copies ran while one was open for 6% of the time, Pallas kernels for 39%

profile of v1, /device:TPU:1, one launch (start us, length us, event | category | flops | bytes accessed | tf_op | source)
XLA Modules:
  0.0 159.8 jit_solution(14164571959058980182)
XLA Ops:
  0.6 0.7 reduce
  1.3 0.1 reshape.34.ids_a
  1.4 0.7 reduce.1
  2.1 0.1 reshape.35.ids_o
  2.2 1.4 copy-done.2
  3.6 1.4 copy-done.3
  5.0 3.3 %pack.1 = (f32[864,128]{1,0:T(8,128)}, f32[864,128]{1,0:T(8,128)S(1)}, f32[864,128]{1,0:T(8,128)}, f32[1008,128]{1,0:T(8,128)}, f32[1008,128]{1,0:T(8,128)S(1)},...) custom-call(s32[216]{0:T(256)S(1)} %reshape.34.ids_a, ...), custom_call_target="tpu_custom_call" | custom-call | bytes 13200000 | tf_op jit(solution)/shard_map/pack/pallas_call | solution.py:63
  8.4 0.8 copy-done.8
  9.2 6.8 %collective-permute-start = (f32[864,128]{1,0:T(8,128)}, f32[864,128]{1,0:T(8,128)}, u32[]{:S(2)}, u32[]{:S(2)}) collective-permute-start(f32[864,128]{1,0:T(8,128)} %get-tuple-element.22), channel_id=1, source_target_pairs={{0,15},{1,0},{2,1},{3,2},{4,3},{5,4},{6,5},{7,6},{8,7},{9,8},{10,9... | collective-permute-start | bytes 1327112 | tf_op jit(solution)/shard_map/ppermute | solution.py:68
  16.0 4.8 %collective-permute-start.8 = (f32[1008,128]{1,0:T(8,128)}, f32[1008,128]{1,0:T(8,128)S(1)}, u32[]{:S(2)}, u32[]{:S(2)}) collective-permute-start(f32[1008,128]{1,0:T(8,128)} %get-tuple-element.30), channel_id=1, source_target_pairs={{0,15},{1,0},{2,1},{3,2},{4,3},{5,4},{6,5},{7,6},{8,7},{9,8},{10,9... | collective-permute-start | bytes 1548296 | tf_op jit(solution)/shard_map/ppermute | solution.py:68
  20.7 4.8 %collective-permute-start.16 = (f32[1008,128]{1,0:T(8,128)}, f32[1008,128]{1,0:T(8,128)S(1)}, u32[]{:S(2)}, u32[]{:S(2)}) collective-permute-start(f32[1008,128]{1,0:T(8,128)} %get-tuple-element.36), channel_id=1, source_target_pairs={{0,15},{1,0},{2,1},{3,2},{4,3},{5,4},{6,5},{7,6},{8,7},{9,8},{10,9... | collective-permute-start | bytes 1548296 | tf_op jit(solution)/shard_map/ppermute | solution.py:68
  25.5 1.9 %slice.114 = s32[512,4]{1,0:T(8,128)} slice(s32[512,128]{1,0:T(8,128)S(1)} %bitcast.11), slice={[0:512:1], [0:128:32]} | slice | bytes 16384 | tf_op jit(solution)/shard_map/slice | solution.py:380
  27.5 1.7 %reshape.39 = s32[2048]{0:T(1024)} reshape(s32[512,4]{1,0:T(8,128)} %slice.114) | data formatting | bytes 16384 | tf_op jit(solution)/shard_map/reshape | solution.py:380
  29.2 1.9 %slice.115 = s32[512,4]{1,0:T(8,128)} slice(s32[512,128]{1,0:T(8,128)S(1)} %bitcast.6), slice={[0:512:1], [0:128:32]} | slice | bytes 16384 | tf_op jit(solution)/shard_map/slice | solution.py:380
  31.1 1.7 %reshape.41 = s32[2048]{0:T(1024)} reshape(s32[512,4]{1,0:T(8,128)} %slice.115) | data formatting | bytes 16384 | tf_op jit(solution)/shard_map/reshape | solution.py:380
  32.9 0.9 copy-done.9
  33.8 1.0 fusion.16
  34.8 1.0 fusion.18
  35.9 2.1 %collective-permute-start.2 = (f32[864,128]{1,0:T(8,128)S(1)}, f32[864,128]{1,0:T(8,128)S(1)}, u32[]{:S(2)}, u32[]{:S(2)}) collective-permute-start(f32[864,128]{1,0:T(8,128)S(1)} %pad_maximum_fusion.8), channel_id=1, source_target_pairs={{0,112},{16,0},{32,16},{48,32},{64,48},{80,64},{96,80},{112,96},{1... | collective-permute-start | bytes 1327112 | tf_op jit(solution)/shard_map/ppermute | solution.py:68
  38.0 2.0 %collective-permute-start.3 = (f32[864,128]{1,0:T(8,128)S(1)}, f32[864,128]{1,0:T(8,128)S(1)}, u32[]{:S(2)}, u32[]{:S(2)}) collective-permute-start(f32[864,128]{1,0:T(8,128)S(1)} %pad_maximum_fusion.9), channel_id=1, source_target_pairs={{0,16},{16,32},{32,48},{48,64},{64,80},{80,96},{96,112},{112,0},{1... | collective-permute-start | bytes 1327112 | tf_op jit(solution)/shard_map/ppermute | solution.py:68
  40.1 1.2 collective-permute-done.9.rest_4_
  41.3 3.3 %collective-permute-start.10 = (f32[1008,128]{1,0:T(8,128)S(1)}, f32[1008,128]{1,0:T(8,128)S(1)}, u32[]{:S(2)}, u32[]{:S(2)}) collective-permute-start(f32[1008,128]{1,0:T(8,128)S(1)} %pad_maximum_fusion), channel_id=1, source_target_pairs={{0,112},{16,0},{32,16},{48,32},{64,48},{80,64},{96,80},{112,96},{1... | collective-permute-start | bytes 1548296 | tf_op jit(solution)/shard_map/ppermute | solution.py:68
  44.7 2.5 %collective-permute-done.16.rest_2_ = f32[1008,128]{1,0:T(8,128)S(1)} collective-permute-done((f32[1008,128]{1,0:T(8,128)}, f32[1008,128]{1,0:T(8,128)S(1)}, u32[]{:S(2)}, u32[]{:S(2)}) %collective-permute-start.16) | collective-permute-done | bytes 516128 | tf_op jit(solution)/shard_map/ppermute | solution.py:68
  47.2 2.7 %collective-permute-start.11 = (f32[1008,128]{1,0:T(8,128)S(1)}, f32[1008,128]{1,0:T(8,128)S(1)}, u32[]{:S(2)}, u32[]{:S(2)}) collective-permute-start(f32[1008,128]{1,0:T(8,128)S(1)} %pad_maximum_fusion.1), channel_id=1, source_target_pairs={{0,16},{16,32},{32,48},{48,64},{64,80},{80,96},{96,112},{112,0},{1... | collective-permute-start | bytes 1548296 | tf_op jit(solution)/shard_map/ppermute | solution.py:68
  50.0 0.0 copy-start.5
  50.0 2.3 %collective-permute-done.17.rest_4_ = f32[1008,128]{1,0:T(8,128)S(1)} collective-permute-done((f32[1008,128]{1,0:T(8,128)S(1)}, f32[1008,128]{1,0:T(8,128)S(1)}, u32[]{:S(2)}, u32[]{:S(2)}) %collective-permute-start.17) | collective-permute-done | bytes 516128 | tf_op jit(solution)/shard_map/ppermute | solution.py:68
  52.4 1.9 %collective-permute-start.18 = (f32[1008,128]{1,0:T(8,128)S(1)}, f32[1008,128]{1,0:T(8,128)S(1)}, u32[]{:S(2)}, u32[]{:S(2)}) collective-permute-start(f32[1008,128]{1,0:T(8,128)S(1)} %pad_maximum_fusion.4), channel_id=1, source_target_pairs={{0,112},{16,0},{32,16},{48,32},{64,48},{80,64},{96,80},{112,96},{1... | collective-permute-start | bytes 1548296 | tf_op jit(solution)/shard_map/ppermute | solution.py:68
  54.3 1.2 collective-permute-start.19
  56.2 16.1 %bulk.1 = (f32[512,128]{1,0:T(8,128)S(1)}, f32[2056,128]{1,0:T(8,128)S(1)}) custom-call(s32[1]{0:T(128)S(6)} %copy.13.count, s32[2048]{0:T(1024)S(1)} %get-tuple-element.79.slots_a, s32[2048]{0:T(1024)S(1)} %get-tuple-element.78.slots_o, s32[512,128]{1,0:T(8,128)S(1)} %bitcast.12, s32[512,128]{1,0:T(8,128)S(1)} %bitcast.7, f32[512,128]{1,0:T(8,128)S(1)} %bitcast.16, ...), custom_call_target="tpu_custom_call" | custom-call | bytes 66000000 | tf_op jit(solution)/shard_map/bulk/pallas_call | solution.py:258
  72.4 15.5 %lead.1 = (f32[576,128]{1,0:T(8,128)S(1)}, f32[576,128]{1,0:T(8,128)S(1)}, f32[576,128]{1,0:T(8,128)S(1)}) custom-call(s32[2048]{0:T(1024)S(1)} %get-tuple-element.79.slots_a, s32[2048]{0:T(1024)S(1)} %get-tuple-element.78.slots_o, s32[512,128]{1,0:T(8,128)S(1)} %bitcast.13, s32[512,128]{1,0:T(8,128)S(1)} %bitcast.8, f32[2056,128]{1,0:T(8,128)S(1)} %get-tuple-element.25.lead), custom_call_target="tpu_custom_call" | custom-call | bytes 39600000 | tf_op jit(solution)/shard_map/lead/pallas_call | solution.py:286
  87.9 0.5 collective-permute-start.4
  88.4 0.0 collective-permute-start.5
  88.5 15.1 %tracers.2 = (f32[1008,128]{1,0:T(8,128)S(1)}, f32[1008,128]{1,0:T(8,128)S(1)}, f32[1008,128]{1,0:T(8,128)S(1)}) custom-call(s32[2048]{0:T(1024)S(1)} %get-tuple-element.79.slots_a, s32[2048]{0:T(1024)S(1)} %get-tuple-element.78.slots_o, s32[512,128]{1,0:T(8,128)S(1)} %bitcast.14, s32[512,128]{1,0:T(8,128)S(1)} %bitcast.9, ...), custom_call_target="tpu_custom_call" | custom-call | bytes 59400000 | tf_op jit(solution)/shard_map/tracers/pallas_call | solution.py:317
  103.6 1.7 %collective-permute-start.12 = (f32[1008,128]{1,0:T(8,128)S(1)}, f32[1008,128]{1,0:T(8,128)S(1)}, u32[]{:S(2)}, u32[]{:S(2)}) collective-permute-start(f32[1008,128]{1,0:T(8,128)S(1)} %get-tuple-element.33), channel_id=1, source_target_pairs={{0,16},{16,32},{32,48},{48,64},{64,80},{80,96},{96,112},{112,0},{1... | collective-permute-start | bytes 1548296 | tf_op jit(solution)/shard_map/ppermute | solution.py:68
  105.3 0.8 collective-permute-start.13
  106.2 15.1 %tracers.3 = (f32[1008,128]{1,0:T(8,128)S(1)}, f32[1008,128]{1,0:T(8,128)S(1)}, f32[1008,128]{1,0:T(8,128)S(1)}) custom-call(s32[2048]{0:T(1024)S(1)} %get-tuple-element.79.slots_a, s32[2048]{0:T(1024)S(1)} %get-tuple-element.78.slots_o, s32[512,128]{1,0:T(8,128)S(1)} %bitcast.15, s32[512,128]{1,0:T(8,128)S(1)} %bitcast.10, ...), custom_call_target="tpu_custom_call" | custom-call | bytes 59400000 | tf_op jit(solution)/shard_map/tracers/pallas_call | solution.py:317
  121.3 0.9 collective-permute-start.20
  122.2 2.0 %collective-permute-start.21 = (f32[1008,128]{1,0:T(8,128)S(1)}, f32[1008,128]{1,0:T(8,128)S(1)}, u32[]{:S(2)}, u32[]{:S(2)}) collective-permute-start(f32[1008,128]{1,0:T(8,128)S(1)} %get-tuple-element.41), channel_id=1, source_target_pairs={{0,112},{16,0},{32,16},{48,32},{64,48},{80,64},{96,80},{112,96},{1... | collective-permute-start | bytes 1548296 | tf_op jit(solution)/shard_map/ppermute | solution.py:68
  124.3 0.1 collective-permute-start.6
  124.6 0.1 collective-permute-start.14
  124.7 4.8 %collective-permute-start.15 = (f32[1008,128]{1,0:T(8,128)S(1)}, f32[1008,128]{1,0:T(8,128)S(1)}, u32[]{:S(2)}, u32[]{:S(2)}) collective-permute-start(f32[1008,128]{1,0:T(8,128)S(1)} %pad_maximum_fusion.3), channel_id=1, source_target_pairs={{0,15},{1,0},{2,1},{3,2},{4,3},{5,4},{6,5},{7,6},{8,7},{9,8},{10,9... | collective-permute-start | bytes 1548296 | tf_op jit(solution)/shard_map/ppermute | solution.py:68
  129.6 1.5 collective-permute-done.21.rest_14_
  131.1 0.1 collective-permute-start.22
  131.2 4.8 %collective-permute-start.23 = (f32[1008,128]{1,0:T(8,128)S(1)}, f32[1008,128]{1,0:T(8,128)S(1)}, u32[]{:S(2)}, u32[]{:S(2)}) collective-permute-start(f32[1008,128]{1,0:T(8,128)S(1)} %pad_maximum_fusion.7), channel_id=1, source_target_pairs={{0,15},{1,0},{2,1},{3,2},{4,3},{5,4},{6,5},{7,6},{8,7},{9,8},{10,9... | collective-permute-start | bytes 1548296 | tf_op jit(solution)/shard_map/ppermute | solution.py:68
  136.1 0.1 collective-permute-start.7
  136.2 18.5 %collective-permute-done.7.rest_1_ = f32[576,128]{1,0:T(8,128)S(1)} collective-permute-done((f32[576,128]{1,0:T(8,128)S(1)}, f32[576,128]{1,0:T(8,128)S(1)}, u32[]{:S(2)}, u32[]{:S(2)}) %collective-permute-start.7) | collective-permute-done | bytes 294944 | tf_op jit(solution)/shard_map/ppermute | solution.py:68
  154.7 0.7 collective-permute-done.22.rest_10_
  155.4 4.4 %unpack.1 = (f32[18,16384]{1,0:T(8,128)}, f32[18,16384]{1,0:T(8,128)}) custom-call(s32[216]{0:T(256)S(1)} %reshape.34.ids_a, s32[216]{0:T(256)S(1)} %reshape.35.ids_o, f32[128,128]{1,0:T(8,128)S(1)} %bitcast.18, f32[128,128]{1,0:T(8,128)S(1)} %bitcast.19, f32[576,128]{1,0:T(8,128)S(1)} %collective-permute-done.6.rest_0_, ...), custom_call_target="tpu_custom_call" | custom-call | bytes 19800000 | tf_op jit(solution)/shard_map/unpack/pallas_call | solution.py:366
  (69 shorter events, 0.8 us)
Async XLA Ops:
  2.2 1.4 copy-start.2
  3.6 1.4 copy-start.3
  5.0 20.5 %copy-start.1 = (s32[65536]{0:T(1024)S(1)}, s32[65536]{0:T(1024)}, u32[]{:S(2)}) copy-start(s32[65536]{0:T(1024)} %param.17) | copy-start | bytes 786436
  5.0 24.1 %copy-start = (s32[65536]{0:T(1024)S(1)}, s32[65536]{0:T(1024)}, u32[]{:S(2)}) copy-start(s32[65536]{0:T(1024)} %param.18) | copy-start | bytes 786436
  8.4 0.8 copy-start.8
  9.2 23.7 %collective-permute-start = (f32[864,128]{1,0:T(8,128)}, f32[864,128]{1,0:T(8,128)}, u32[]{:S(2)}, u32[]{:S(2)}) collective-permute-start(f32[864,128]{1,0:T(8,128)} %get-tuple-element.22), channel_id=1, source_target_pairs={{0,15},{1,0},{2,1},{3,2},{4,3},{5,4},{6,5},{7,6},{8,7},{9,8},{10,9... | collective-permute-start | bytes 1327112 | tf_op jit(solution)/shard_map/ppermute | solution.py:68
  16.0 18.9 %collective-permute-start.1 = (f32[864,128]{1,0:T(8,128)}, f32[864,128]{1,0:T(8,128)}, u32[]{:S(2)}, u32[]{:S(2)}) collective-permute-start(f32[864,128]{1,0:T(8,128)} %get-tuple-element.24), channel_id=1, source_target_pairs={{0,1},{1,2},{2,3},{3,4},{4,5},{5,6},{6,7},{7,8},{8,9},{9,10},{10,1... | collective-permute-start | bytes 1327112 | tf_op jit(solution)/shard_map/ppermute | solution.py:68
  16.0 22.1 %collective-permute-start.8 = (f32[1008,128]{1,0:T(8,128)}, f32[1008,128]{1,0:T(8,128)S(1)}, u32[]{:S(2)}, u32[]{:S(2)}) collective-permute-start(f32[1008,128]{1,0:T(8,128)} %get-tuple-element.30), channel_id=1, source_target_pairs={{0,15},{1,0},{2,1},{3,2},{4,3},{5,4},{6,5},{7,6},{8,7},{9,8},{10,9... | collective-permute-start | bytes 1548296 | tf_op jit(solution)/shard_map/ppermute | solution.py:68
  20.7 20.5 %collective-permute-start.9 = (f32[1008,128]{1,0:T(8,128)}, f32[1008,128]{1,0:T(8,128)S(1)}, u32[]{:S(2)}, u32[]{:S(2)}) collective-permute-start(f32[1008,128]{1,0:T(8,128)} %get-tuple-element.32), channel_id=1, source_target_pairs={{0,1},{1,2},{2,3},{3,4},{4,5},{5,6},{6,7},{7,8},{8,9},{9,10},{10,1... | collective-permute-start | bytes 1548296 | tf_op jit(solution)/shard_map/ppermute | solution.py:68
  20.7 26.5 %collective-permute-start.16 = (f32[1008,128]{1,0:T(8,128)}, f32[1008,128]{1,0:T(8,128)S(1)}, u32[]{:S(2)}, u32[]{:S(2)}) collective-permute-start(f32[1008,128]{1,0:T(8,128)} %get-tuple-element.36), channel_id=1, source_target_pairs={{0,15},{1,0},{2,1},{3,2},{4,3},{5,4},{6,5},{7,6},{8,7},{9,8},{10,9... | collective-permute-start | bytes 1548296 | tf_op jit(solution)/shard_map/ppermute | solution.py:68
  32.8 1.0 copy-start.9
  33.8 18.5 %collective-permute-start.17 = (f32[1008,128]{1,0:T(8,128)S(1)}, f32[1008,128]{1,0:T(8,128)S(1)}, u32[]{:S(2)}, u32[]{:S(2)}) collective-permute-start(f32[1008,128]{1,0:T(8,128)S(1)} %copy-done.9), channel_id=1, source_target_pairs={{0,1},{1,2},{2,3},{3,4},{4,5},{5,6},{6,7},{7,8},{8,9},{9,10},{10,1... | collective-permute-start | bytes 1548296 | tf_op jit(solution)/shard_map/ppermute | solution.py:68
  35.9 18.4 %collective-permute-start.2 = (f32[864,128]{1,0:T(8,128)S(1)}, f32[864,128]{1,0:T(8,128)S(1)}, u32[]{:S(2)}, u32[]{:S(2)}) collective-permute-start(f32[864,128]{1,0:T(8,128)S(1)} %pad_maximum_fusion.8), channel_id=1, source_target_pairs={{0,112},{16,0},{32,16},{48,32},{64,48},{80,64},{96,80},{112,96},{1... | collective-permute-start | bytes 1327112 | tf_op jit(solution)/shard_map/ppermute | solution.py:68
  38.0 18.2 %collective-permute-start.3 = (f32[864,128]{1,0:T(8,128)S(1)}, f32[864,128]{1,0:T(8,128)S(1)}, u32[]{:S(2)}, u32[]{:S(2)}) collective-permute-start(f32[864,128]{1,0:T(8,128)S(1)} %pad_maximum_fusion.9), channel_id=1, source_target_pairs={{0,16},{16,32},{32,48},{48,64},{64,80},{80,96},{96,112},{112,0},{1... | collective-permute-start | bytes 1327112 | tf_op jit(solution)/shard_map/ppermute | solution.py:68
  41.3 47.1 %collective-permute-start.10 = (f32[1008,128]{1,0:T(8,128)S(1)}, f32[1008,128]{1,0:T(8,128)S(1)}, u32[]{:S(2)}, u32[]{:S(2)}) collective-permute-start(f32[1008,128]{1,0:T(8,128)S(1)} %pad_maximum_fusion), channel_id=1, source_target_pairs={{0,112},{16,0},{32,16},{48,32},{64,48},{80,64},{96,80},{112,96},{1... | collective-permute-start | bytes 1548296 | tf_op jit(solution)/shard_map/ppermute | solution.py:68
  44.7 10.8 %copy-start.10 = (s32[2048]{0:T(1024)S(1)}, s32[2048]{0:T(1024)}, u32[]{:S(2)}) copy-start(s32[2048]{0:T(1024)} %reshape.39) | copy-start | bytes 24580
  44.7 10.8 %copy-start.11 = (s32[2048]{0:T(1024)S(1)}, s32[2048]{0:T(1024)}, u32[]{:S(2)}) copy-start(s32[2048]{0:T(1024)} %reshape.41) | copy-start | bytes 24580
  47.2 41.2 %collective-permute-start.11 = (f32[1008,128]{1,0:T(8,128)S(1)}, f32[1008,128]{1,0:T(8,128)S(1)}, u32[]{:S(2)}, u32[]{:S(2)}) collective-permute-start(f32[1008,128]{1,0:T(8,128)S(1)} %pad_maximum_fusion.1), channel_id=1, source_target_pairs={{0,16},{16,32},{32,48},{48,64},{64,80},{80,96},{96,112},{112,0},{1... | collective-permute-start | bytes 1548296 | tf_op jit(solution)/shard_map/ppermute | solution.py:68
  50.0 6.2 %copy-start.4 = (f32[65536]{0:T(1024)S(1)}, f32[65536]{0:T(1024)}, u32[]{:S(2)}) copy-start(f32[65536]{0:T(1024)} %param.19) | copy-start | bytes 786436
  50.0 6.2 %copy-start.5 = (s32[65536]{0:T(1024)S(1)}, s32[65536]{0:T(1024)}, u32[]{:S(2)}) copy-start(s32[65536]{0:T(1024)} %param.20) | copy-start | bytes 786436
  52.4 52.9 %collective-permute-start.18 = (f32[1008,128]{1,0:T(8,128)S(1)}, f32[1008,128]{1,0:T(8,128)S(1)}, u32[]{:S(2)}, u32[]{:S(2)}) collective-permute-start(f32[1008,128]{1,0:T(8,128)S(1)} %pad_maximum_fusion.4), channel_id=1, source_target_pairs={{0,112},{16,0},{32,16},{48,32},{64,48},{80,64},{96,80},{112,96},{1... | collective-permute-start | bytes 1548296 | tf_op jit(solution)/shard_map/ppermute | solution.py:68
  54.3 51.9 %collective-permute-start.19 = (f32[1008,128]{1,0:T(8,128)S(1)}, f32[1008,128]{1,0:T(8,128)S(1)}, u32[]{:S(2)}, u32[]{:S(2)}) collective-permute-start(f32[1008,128]{1,0:T(8,128)S(1)} %pad_maximum_fusion.5), channel_id=1, source_target_pairs={{0,16},{16,32},{32,48},{48,64},{64,80},{80,96},{96,112},{112,0},{1... | collective-permute-start | bytes 1548296 | tf_op jit(solution)/shard_map/ppermute | solution.py:68
  87.9 34.3 %collective-permute-start.4 = (f32[576,128]{1,0:T(8,128)S(1)}, f32[576,128]{1,0:T(8,128)S(1)}, u32[]{:S(2)}, u32[]{:S(2)}) collective-permute-start(f32[576,128]{1,0:T(8,128)S(1)} %get-tuple-element.26), channel_id=1, source_target_pairs={{0,16},{16,32},{32,48},{48,64},{64,80},{80,96},{96,112},{112,0},{1... | collective-permute-start | bytes 884744 | tf_op jit(solution)/shard_map/ppermute | solution.py:68
  88.4 35.9 %collective-permute-start.5 = (f32[576,128]{1,0:T(8,128)S(1)}, f32[576,128]{1,0:T(8,128)S(1)}, u32[]{:S(2)}, u32[]{:S(2)}) collective-permute-start(f32[576,128]{1,0:T(8,128)S(1)} %get-tuple-element.28), channel_id=1, source_target_pairs={{0,112},{16,0},{32,16},{48,32},{64,48},{80,64},{96,80},{112,96},{1... | collective-permute-start | bytes 884744 | tf_op jit(solution)/shard_map/ppermute | solution.py:68
  103.6 20.8 %collective-permute-start.12 = (f32[1008,128]{1,0:T(8,128)S(1)}, f32[1008,128]{1,0:T(8,128)S(1)}, u32[]{:S(2)}, u32[]{:S(2)}) collective-permute-start(f32[1008,128]{1,0:T(8,128)S(1)} %get-tuple-element.33), channel_id=1, source_target_pairs={{0,16},{16,32},{32,48},{48,64},{64,80},{80,96},{96,112},{112,0},{1... | collective-permute-start | bytes 1548296 | tf_op jit(solution)/shard_map/ppermute | solution.py:68
  105.3 19.1 %collective-permute-start.13 = (f32[1008,128]{1,0:T(8,128)S(1)}, f32[1008,128]{1,0:T(8,128)S(1)}, u32[]{:S(2)}, u32[]{:S(2)}) collective-permute-start(f32[1008,128]{1,0:T(8,128)S(1)} %get-tuple-element.35), channel_id=1, source_target_pairs={{0,112},{16,0},{32,16},{48,32},{64,48},{80,64},{96,80},{112,96},{1... | collective-permute-start | bytes 1548296 | tf_op jit(solution)/shard_map/ppermute | solution.py:68
  121.3 8.2 %collective-permute-start.20 = (f32[1008,128]{1,0:T(8,128)S(1)}, f32[1008,128]{1,0:T(8,128)S(1)}, u32[]{:S(2)}, u32[]{:S(2)}) collective-permute-start(f32[1008,128]{1,0:T(8,128)S(1)} %get-tuple-element.39), channel_id=1, source_target_pairs={{0,16},{16,32},{32,48},{48,64},{64,80},{80,96},{96,112},{112,0},{1... | collective-permute-start | bytes 1548296 | tf_op jit(solution)/shard_map/ppermute | solution.py:68
  122.2 8.8 %collective-permute-start.21 = (f32[1008,128]{1,0:T(8,128)S(1)}, f32[1008,128]{1,0:T(8,128)S(1)}, u32[]{:S(2)}, u32[]{:S(2)}) collective-permute-start(f32[1008,128]{1,0:T(8,128)S(1)} %get-tuple-element.41), channel_id=1, source_target_pairs={{0,112},{16,0},{32,16},{48,32},{64,48},{80,64},{96,80},{112,96},{1... | collective-permute-start | bytes 1548296 | tf_op jit(solution)/shard_map/ppermute | solution.py:68
  124.3 11.7 %collective-permute-start.6 = (f32[576,128]{1,0:T(8,128)S(1)}, f32[576,128]{1,0:T(8,128)S(1)}, u32[]{:S(2)}, u32[]{:S(2)}) collective-permute-start(f32[576,128]{1,0:T(8,128)S(1)} %pad_maximum_fusion.10), channel_id=1, source_target_pairs={{0,1},{1,2},{2,3},{3,4},{4,5},{5,6},{6,7},{7,8},{8,9},{9,10},{10,1... | collective-permute-start | bytes 884744 | tf_op jit(solution)/shard_map/ppermute | solution.py:68
  124.6 30.2 %collective-permute-start.14 = (f32[1008,128]{1,0:T(8,128)S(1)}, f32[1008,128]{1,0:T(8,128)S(1)}, u32[]{:S(2)}, u32[]{:S(2)}) collective-permute-start(f32[1008,128]{1,0:T(8,128)S(1)} %pad_maximum_fusion.2), channel_id=1, source_target_pairs={{0,1},{1,2},{2,3},{3,4},{4,5},{5,6},{6,7},{7,8},{8,9},{9,10},{10,1... | collective-permute-start | bytes 1548296 | tf_op jit(solution)/shard_map/ppermute | solution.py:68
  124.7 30.1 %collective-permute-start.15 = (f32[1008,128]{1,0:T(8,128)S(1)}, f32[1008,128]{1,0:T(8,128)S(1)}, u32[]{:S(2)}, u32[]{:S(2)}) collective-permute-start(f32[1008,128]{1,0:T(8,128)S(1)} %pad_maximum_fusion.3), channel_id=1, source_target_pairs={{0,15},{1,0},{2,1},{3,2},{4,3},{5,4},{6,5},{7,6},{8,7},{9,8},{10,9... | collective-permute-start | bytes 1548296 | tf_op jit(solution)/shard_map/ppermute | solution.py:68
  129.6 25.9 %copy-start.6 = (f32[16384]{0:T(1024)S(1)}, f32[16384]{0:T(1024)}, u32[]{:S(2)}) copy-start(f32[16384]{0:T(1024)} %param.13) | copy-start | bytes 196612
  129.6 25.9 %copy-start.7 = (f32[16384]{0:T(1024)S(1)}, f32[16384]{0:T(1024)}, u32[]{:S(2)}) copy-start(f32[16384]{0:T(1024)} %param.14) | copy-start | bytes 196612
  131.1 24.3 %collective-permute-start.22 = (f32[1008,128]{1,0:T(8,128)S(1)}, f32[1008,128]{1,0:T(8,128)S(1)}, u32[]{:S(2)}, u32[]{:S(2)}) collective-permute-start(f32[1008,128]{1,0:T(8,128)S(1)} %pad_maximum_fusion.6), channel_id=1, source_target_pairs={{0,1},{1,2},{2,3},{3,4},{4,5},{5,6},{6,7},{7,8},{8,9},{9,10},{10,1... | collective-permute-start | bytes 1548296 | tf_op jit(solution)/shard_map/ppermute | solution.py:68
  131.2 24.2 %collective-permute-start.23 = (f32[1008,128]{1,0:T(8,128)S(1)}, f32[1008,128]{1,0:T(8,128)S(1)}, u32[]{:S(2)}, u32[]{:S(2)}) collective-permute-start(f32[1008,128]{1,0:T(8,128)S(1)} %pad_maximum_fusion.7), channel_id=1, source_target_pairs={{0,15},{1,0},{2,1},{3,2},{4,3},{5,4},{6,5},{7,6},{8,7},{9,8},{10,9... | collective-permute-start | bytes 1548296 | tf_op jit(solution)/shard_map/ppermute | solution.py:68
  136.1 18.6 %collective-permute-start.7 = (f32[576,128]{1,0:T(8,128)S(1)}, f32[576,128]{1,0:T(8,128)S(1)}, u32[]{:S(2)}, u32[]{:S(2)}) collective-permute-start(f32[576,128]{1,0:T(8,128)S(1)} %pad_maximum_fusion.11), channel_id=1, source_target_pairs={{0,15},{1,0},{2,1},{3,2},{4,3},{5,4},{6,5},{7,6},{8,7},{9,8},{10,9... | collective-permute-start | bytes 884744 | tf_op jit(solution)/shard_map/ppermute | solution.py:68

commit v2 on v1

v2 whole, which is shorter than its diff:
```python
import functools

import jax
import jax.numpy as jnp
import numpy as np
from jax import lax
from jax.experimental import pallas as pl
from jax.experimental.pallas import tpu as pltpu
from jax.sharding import PartitionSpec as P

ITERS = 6
GRP = 32
LANES = 128
CAP = 24
SLOTS = 9 * CAP
LEAD = 6
TRACERS = 14
FLUXES = 18
NEIGHBOURS = ((0, 1), (0, -1), (1, 1), (-1, -1), (-1, 1), (1, -1), (1, 0), (-1, 0))

VMEM = pl.BlockSpec(memory_space=pltpu.VMEM)
SMEM = pl.BlockSpec(memory_space=pltpu.SMEM)
F32 = jnp.float32
BF16 = jnp.bfloat16


def cost(us):
    return pl.CostEstimate(flops=0, bytes_accessed=int(us * 3.3e6), transcendentals=0)


def call(body, name, out_shape, in_specs, scratch=(), us=10):
    return pl.pallas_call(
        body,
        name=name,
        out_shape=out_shape,
        in_specs=in_specs,
        out_specs=jax.tree.map(lambda _: VMEM, out_shape),
        scratch_shapes=list(scratch),
        compiler_params=pltpu.CompilerParams(vmem_limit_bytes=40 * 1024 * 1024),
        cost_estimate=cost(us),
    )


def shape(*dims):
    return jax.ShapeDtypeStruct(dims, F32)


def block_column(ids, n, c):
    return pl.ds(pl.multiple_of(jnp.maximum(ids[n, 0, c], 0) * LANES, LANES), LANES)


def pack_lead_body(ids_a, ids_o, fields_a, fields_o, *rest):
    outs, tops, sems = rest[:3], rest[3:5], rest[5]
    copies = [
        pltpu.make_async_copy(fields.at[pl.ds(0, 8), :], top, sems.at[k])
        for k, (fields, top) in enumerate(zip((fields_a, fields_o), tops))
    ]
    for copy in copies:
        copy.start()
    for copy in copies:
        copy.wait()
    for n in range(9):
        p, q = n // 3, n % 3

        def step(c, _):
            for comp, (ids, top) in enumerate(zip((ids_a, ids_o), tops)):
                v = top[:, block_column(ids, n, c)]
                outs[q][pl.ds(((p * 2 + comp) * CAP + c) * LEAD, LEAD), :] = v[:LEAD]
            return 0

        lax.fori_loop(0, CAP, step, 0, unroll=CAP)


def pack_lead(ids_a, ids_o, fields_a, fields_o):
    hbm = pl.BlockSpec(memory_space=pltpu.HBM)
    return call(
        pack_lead_body,
        "pack_lead",
        (shape(3 * 2 * CAP * LEAD, LANES),) * 3,
        [SMEM, SMEM, hbm, hbm],
        [pltpu.VMEM((8, fields_a.shape[1]), F32)] * 2 + [pltpu.SemaphoreType.DMA((2,))],
        us=2,
    )(ids_a, ids_o, fields_a, fields_o)


def pack_tracers_body(ids_a, ids_o, fields_a, fields_o, *outs):
    for n in range(9):
        p, q = n // 3, n % 3

        def step(c, _):
            for comp, (ids, fields) in enumerate(((ids_a, fields_a), (ids_o, fields_o))):
                col = block_column(ids, n, c)
                row = ((q * 2 + comp) * CAP + c) * TRACERS
                outs[p][pl.ds(row, 2), :] = fields[0:8, col][6:]
                outs[p][pl.ds(row + 2, 8), :] = fields[8:16, col]
                outs[p][pl.ds(row + 10, 4), :] = fields[16:20, col]
            return 0

        lax.fori_loop(0, CAP, step, 0, unroll=8)


def pack_tracers(ids_a, ids_o, fields_a, fields_o):
    outs = (shape(3 * 2 * CAP * TRACERS, LANES),) * 3
    return call(pack_tracers_body, "pack_tracers", outs, [SMEM, SMEM, VMEM, VMEM], us=4)(ids_a, ids_o, fields_a, fields_o)


def hop(value, axis, steps):
    count = lax.axis_size(axis)
    return lax.ppermute(value, axis, [(s, (s + steps) % count) for s in range(count)])


def send(value, p, q):
    nx, ny = lax.axis_size("gx"), lax.axis_size("gy")
    pairs = [(x * ny + y, (x + p) % nx * ny + (y + q) % ny) for x in range(nx) for y in range(ny)]
    return lax.ppermute(value, ("gx", "gy"), pairs)


def exchange(values, sign):
    out = list(values)
    for p, q in NEIGHBOURS:
        n = (p + 1) * 3 + q + 1
        out[n] = send(values[n], sign * p, sign * q)
    return out


def third(value, k):
    size = value.shape[0] // 3
    return value[k * size : (k + 1) * size]


def to_owners(lead, tracers):
    lead = [hop(lead[0], "gy", -1), lead[1], hop(lead[2], "gy", 1)]
    tracers_x = [hop(tracers[0], "gx", -1), tracers[1], hop(tracers[2], "gx", 1)]
    lead[0], lead[2], _ = lax.optimization_barrier((lead[0], lead[2], tracers[1]))
    ahead = hop(jnp.concatenate([third(v, 2) for v in lead]), "gx", 1)
    behind = hop(jnp.concatenate([third(v, 0) for v in lead]), "gx", -1)
    up = hop(jnp.concatenate([third(v, 2) for v in tracers_x]), "gy", 1)
    down = hop(jnp.concatenate([third(v, 0) for v in tracers_x]), "gy", -1)
    return (behind, ahead, *lead), (down, up, *tracers_x)


def join_slabs(pieces, slabs, rows):
    behind, ahead, *came = pieces
    for p in range(3):
        for q in range(3):
            for comp in range(2):
                if p == 1:
                    source, at = came[q], (2 + comp) * rows
                else:
                    source, at = (behind, None, ahead)[p], (q * 2 + comp) * rows
                slabs[comp][pl.ds((p * 3 + q) * rows, rows), :] = source[pl.ds(at, rows), :]


def take_lanes(v, index):
    dims = lax.GatherDimensionNumbers(
        offset_dims=(),
        collapsed_slice_dims=(1,),
        start_index_map=(1,),
        operand_batching_dims=(0,),
        start_indices_batching_dims=(0,),
    )
    return lax.gather(v, index[..., None], dims, (1, 1), mode=lax.GatherScatterMode.PROMISE_IN_BOUNDS)


def gather_row(slab, slots, r, stride, first, lanes, quarter):
    out = None
    index = jnp.broadcast_to(lanes, (8, LANES))
    for j in range(4):
        v = take_lanes(slab[pl.ds(slots[j, r] * stride + first, 8), :], index)
        out = v if out is None else jnp.where(quarter >= j, v, out)
    return out


def odd_arctan_coefficients():
    z_top = 0.325
    nodes = (np.cos((np.arange(400) + 0.5) * np.pi / 400) + 1) / 2 * z_top
    t = np.sqrt(nodes)
    fit = np.polynomial.chebyshev.Chebyshev.fit(nodes, np.arctan(t) / t, 7, domain=[0, z_top])
    return [float(c) for c in fit.convert(kind=np.polynomial.Polynomial).coef]


ARCTAN = odd_arctan_coefficients()


def small_arctan(t):
    z = t * t
    total = jnp.full_like(t, ARCTAN[-1])
    for c in ARCTAN[-2::-1]:
        total = total * z + c
    return t * total


def bulk(a, o):
    shear_x = 6.0 * a[0] - 0.3 * o[0]
    shear_y = 6.0 * a[1] - 0.3 * o[1]
    speed2 = shear_x * shear_x + shear_y * shear_y + 0.25 + 0.1 * a[5] * a[5]
    speed = jnp.sqrt(speed2)
    dtemp = 3.0 * (a[2] - o[2])
    dhum = 0.002 * (a[3] - o[3])
    height = 10.0 * jnp.exp(0.3 * a[4])
    log_height = jnp.log(height * 10000.0)
    log_m = log_height - 0.5 * o[4]
    log_h = log_height - 0.5 * o[5]
    rm = 0.4 / log_m
    rh = 0.4 / log_h
    base = (0.4 * 9.8) * height * (dtemp / 290.0 + 0.61 * dhum) / speed2
    for _ in range(ITERS):
        zeta = jnp.clip(base * rh / (rm * rm), -10.0, 3.0)
        u2 = jnp.sqrt(1.0 - 16.0 * jnp.minimum(zeta, 0.0))
        u = jnp.sqrt(u2)
        one_u = 1.0 + u
        one_u2 = 1.0 + u2
        stable = -5.0 * zeta
        psi_m = jnp.where(
            zeta > 0.0,
            stable,
            jnp.log(one_u * one_u * one_u2 * 0.125) - 2.0 * small_arctan((u - 1.0) / one_u),
        )
        psi_h = jnp.where(zeta > 0.0, stable, 2.0 * jnp.log(one_u2 * 0.5))
        rm = 0.5 * rm + 0.2 / (log_m - psi_m)
        rh = 0.5 * rh + 0.2 / (log_h - psi_h)
    drag = 25.0 * rm * rm * speed
    transfer = 25.0 * rm * rh * speed
    return (drag * shear_x, drag * shear_y, transfer * dtemp, 500.0 * transfer * dhum), transfer


def onehots(lanes_a, lanes_o, column):
    one, zero = jnp.ones((), BF16), jnp.zeros((), BF16)
    a = jnp.where(column == lanes_a.astype(BF16), one, zero)
    o = jnp.where(column == lanes_o.astype(BF16), one, zero)
    return jnp.concatenate([a, o], axis=0)


def two_pieces(v):
    high = v.astype(BF16).astype(F32)
    return high, v - high


def scatter_row(values, lanes_a, lanes_o, column, quarter):
    pieces = [x for v in values for x in two_pieces(v)]
    left = jnp.concatenate([jnp.where(quarter == j, x, 0.0) for j in range(4) for x in pieces], axis=0).astype(BF16)
    right = onehots(lanes_a, lanes_o, column)
    sums = lax.dot_general(left, right, (((1,), (1,)), ((), ())), preferred_element_type=F32)
    rows = 16 * len(values)
    return [
        [sums[rows * j + 16 * k : rows * j + 16 * k + 8] + sums[rows * j + 16 * k + 8 : rows * j + 16 * k + 16] for k in range(len(values))]
        for j in range(4)
    ]


def add_groups(sums, slots_a, slots_o, r, acc_a, acc_o):
    for j in range(4):
        base_a, base_o = slots_a[j, r] * 24, slots_o[j, r] * 24
        for k, x in enumerate(sums[j]):
            acc_a[pl.ds(pl.multiple_of(base_a + 8 * k, 8), 8), :] += x[:, :LANES]
            acc_o[pl.ds(pl.multiple_of(base_o + 8 * k, 8), 8), :] += x[:, LANES:]


def slots_body(ref_a, ref_o, out_a, out_o):
    pick = jnp.where(
        lax.broadcasted_iota(jnp.int32, (8, LANES), 1) == GRP * lax.broadcasted_iota(jnp.int32, (8, LANES), 0), 1.0, 0.0
    ).astype(BF16)
    for ref, out in ((ref_a, out_a), (ref_o, out_o)):
        slot = (ref[...] >> 7).astype(F32).astype(BF16)
        picked = lax.dot_general(pick, slot, (((1,), (1,)), ((), ())), preferred_element_type=F32)
        out[...] = picked.astype(jnp.int32)


def group_slots(refs):
    out = (jax.ShapeDtypeStruct((8, refs[0].shape[0]), jnp.int32),) * 2
    return call(slots_body, "slots", out, [VMEM, VMEM], us=1)(*refs)


def iota_quarter():
    return lax.broadcasted_iota(jnp.int32, (8, LANES), 1) // GRP


def iota_column():
    return lax.broadcasted_iota(jnp.int32, (LANES, LANES), 0).astype(BF16)


def first_body(nrows, count, slots_a, slots_o, ref_a, ref_o, area, mask, *rest):
    pieces, (weight, lead, slab_a, slab_o, cells_a, cells_o) = rest[:5], rest[5:]
    join_slabs(pieces, (slab_a, slab_o), CAP * LEAD)
    quarter = iota_quarter()

    def gather(r, _):
        for ref, slab, slots, cells in ((ref_a, slab_a, slots_a, cells_a), (ref_o, slab_o, slots_o, cells_o)):
            lanes = ref[pl.ds(r, 1), :] & (LANES - 1)
            cells[pl.ds(r, 8, stride=nrows), :] = gather_row(slab, slots, r, LEAD, 0, lanes, quarter)
        return 0

    lax.fori_loop(0, nrows, gather, 0, unroll=32)
    live = count[0]
    depth = 64

    def iterate(i, _):
        row = pl.multiple_of(i * depth, depth)
        a = [cells_a[pl.ds(pl.multiple_of(f * nrows + row, depth), depth), :] for f in range(6)]
        o = [cells_o[pl.ds(pl.multiple_of(f * nrows + row, depth), depth), :] for f in range(6)]
        here = pl.ds(row, depth)
        place = (row + lax.broadcasted_iota(jnp.int32, (depth, LANES), 0)) * LANES
        place = place + lax.broadcasted_iota(jnp.int32, (depth, LANES), 1)
        w = jnp.where((place < live) & (mask[here, :] == 1), area[here, :], 0.0)
        fluxes, transfer = bulk(a, o)
        weight[here, :] = transfer * w
        for k, flux in enumerate(fluxes):
            lead[pl.ds(row * 4 + k, depth, stride=4), :] = flux * w
        return 0

    lax.fori_loop(0, nrows // depth, iterate, 0)


def first(count, slots, refs, area, mask, pieces):
    nrows = area.shape[0]
    return call(
        functools.partial(first_body, nrows),
        "bulk",
        (shape(nrows, LANES), shape(nrows * 4 + 8, LANES)),
        [SMEM] * 3 + [VMEM] * 9,
        [pltpu.VMEM((SLOTS * LEAD + 8, LANES), F32)] * 2 + [pltpu.VMEM((8 * nrows, LANES), F32)] * 2,
        us=20,
    )(count, *slots, *refs, area, mask, *pieces)


def scatter_body(nrows, slots_a, slots_o, ref_a, ref_o, weight, lead, *rest):
    (down, up, *came), outs, slabs, accs = rest[:5], rest[5:14], rest[14:16], rest[16:]
    size = CAP * TRACERS
    for n in range(9):
        p, q = n // 3, n % 3
        for comp in range(2):
            source, at = (came[p], 2 + comp) if q == 1 else ((down, None, up)[q], p * 2 + comp)
            slabs[comp][pl.ds(n * size, size), :] = source[pl.ds(at * size, size), :]
    for acc in accs:
        acc[...] = jnp.zeros_like(acc)
    quarter, column = iota_quarter(), iota_column()

    def step(r, _):
        lanes_a, lanes_o = ref_a[pl.ds(r, 1), :] & (LANES - 1), ref_o[pl.ds(r, 1), :] & (LANES - 1)
        w = jnp.broadcast_to(weight[pl.ds(r, 1), :], (8, LANES))
        values = [lead[pl.ds(r * 4, 8), :]]
        for at in (0, 8):
            a = gather_row(slabs[0], slots_a, r, TRACERS, at, lanes_a, quarter)
            o = gather_row(slabs[1], slots_o, r, TRACERS, at, lanes_o, quarter)
            values.append((a - o) * w)
        add_groups(scatter_row(values, lanes_a, lanes_o, column, quarter), slots_a, slots_o, r, *accs)
        return 0

    lax.fori_loop(0, nrows, step, 0, unroll=32)
    for n in range(9):

        def split(c, _):
            for comp in range(2):
                at = pl.multiple_of((n * CAP + c) * 24, 8)
                to = (comp * CAP + c) * FLUXES
                outs[n][pl.ds(to, 4), :] = accs[comp][pl.ds(at, 8), :][:4]
                outs[n][pl.ds(to + 4, 8), :] = accs[comp][pl.ds(at + 8, 8), :]
                outs[n][pl.ds(to + 12, 6), :] = accs[comp][pl.ds(at + 16, 8), :][:6]
            return 0

        lax.fori_loop(0, CAP, split, 0, unroll=8)


def scatter(slots, refs, weight, lead, pieces):
    nrows = weight.shape[0]
    return call(
        functools.partial(scatter_body, nrows),
        "scatter",
        (shape(2 * CAP * FLUXES, LANES),) * 9,
        [SMEM] * 2 + [VMEM] * 9,
        [pltpu.VMEM((SLOTS * TRACERS + 8, LANES), F32)] * 2 + [pltpu.VMEM((SLOTS * 24, LANES), F32)] * 2,
        us=22,
    )(*slots, *refs, weight, lead, *pieces)


def unpack_body(nblocks, ids_a, ids_o, area_a, area_o, *rest):
    parts, outs, accs = rest[:9], rest[9:11], rest[11:]
    for acc in accs:
        acc[...] = jnp.zeros_like(acc)
    for n in range(9):

        def step(c, _):
            for comp, ids in enumerate((ids_a, ids_o)):
                at = pl.multiple_of(jnp.maximum(ids[n, 0, c], 0) * 24, 8)
                base = (comp * CAP + c) * FLUXES
                for first, rows in ((0, 8), (8, 8), (16, 2)):
                    accs[comp][pl.ds(at + first, rows), :] += parts[n][pl.ds(base + first, rows), :]
            return 0

        lax.fori_loop(0, CAP, step, 0, unroll=8)

    def finish(b, _):
        col = pl.ds(pl.multiple_of(b * LANES, LANES), LANES)
        at = pl.multiple_of(b * 24, 8)
        for comp, area in enumerate((area_a, area_o)):
            for first, rows in ((0, 8), (8, 8), (16, 2)):
                outs[comp][first : first + rows, col] = accs[comp][pl.ds(at + first, rows), :] / area[pl.ds(b, 1), :]
        return 0

    lax.fori_loop(0, nblocks, finish, 0, unroll=8)


def unpack(ids_a, ids_o, area_a, area_o, parts):
    nblocks = area_a.shape[0]
    return call(
        functools.partial(unpack_body, nblocks),
        "unpack",
        (shape(FLUXES, nblocks * LANES),) * 2,
        [SMEM] * 2 + [VMEM] * 11,
        [pltpu.VMEM((nblocks * 24, LANES), F32)] * 2,
        us=5,
    )(ids_a, ids_o, area_a, area_o, *parts)


def shards(fields_a, fields_o, area_a, area_o, send_a, send_o, atm_ref, ocn_ref, cell_area, cell_mask, cell_count):
    refs = (atm_ref.reshape(-1, LANES), ocn_ref.reshape(-1, LANES))
    send_a, send_o = send_a.transpose(1, 0, 2), send_o.transpose(1, 0, 2)
    lead = list(pack_lead(send_a, send_o, fields_a, fields_o))
    lead[1], ids_a, ids_o = lax.optimization_barrier((lead[1], send_a, send_o))
    lead_came, came = to_owners(lead, pack_tracers(ids_a, ids_o, fields_a, fields_o))
    slots = group_slots(refs)
    weight, led = first(cell_count, slots, refs, cell_area.reshape(-1, LANES), cell_mask.reshape(-1, LANES), lead_came)
    back = exchange(scatter(slots, refs, weight, led, came), -1)
    return unpack(send_a, send_o, area_a.reshape(-1, LANES), area_o.reshape(-1, LANES), back)


def solution(mesh):
    both = ("gx", "gy")
    in_specs = (P(None, both), P(None, both), P(both), P(both), P(both, None, None), P(both, None, None)) + (P(both),) * 5
    return jax.shard_map(shards, mesh=mesh, in_specs=in_specs, out_specs=(P(None, both),) * 2, check_vma=False)
```

time: 163 us -> 124 us (0.76); the launches traced: 160 us -> 123 us
  Pallas kernels: 69.5 us -> 48.3 us
  local copies, waits for them, and re-layouts: 14.4 us -> 4.43 us
  starting transfers between devices: 45.7 us -> 40.3 us
    ppermute x24 -> x8, starting transfers between devices: 45.7 us -> 18.6 us  [hop(): lax.ppermute(value, axis, [(s, (s + steps) % count) for s in range(count)])]
    ppermute x0 -> x8, starting transfers between devices: none -> 21.7 us  [send(): return lax.ppermute(value, ('gx', 'gy'), pairs)]
    pallas_call x5, Pallas kernels: 53.4 us -> 32.3 us  [the longest x1 24.5 us: scatter(): call(functools.partial(scatter_body, nrows), 'scatter', (shape(2 * CAP *...]
    ppermute x0 -> x8, waiting for transfers between devices: none -> 15.6 us  [send(): return lax.ppermute(value, ('gx', 'gy'), pairs)]
    ppermute x24 -> x8, waiting for transfers between devices: 26.7 us -> 12.2 us  [hop(): lax.ppermute(value, axis, [(s, (s + steps) % count) for s in range(count)])]
    slice x2 -> x0, local copies, waits for them, and re-layouts: 3.85 us -> none  [shards(): slots = tuple((ref[:, ::GRP].reshape(-1) // LANES for ref in refs))]
    reshape x4 -> x0, local copies, waits for them, and re-layouts: 3.57 us -> none  [the longest x2 3.41 us: shards(): slots = tuple((ref[:, ::GRP].reshape(-1) // LANES for ref in refs))]
    slice x18 -> x5, local copies, waits for them, and re-layouts: 2.36 us -> 0.2 us  [third(): return value[k * size:(k + 1) * size]]
  transfers between devices with their start and end apart: 24 -> 16, of which waited for: 6 -> 6; matrix products, arithmetic and copies ran while one was open for 6% -> 0% of each run, Pallas kernels for 39% -> 13%
where the time goes in v2:
time: 124 us; the launch traced here: 123 us
  Pallas kernels  48.3 us (39%)
  starting transfers between devices  40.3 us (32%)
  waiting for transfers between devices  27.8 us (22%)
  local copies, waits for them, and re-layouts  4.43 us (4%)
  between operations  1.55 us (1%)
    pallas_call x1, Pallas kernels, scatter(): call(functools.partial(scatter_body, nrows), 'scatter', (shape(2 * CAP *...  24.5 us
    ppermute x8, starting transfers between devices, send(): return lax.ppermute(value, ('gx', 'gy'), pairs)  21.7 us
    ppermute x8, starting transfers between devices, hop(): lax.ppermute(value, axis, [(s, (s + steps) % count) for s in range(count)])  18.6 us
    pallas_call x1, Pallas kernels, first(): call(functools.partial(first_body, nrows), 'bulk', (shape(nrows, LANES),...  16 us
    ppermute x8, waiting for transfers between devices, send(): return lax.ppermute(value, ('gx', 'gy'), pairs)  15.6 us
    ppermute x8, waiting for transfers between devices, hop(): lax.ppermute(value, axis, [(s, (s + steps) % count) for s in range(count)])  12.2 us
    unnamed x24, local copies, waits for them, and re-layouts  4.23 us
    pallas_call x1, Pallas kernels, unpack(): call(functools.partial(unpack_body, nblocks), 'unpack', (shape(FLUXES, nb...  4.17 us
  transfers between devices with their start and end apart: 16, of which 6 were waited for; matrix products, arithmetic and copies ran while one was open for 0% of the time, Pallas kernels for 13%

profile of v2, /device:TPU:1, one launch (start us, length us, event | category | flops | bytes accessed | tf_op | source)
XLA Modules:
  0.0 122.6 jit_solution(11004399797694253651)
XLA Ops:
  0.6 1.4 %copy-done = f32[20,16384]{1,0:T(8,128)S(1)} copy-done((f32[20,16384]{1,0:T(8,128)S(1)}, f32[20,16384]{1,0:T(8,128)}, u32[]{:S(2)}) %copy-start) | copy-done | bytes 1310744
  2.0 1.4 %copy-done.1 = f32[20,16384]{1,0:T(8,128)S(1)} copy-done((f32[20,16384]{1,0:T(8,128)S(1)}, f32[20,16384]{1,0:T(8,128)}, u32[]{:S(2)}) %copy-start.1) | copy-done | bytes 1310744
  3.4 0.7 copy-done.8
  4.1 0.7 copy-done.10
  4.8 1.6 %pack_lead.1 = (f32[864,128]{1,0:T(8,128)S(1)}, f32[864,128]{1,0:T(8,128)S(1)}, f32[864,128]{1,0:T(8,128)S(1)}) custom-call(s32[9,1,24]{2,1,0:T(1,128)S(1)} %bitcast.18, s32[9,1,24]{2,1,0:T(1,128)S(1)} %bitcast.21, f32[20,16384]{1,0:T(8,128)S(1)} %copy-done, f32[20,16384]{1,0:T(8,128)S(1)} %copy-done.1), custom_call_target="tpu_custom_call" | custom-call | bytes 6600000 | tf_op jit(solution)/shard_map/pack_lead/pallas_call | solution.py:76
  6.4 1.9 %pack_tracers.1 = (f32[2016,128]{1,0:T(8,128)S(1)}, f32[2016,128]{1,0:T(8,128)S(1)}, f32[2016,128]{1,0:T(8,128)S(1)}) custom-call(s32[9,1,24]{2,1,0:T(1,128)S(1)} %bitcast.19, s32[9,1,24]{2,1,0:T(1,128)S(1)} %bitcast.22, f32[20,16384]{1,0:T(8,128)S(1)} %copy-done, f32[20,16384]{1,0:T(8,128)S(1)} %copy-done.1), custom_call_target="tpu_custom_call" | custom-call | bytes 13200000 | tf_op jit(solution)/shard_map/pack_tracers/pallas_call | solution.py:104
  8.3 1.4 %collective-permute-start.4 = (f32[2016,128]{1,0:T(8,128)S(1)}, f32[2016,128]{1,0:T(8,128)S(1)}, u32[]{:S(2)}, u32[]{:S(2)}) collective-permute-start(f32[2016,128]{1,0:T(8,128)S(1)} %get-tuple-element.39), channel_id=1, source_target_pairs={{0,112},{16,0},{32,16},{48,32},{64,48},{80,64},{96,80},{112,96},{1... | collective-permute-start | bytes 3096584 | tf_op jit(solution)/shard_map/ppermute | solution.py:109
  9.7 1.3 %collective-permute-start.5 = (f32[2016,128]{1,0:T(8,128)S(1)}, f32[2016,128]{1,0:T(8,128)S(1)}, u32[]{:S(2)}, u32[]{:S(2)}) collective-permute-start(f32[2016,128]{1,0:T(8,128)S(1)} %get-tuple-element.40), channel_id=1, source_target_pairs={{0,16},{16,32},{32,48},{48,64},{64,80},{80,96},{96,112},{112,0},{1... | collective-permute-start | bytes 3096584 | tf_op jit(solution)/shard_map/ppermute | solution.py:109
  11.0 6.0 %collective-permute-start = (f32[864,128]{1,0:T(8,128)S(1)}, f32[864,128]{1,0:T(8,128)S(1)}, u32[]{:S(2)}, u32[]{:S(2)}) collective-permute-start(f32[864,128]{1,0:T(8,128)S(1)} %get-tuple-element.28), channel_id=1, source_target_pairs={{0,15},{1,0},{2,1},{3,2},{4,3},{5,4},{6,5},{7,6},{8,7},{9,8},{10,9... | collective-permute-start | bytes 1327112 | tf_op jit(solution)/shard_map/ppermute | solution.py:109
  17.0 0.0 collective-permute-start.1
  17.0 6.6 %collective-permute-done.4.rest_2_ = f32[2016,128]{1,0:T(8,128)S(1)} collective-permute-done((f32[2016,128]{1,0:T(8,128)S(1)}, f32[2016,128]{1,0:T(8,128)S(1)}, u32[]{:S(2)}, u32[]{:S(2)}) %collective-permute-start.4) | collective-permute-done | bytes 1032224 | tf_op jit(solution)/shard_map/ppermute | solution.py:109
  23.7 0.0 collective-permute-done.5.rest_4_
  23.7 0.1 pad_maximum_fusion
  23.8 6.0 %collective-permute-start.6 = (f32[2016,128]{1,0:T(8,128)S(1)}, f32[2016,128]{1,0:T(8,128)S(1)}, u32[]{:S(2)}, u32[]{:S(2)}) collective-permute-start(f32[2016,128]{1,0:T(8,128)S(1)} %pad_maximum_fusion), channel_id=1, source_target_pairs={{0,15},{1,0},{2,1},{3,2},{4,3},{5,4},{6,5},{7,6},{8,7},{9,8},{10,9... | collective-permute-start | bytes 3096584 | tf_op jit(solution)/shard_map/ppermute | solution.py:109
  29.8 0.1 pad_maximum_fusion.1
  29.9 0.1 collective-permute-start.7
  30.0 0.0 copy-start.2
  30.0 0.0 copy-start.3
  30.0 0.0 copy-start.4
  30.0 0.0 copy-start.5
  30.1 0.0 collective-permute-done.rest_2_
  30.1 0.4 collective-permute-done.1.rest_4_
  30.5 3.8 %collective-permute-start.2 = (f32[864,128]{1,0:T(8,128)S(1)}, f32[864,128]{1,0:T(8,128)S(1)}, u32[]{:S(2)}, u32[]{:S(2)}) collective-permute-start(f32[864,128]{1,0:T(8,128)S(1)} %pad_maximum_fusion.2), channel_id=1, source_target_pairs={{0,112},{16,0},{32,16},{48,32},{64,48},{80,64},{96,80},{112,96},{1... | collective-permute-start | bytes 1327112 | tf_op jit(solution)/shard_map/ppermute | solution.py:109
  34.3 0.0 collective-permute-start.3
  35.0 0.2 slots.1
  35.2 5.2 %collective-permute-done.2.rest_0_ = f32[864,128]{1,0:T(8,128)S(1)} collective-permute-done((f32[864,128]{1,0:T(8,128)S(1)}, f32[864,128]{1,0:T(8,128)S(1)}, u32[]{:S(2)}, u32[]{:S(2)}) %collective-permute-start.2) | collective-permute-done | bytes 442400 | tf_op jit(solution)/shard_map/ppermute | solution.py:109
  40.4 0.0 collective-permute-done.3.rest_1_
  40.5 16.0 %bulk.1 = (f32[512,128]{1,0:T(8,128)S(1)}, f32[2056,128]{1,0:T(8,128)S(1)}) custom-call(s32[1]{0:T(128)S(6)} %copy.13.count, s32[8,512]{1,0:T(8,128)S(1)} %get-tuple-element.26.slots_a, s32[8,512]{1,0:T(8,128)S(1)} %get-tuple-element.27.slots_o, s32[512,128]{1,0:T(8,128)S(1)} %bitcast.9, s32[512,128]{1,0:T(8,128)S(1)} %bitcast.12, f32[512,128]{1,0:T(8,128)S(1)} %bitcast.14, ...), custom_call_target="tpu_custom_call" | custom-call | bytes 66000000 | tf_op jit(solution)/shard_map/bulk/pallas_call | solution.py:316
  56.5 0.0 collective-permute-done.7.rest_1_
  56.5 0.0 copy-start.6
  56.5 0.0 copy-start.7
  56.5 0.0 copy-start.9
  56.5 0.0 copy-start.11
  56.5 24.5 %scatter.1 = (f32[864,128]{1,0:T(8,128)S(1)}, f32[864,128]{1,0:T(8,128)S(1)}, f32[864,128]{1,0:T(8,128)S(1)}, f32[864,128]{1,0:T(8,128)S(1)}, f32[864,128]{1,0:T...) custom-call(s32[8,512]{1,0:T(8,128)S(1)} %get-tuple-element.26.slots, ...), custom_call_target="tpu_custom_call" | custom-call | bytes 72600000 | tf_op jit(solution)/shard_map/scatter/pallas_call | solution.py:366
  81.0 0.1 collective-permute-start.8
  81.1 3.1 %collective-permute-start.9 = (f32[864,128]{1,0:T(8,128)S(1)}, f32[864,128]{1,0:T(8,128)S(1)}, u32[]{:S(2)}, u32[]{:S(2)}) collective-permute-start(f32[864,128]{1,0:T(8,128)S(1)} %get-tuple-element.42), channel_id=1, source_target_pairs={{0,16},{1,17},{2,18},{3,19},{4,20},{5,21},{6,22},{7,23},{8,24},{9,... | collective-permute-start | bytes 1327112 | tf_op jit(solution)/shard_map/ppermute | solution.py:115
  84.2 5.8 %collective-permute-start.10 = (f32[864,128]{1,0:T(8,128)S(1)}, f32[864,128]{1,0:T(8,128)S(1)}, u32[]{:S(2)}, u32[]{:S(2)}) collective-permute-start(f32[864,128]{1,0:T(8,128)S(1)} %get-tuple-element.43), channel_id=1, source_target_pairs={{0,31},{1,16},{2,17},{3,18},{4,19},{5,20},{6,21},{7,22},{8,23},{9,... | collective-permute-start | bytes 1327112 | tf_op jit(solution)/shard_map/ppermute | solution.py:115
  90.0 0.0 collective-permute-start.11
  90.0 4.8 %collective-permute-start.12 = (f32[864,128]{1,0:T(8,128)S(1)}, f32[864,128]{1,0:T(8,128)S(1)}, u32[]{:S(2)}, u32[]{:S(2)}) collective-permute-start(f32[864,128]{1,0:T(8,128)S(1)} %get-tuple-element.46), channel_id=1, source_target_pairs={{0,15},{1,0},{2,1},{3,2},{4,3},{5,4},{6,5},{7,6},{8,7},{9,8},{10,9... | collective-permute-start | bytes 1327112 | tf_op jit(solution)/shard_map/ppermute | solution.py:115
  94.8 5.2 %collective-permute-done.8.rest_0_ = f32[864,128]{1,0:T(8,128)S(1)} collective-permute-done((f32[864,128]{1,0:T(8,128)S(1)}, f32[864,128]{1,0:T(8,128)S(1)}, u32[]{:S(2)}, u32[]{:S(2)}) %collective-permute-start.8) | collective-permute-done | bytes 442400 | tf_op jit(solution)/shard_map/ppermute | solution.py:115
  100.0 4.4 %collective-permute-start.14 = (f32[864,128]{1,0:T(8,128)S(1)}, f32[864,128]{1,0:T(8,128)S(1)}, u32[]{:S(2)}, u32[]{:S(2)}) collective-permute-start(f32[864,128]{1,0:T(8,128)S(1)} %get-tuple-element.48), channel_id=1, source_target_pairs={{0,112},{1,113},{2,114},{3,115},{4,116},{5,117},{6,118},{7,119},{8... | collective-permute-start | bytes 1327112 | tf_op jit(solution)/shard_map/ppermute | solution.py:115
  104.4 0.0 collective-permute-done.10.rest_2_
  104.4 3.5 %collective-permute-start.15 = (f32[864,128]{1,0:T(8,128)S(1)}, f32[864,128]{1,0:T(8,128)S(1)}, u32[]{:S(2)}, u32[]{:S(2)}) collective-permute-start(f32[864,128]{1,0:T(8,128)S(1)} %get-tuple-element.49), channel_id=1, source_target_pairs={{0,127},{1,112},{2,113},{3,114},{4,115},{5,116},{6,117},{7,118},{8... | collective-permute-start | bytes 1327112 | tf_op jit(solution)/shard_map/ppermute | solution.py:115
  107.9 3.5 %collective-permute-done.11.rest_3_ = f32[864,128]{1,0:T(8,128)S(1)} collective-permute-done((f32[864,128]{1,0:T(8,128)S(1)}, f32[864,128]{1,0:T(8,128)S(1)}, u32[]{:S(2)}, u32[]{:S(2)}) %collective-permute-start.11) | collective-permute-done | bytes 442400 | tf_op jit(solution)/shard_map/ppermute | solution.py:115
  111.4 0.0 collective-permute-done.12.rest_5_
  111.4 7.0 %collective-permute-done.13.rest_6_ = f32[864,128]{1,0:T(8,128)S(1)} collective-permute-done((f32[864,128]{1,0:T(8,128)S(1)}, f32[864,128]{1,0:T(8,128)S(1)}, u32[]{:S(2)}, u32[]{:S(2)}) %collective-permute-start.13) | collective-permute-done | bytes 442400 | tf_op jit(solution)/shard_map/ppermute | solution.py:115
  118.4 0.0 collective-permute-done.14.rest_7_
  118.4 4.2 %unpack.1 = (f32[18,16384]{1,0:T(8,128)}, f32[18,16384]{1,0:T(8,128)}) custom-call(s32[9,1,24]{2,1,0:T(1,128)S(1)} %bitcast.20, s32[9,1,24]{2,1,0:T(1,128)S(1)} %bitcast.23, f32[128,128]{1,0:T(8,128)S(1)} %bitcast.16, f32[128,128]{1,0:T(8,128)S(1)} %bitcast.17, f32[864,128]{1,0:T(8,128)S(1)} %collective-permute-done.8.rest_0_, ...), custom_call_target="tpu_custom_call" | custom-call | bytes 16500000 | tf_op jit(solution)/shard_map/unpack/pallas_call | solution.py:405
  (23 shorter events, 0.3 us)
Async XLA Ops:
  0.6 1.4 %copy-start = (f32[20,16384]{1,0:T(8,128)S(1)}, f32[20,16384]{1,0:T(8,128)}, u32[]{:S(2)}) copy-start(f32[20,16384]{1,0:T(8,128)} %fields_a.3) | copy-start | bytes 3932164
  2.0 1.4 %copy-start.1 = (f32[20,16384]{1,0:T(8,128)S(1)}, f32[20,16384]{1,0:T(8,128)}, u32[]{:S(2)}) copy-start(f32[20,16384]{1,0:T(8,128)} %fields_o.3) | copy-start | bytes 3932164
  3.4 0.7 copy-start.8
  4.1 0.7 copy-start.10
  8.3 15.3 %collective-permute-start.4 = (f32[2016,128]{1,0:T(8,128)S(1)}, f32[2016,128]{1,0:T(8,128)S(1)}, u32[]{:S(2)}, u32[]{:S(2)}) collective-permute-start(f32[2016,128]{1,0:T(8,128)S(1)} %get-tuple-element.39), channel_id=1, source_target_pairs={{0,112},{16,0},{32,16},{48,32},{64,48},{80,64},{96,80},{112,96},{1... | collective-permute-start | bytes 3096584 | tf_op jit(solution)/shard_map/ppermute | solution.py:109
  9.7 13.9 %collective-permute-start.5 = (f32[2016,128]{1,0:T(8,128)S(1)}, f32[2016,128]{1,0:T(8,128)S(1)}, u32[]{:S(2)}, u32[]{:S(2)}) collective-permute-start(f32[2016,128]{1,0:T(8,128)S(1)} %get-tuple-element.40), channel_id=1, source_target_pairs={{0,16},{16,32},{32,48},{48,64},{64,80},{80,96},{96,112},{112,0},{1... | collective-permute-start | bytes 3096584 | tf_op jit(solution)/shard_map/ppermute | solution.py:109
  11.0 19.0 %collective-permute-start = (f32[864,128]{1,0:T(8,128)S(1)}, f32[864,128]{1,0:T(8,128)S(1)}, u32[]{:S(2)}, u32[]{:S(2)}) collective-permute-start(f32[864,128]{1,0:T(8,128)S(1)} %get-tuple-element.28), channel_id=1, source_target_pairs={{0,15},{1,0},{2,1},{3,2},{4,3},{5,4},{6,5},{7,6},{8,7},{9,8},{10,9... | collective-permute-start | bytes 1327112 | tf_op jit(solution)/shard_map/ppermute | solution.py:109
  17.0 13.5 %collective-permute-start.1 = (f32[864,128]{1,0:T(8,128)S(1)}, f32[864,128]{1,0:T(8,128)S(1)}, u32[]{:S(2)}, u32[]{:S(2)}) collective-permute-start(f32[864,128]{1,0:T(8,128)S(1)} %get-tuple-element.29), channel_id=1, source_target_pairs={{0,1},{1,2},{2,3},{3,4},{4,5},{5,6},{6,7},{7,8},{8,9},{9,10},{10,1... | collective-permute-start | bytes 1327112 | tf_op jit(solution)/shard_map/ppermute | solution.py:109
  23.8 32.6 %collective-permute-start.6 = (f32[2016,128]{1,0:T(8,128)S(1)}, f32[2016,128]{1,0:T(8,128)S(1)}, u32[]{:S(2)}, u32[]{:S(2)}) collective-permute-start(f32[2016,128]{1,0:T(8,128)S(1)} %pad_maximum_fusion), channel_id=1, source_target_pairs={{0,15},{1,0},{2,1},{3,2},{4,3},{5,4},{6,5},{7,6},{8,7},{9,8},{10,9... | collective-permute-start | bytes 3096584 | tf_op jit(solution)/shard_map/ppermute | solution.py:109
  29.9 26.6 %collective-permute-start.7 = (f32[2016,128]{1,0:T(8,128)S(1)}, f32[2016,128]{1,0:T(8,128)S(1)}, u32[]{:S(2)}, u32[]{:S(2)}) collective-permute-start(f32[2016,128]{1,0:T(8,128)S(1)} %pad_maximum_fusion.1), channel_id=1, source_target_pairs={{0,1},{1,2},{2,3},{3,4},{4,5},{5,6},{6,7},{7,8},{8,9},{9,10},{10,1... | collective-permute-start | bytes 3096584 | tf_op jit(solution)/shard_map/ppermute | solution.py:109
  30.0 5.0 %copy-start.2 = (s32[65536]{0:T(1024)S(1)}, s32[65536]{0:T(1024)}, u32[]{:S(2)}) copy-start(s32[65536]{0:T(1024)} %param.17) | copy-start | bytes 786436
  30.0 5.0 %copy-start.3 = (s32[65536]{0:T(1024)S(1)}, s32[65536]{0:T(1024)}, u32[]{:S(2)}) copy-start(s32[65536]{0:T(1024)} %param.18) | copy-start | bytes 786436
  30.0 10.4 %copy-start.4 = (f32[65536]{0:T(1024)S(1)}, f32[65536]{0:T(1024)}, u32[]{:S(2)}) copy-start(f32[65536]{0:T(1024)} %param.19) | copy-start | bytes 786436
  30.0 10.4 %copy-start.5 = (s32[65536]{0:T(1024)S(1)}, s32[65536]{0:T(1024)}, u32[]{:S(2)}) copy-start(s32[65536]{0:T(1024)} %param.20) | copy-start | bytes 786436
  30.5 9.9 %collective-permute-start.2 = (f32[864,128]{1,0:T(8,128)S(1)}, f32[864,128]{1,0:T(8,128)S(1)}, u32[]{:S(2)}, u32[]{:S(2)}) collective-permute-start(f32[864,128]{1,0:T(8,128)S(1)} %pad_maximum_fusion.2), channel_id=1, source_target_pairs={{0,112},{16,0},{32,16},{48,32},{64,48},{80,64},{96,80},{112,96},{1... | collective-permute-start | bytes 1327112 | tf_op jit(solution)/shard_map/ppermute | solution.py:109
  34.3 6.1 %collective-permute-start.3 = (f32[864,128]{1,0:T(8,128)S(1)}, f32[864,128]{1,0:T(8,128)S(1)}, u32[]{:S(2)}, u32[]{:S(2)}) collective-permute-start(f32[864,128]{1,0:T(8,128)S(1)} %pad_maximum_fusion.3), channel_id=1, source_target_pairs={{0,16},{16,32},{32,48},{48,64},{64,80},{80,96},{96,112},{112,0},{1... | collective-permute-start | bytes 1327112 | tf_op jit(solution)/shard_map/ppermute | solution.py:109
  56.5 61.9 %copy-start.6 = (f32[16384]{0:T(1024)S(1)}, f32[16384]{0:T(1024)}, u32[]{:S(2)}) copy-start(f32[16384]{0:T(1024)} %param.13) | copy-start | bytes 196612
  56.5 61.9 %copy-start.7 = (f32[16384]{0:T(1024)S(1)}, f32[16384]{0:T(1024)}, u32[]{:S(2)}) copy-start(f32[16384]{0:T(1024)} %param.14) | copy-start | bytes 196612
  56.5 61.9 %copy-start.9 = (s32[1,9,24]{2,0,1:T(1,128)S(1)}, s32[1,9,24]{2,0,1:T(1,128)}, u32[]{:S(2)}) copy-start(s32[1,9,24]{2,0,1:T(1,128)} %param.15) | copy-start | bytes 2596
  56.5 61.9 %copy-start.11 = (s32[1,9,24]{2,0,1:T(1,128)S(1)}, s32[1,9,24]{2,0,1:T(1,128)}, u32[]{:S(2)}) copy-start(s32[1,9,24]{2,0,1:T(1,128)} %param.16) | copy-start | bytes 2596
  81.0 18.9 %collective-permute-start.8 = (f32[864,128]{1,0:T(8,128)S(1)}, f32[864,128]{1,0:T(8,128)S(1)}, u32[]{:S(2)}, u32[]{:S(2)}) collective-permute-start(f32[864,128]{1,0:T(8,128)S(1)} %get-tuple-element.41), channel_id=1, source_target_pairs={{0,17},{1,18},{2,19},{3,20},{4,21},{5,22},{6,23},{7,24},{8,25},{9,... | collective-permute-start | bytes 1327112 | tf_op jit(solution)/shard_map/ppermute | solution.py:115
  81.1 18.9 %collective-permute-start.9 = (f32[864,128]{1,0:T(8,128)S(1)}, f32[864,128]{1,0:T(8,128)S(1)}, u32[]{:S(2)}, u32[]{:S(2)}) collective-permute-start(f32[864,128]{1,0:T(8,128)S(1)} %get-tuple-element.42), channel_id=1, source_target_pairs={{0,16},{1,17},{2,18},{3,19},{4,20},{5,21},{6,22},{7,23},{8,24},{9,... | collective-permute-start | bytes 1327112 | tf_op jit(solution)/shard_map/ppermute | solution.py:115
  84.2 20.2 %collective-permute-start.10 = (f32[864,128]{1,0:T(8,128)S(1)}, f32[864,128]{1,0:T(8,128)S(1)}, u32[]{:S(2)}, u32[]{:S(2)}) collective-permute-start(f32[864,128]{1,0:T(8,128)S(1)} %get-tuple-element.43), channel_id=1, source_target_pairs={{0,31},{1,16},{2,17},{3,18},{4,19},{5,20},{6,21},{7,22},{8,23},{9,... | collective-permute-start | bytes 1327112 | tf_op jit(solution)/shard_map/ppermute | solution.py:115
  90.0 21.4 %collective-permute-start.11 = (f32[864,128]{1,0:T(8,128)S(1)}, f32[864,128]{1,0:T(8,128)S(1)}, u32[]{:S(2)}, u32[]{:S(2)}) collective-permute-start(f32[864,128]{1,0:T(8,128)S(1)} %get-tuple-element.44), channel_id=1, source_target_pairs={{0,1},{1,2},{2,3},{3,4},{4,5},{5,6},{6,7},{7,8},{8,9},{9,10},{10,1... | collective-permute-start | bytes 1327112 | tf_op jit(solution)/shard_map/ppermute | solution.py:115
  90.0 21.4 %collective-permute-start.12 = (f32[864,128]{1,0:T(8,128)S(1)}, f32[864,128]{1,0:T(8,128)S(1)}, u32[]{:S(2)}, u32[]{:S(2)}) collective-permute-start(f32[864,128]{1,0:T(8,128)S(1)} %get-tuple-element.46), channel_id=1, source_target_pairs={{0,15},{1,0},{2,1},{3,2},{4,3},{5,4},{6,5},{7,6},{8,7},{9,8},{10,9... | collective-permute-start | bytes 1327112 | tf_op jit(solution)/shard_map/ppermute | solution.py:115
  100.0 18.4 %collective-permute-start.13 = (f32[864,128]{1,0:T(8,128)S(1)}, f32[864,128]{1,0:T(8,128)S(1)}, u32[]{:S(2)}, u32[]{:S(2)}) collective-permute-start(f32[864,128]{1,0:T(8,128)S(1)} %get-tuple-element.47), channel_id=1, source_target_pairs={{0,113},{1,114},{2,115},{3,116},{4,117},{5,118},{6,119},{7,120},{8... | collective-permute-start | bytes 1327112 | tf_op jit(solution)/shard_map/ppermute | solution.py:115
  100.0 18.4 %collective-permute-start.14 = (f32[864,128]{1,0:T(8,128)S(1)}, f32[864,128]{1,0:T(8,128)S(1)}, u32[]{:S(2)}, u32[]{:S(2)}) collective-permute-start(f32[864,128]{1,0:T(8,128)S(1)} %get-tuple-element.48), channel_id=1, source_target_pairs={{0,112},{1,113},{2,114},{3,115},{4,116},{5,117},{6,118},{7,119},{8... | collective-permute-start | bytes 1327112 | tf_op jit(solution)/shard_map/ppermute | solution.py:115
  104.4 14.0 %collective-permute-start.15 = (f32[864,128]{1,0:T(8,128)S(1)}, f32[864,128]{1,0:T(8,128)S(1)}, u32[]{:S(2)}, u32[]{:S(2)}) collective-permute-start(f32[864,128]{1,0:T(8,128)S(1)} %get-tuple-element.49), channel_id=1, source_target_pairs={{0,127},{1,112},{2,113},{3,114},{4,115},{5,116},{6,117},{7,118},{8... | collective-permute-start | bytes 1327112 | tf_op jit(solution)/shard_map/ppermute | solution.py:115

commit v3 on v2

v3 whole, which is shorter than its diff:
```python
import functools

import jax
import jax.numpy as jnp
import numpy as np
from jax import lax
from jax.experimental import pallas as pl
from jax.experimental.pallas import tpu as pltpu
from jax.sharding import PartitionSpec as P

ITERS = 6
GRP = 32
LANES = 128
CAP = 24
SLOTS = 9 * CAP
LEAD = 6
TRACERS = 14
FLUXES = 18
MIDDLE = 8
OUTER = 10

HBM = pl.BlockSpec(memory_space=pltpu.HBM)
VMEM = pl.BlockSpec(memory_space=pltpu.VMEM)
SMEM = pl.BlockSpec(memory_space=pltpu.SMEM)
F32 = jnp.float32
BF16 = jnp.bfloat16


def cost(us):
    return pl.CostEstimate(flops=0, bytes_accessed=int(us * 3.3e6), transcendentals=0)


def call(body, name, out_shape, in_specs, scratch=(), us=10, limit=40, out_space=VMEM):
    return pl.pallas_call(
        body,
        name=name,
        out_shape=out_shape,
        in_specs=in_specs,
        out_specs=jax.tree.map(lambda _: out_space, out_shape),
        scratch_shapes=list(scratch),
        compiler_params=pltpu.CompilerParams(vmem_limit_bytes=limit * 1024 * 1024),
        cost_estimate=cost(us),
    )


def shape(*dims):
    return jax.ShapeDtypeStruct(dims, F32)


def block_column(ids, n, c):
    return pl.ds(pl.multiple_of(jnp.maximum(ids[n, 0, c], 0) * LANES, LANES), LANES)


def pack_body(send_a, send_o, fields_a, fields_o, *rest):
    outs, (ids_a, ids_o, top_a, top_o, low_a, low_o), held, in_sems, out_sems = (
        rest[:6],
        rest[6:12],
        rest[12:18],
        rest[18],
        rest[19],
    )
    lead, tracers = held[:3], held[3:]
    count = fields_a.shape[0]
    moves = [(send_a, ids_a), (send_o, ids_o)]
    moves += [(f.at[pl.ds(0, 8), :], to) for f, to in ((fields_a, top_a), (fields_o, top_o))]
    moves += [(f.at[pl.ds(8, count - 8), :], to) for f, to in ((fields_a, low_a), (fields_o, low_o))]
    copies = [pltpu.make_async_copy(source, to, in_sems.at[k]) for k, (source, to) in enumerate(moves)]
    leave = [pltpu.make_async_copy(source, to, out_sems.at[k]) for k, (source, to) in enumerate(zip(held, outs))]
    for copy in copies:
        copy.start()
    for copy in copies[:4]:
        copy.wait()
    sides = ((ids_a, top_a, low_a), (ids_o, top_o, low_o))
    for n in range(9):
        p, q = n // 3, n % 3

        def lead_step(c, _):
            for comp, (ids, top, _) in enumerate(sides):
                v = top[:, block_column(ids, n, c)]
                lead[q][pl.ds(((p * 2 + comp) * CAP + c) * LEAD, LEAD), :] = v[:LEAD]
                tracers[p][pl.ds(((q * 2 + comp) * CAP + c) * TRACERS, 2), :] = v[LEAD:]
            return 0

        lax.fori_loop(0, CAP, lead_step, 0, unroll=CAP)
    for copy in leave[:3]:
        copy.start()
    for copy in copies[4:]:
        copy.wait()
    for n in range(9):
        p, q = n // 3, n % 3

        def step(c, _):
            for comp, (ids, _, low) in enumerate(sides):
                col = block_column(ids, n, c)
                row = ((q * 2 + comp) * CAP + c) * TRACERS + 2
                tracers[p][pl.ds(row, 8), :] = low[0:8, col]
                tracers[p][pl.ds(row + 8, 4), :] = low[8:12, col]
            return 0

        lax.fori_loop(0, CAP, step, 0, unroll=CAP)
        if q == 2:
            leave[3 + p].start()
    for copy in leave:
        copy.wait()


def pack(send_a, send_o, fields_a, fields_o):
    count, columns = fields_a.shape
    outs = (shape(3 * 2 * CAP * LEAD, LANES),) * 3 + (shape(3 * 2 * CAP * TRACERS, LANES),) * 3
    outs = call(
        pack_body,
        "pack",
        outs,
        [HBM] * 4,
        [pltpu.SMEM(send_a.shape, jnp.int32)] * 2
        + [pltpu.VMEM((8, columns), F32)] * 2
        + [pltpu.VMEM((count - 8, columns), F32)] * 2
        + [pltpu.VMEM(o.shape, F32) for o in outs]
        + [pltpu.SemaphoreType.DMA((6,))] * 2,
        us=4,
        limit=63,
        out_space=HBM,
    )(send_a, send_o, fields_a, fields_o)
    return outs[:3], outs[3:]


def hop(value, axis, steps):
    count = lax.axis_size(axis)
    return lax.ppermute(value, axis, [(s, (s + steps) % count) for s in range(count)])


def third(value, k):
    size = value.shape[0] // 3
    return value[k * size : (k + 1) * size]


def two_ways(y_first, x_first, sign):
    y = [hop(y_first[0], "gy", -sign), y_first[1], hop(y_first[2], "gy", sign)]
    x = [hop(x_first[0], "gx", -sign), x_first[1], hop(x_first[2], "gx", sign)]
    sides = [jnp.concatenate([third(v, k) for v in x]) for k in (0, 2)]
    *_, y[0], y[2] = lax.optimization_barrier((*sides, y[0], y[2]))
    ends = [jnp.concatenate([third(v, k) for v in y]) for k in (0, 2)]
    behind, ahead = hop(ends[0], "gx", -sign), hop(ends[1], "gx", sign)
    down, up = hop(sides[0], "gy", -sign), hop(sides[1], "gy", sign)
    return (behind, ahead, *y), (down, up, *x)


def y_first_rows(pieces, p, q, comp, size):
    behind, ahead, *came = pieces
    if p == 1:
        return came[q], (2 + comp) * size
    return (behind, None, ahead)[p], (q * 2 + comp) * size


def x_first_rows(pieces, p, q, comp, size):
    down, up, *came = pieces
    if q == 1:
        return came[p], (2 + comp) * size
    return (down, None, up)[q], (p * 2 + comp) * size


def join_slabs(find, pieces, slabs, rows):
    for n in range(9):
        for comp in range(2):
            source, at = find(pieces, n // 3, n % 3, comp, rows)
            slabs[comp][pl.ds(n * rows, rows), :] = source[pl.ds(at, rows), :]


def take_lanes(v, index):
    dims = lax.GatherDimensionNumbers(
        offset_dims=(),
        collapsed_slice_dims=(1,),
        start_index_map=(1,),
        operand_batching_dims=(0,),
        start_indices_batching_dims=(0,),
    )
    return lax.gather(v, index[..., None], dims, (1, 1), mode=lax.GatherScatterMode.PROMISE_IN_BOUNDS)


def gather_row(slab, slots, r, stride, first, lanes, quarter):
    out = None
    index = jnp.broadcast_to(lanes, (8, LANES))
    for j in range(4):
        v = take_lanes(slab[pl.ds(slots[j, r] * stride + first, 8), :], index)
        out = v if out is None else jnp.where(quarter >= j, v, out)
    return out


def odd_arctan_coefficients():
    z_top = 0.325
    nodes = (np.cos((np.arange(400) + 0.5) * np.pi / 400) + 1) / 2 * z_top
    t = np.sqrt(nodes)
    fit = np.polynomial.chebyshev.Chebyshev.fit(nodes, np.arctan(t) / t, 7, domain=[0, z_top])
    return [float(c) for c in fit.convert(kind=np.polynomial.Polynomial).coef]


ARCTAN = odd_arctan_coefficients()


def small_arctan(t):
    z = t * t
    total = jnp.full_like(t, ARCTAN[-1])
    for c in ARCTAN[-2::-1]:
        total = total * z + c
    return t * total


def bulk(a, o):
    shear_x = 6.0 * a[0] - 0.3 * o[0]
    shear_y = 6.0 * a[1] - 0.3 * o[1]
    speed2 = shear_x * shear_x + shear_y * shear_y + 0.25 + 0.1 * a[5] * a[5]
    speed = jnp.sqrt(speed2)
    dtemp = 3.0 * (a[2] - o[2])
    dhum = 0.002 * (a[3] - o[3])
    height = 10.0 * jnp.exp(0.3 * a[4])
    log_height = jnp.log(height * 10000.0)
    log_m = log_height - 0.5 * o[4]
    log_h = log_height - 0.5 * o[5]
    rm = 0.4 / log_m
    rh = 0.4 / log_h
    base = (0.4 * 9.8) * height * (dtemp / 290.0 + 0.61 * dhum) / speed2
    for _ in range(ITERS):
        zeta = jnp.clip(base * rh / (rm * rm), -10.0, 3.0)
        u2 = jnp.sqrt(1.0 - 16.0 * jnp.minimum(zeta, 0.0))
        u = jnp.sqrt(u2)
        one_u = 1.0 + u
        one_u2 = 1.0 + u2
        stable = -5.0 * zeta
        psi_m = jnp.where(
            zeta > 0.0,
            stable,
            jnp.log(one_u * one_u * one_u2 * 0.125) - 2.0 * small_arctan((u - 1.0) / one_u),
        )
        psi_h = jnp.where(zeta > 0.0, stable, 2.0 * jnp.log(one_u2 * 0.5))
        rm = 0.5 * rm + 0.2 / (log_m - psi_m)
        rh = 0.5 * rh + 0.2 / (log_h - psi_h)
    drag = 25.0 * rm * rm * speed
    transfer = 25.0 * rm * rh * speed
    return (drag * shear_x, drag * shear_y, transfer * dtemp, 500.0 * transfer * dhum), transfer


def onehots(lanes_a, lanes_o, column):
    one, zero = jnp.ones((), BF16), jnp.zeros((), BF16)
    a = jnp.where(column == lanes_a.astype(BF16), one, zero)
    o = jnp.where(column == lanes_o.astype(BF16), one, zero)
    return jnp.concatenate([a, o], axis=0)


def two_pieces(v):
    high = v.astype(BF16).astype(F32)
    return high, v - high


def scatter_row(values, lanes_a, lanes_o, column, quarter):
    def masked(v):
        return [jnp.where(quarter == j, v, 0.0) for j in range(4)]

    halves = []
    for pieces in zip(*(two_pieces(v) for v in values)):
        lead, one, two = map(masked, pieces)
        halves.append(jnp.concatenate([x for pair in zip(one, two) for x in pair] + lead, axis=0).astype(BF16))
    left = jnp.concatenate(halves, axis=1)
    right = onehots(lanes_a, lanes_o, column)
    right = jnp.concatenate([right, right], axis=1)
    sums = lax.dot_general(left, right, (((1,), (1,)), ((), ())), preferred_element_type=F32)
    return [[sums[at : at + 8] for at in (64 + 8 * j, 16 * j, 16 * j + 8)] for j in range(4)]


def add_groups(sums, slots_a, slots_o, r, acc_a, acc_o):
    for j in range(4):
        base_a, base_o = slots_a[j, r] * 24, slots_o[j, r] * 24
        for k, x in enumerate(sums[j]):
            acc_a[pl.ds(pl.multiple_of(base_a + 8 * k, 8), 8), :] += x[:, :LANES]
            acc_o[pl.ds(pl.multiple_of(base_o + 8 * k, 8), 8), :] += x[:, LANES:]


def slots_body(ref_a, ref_o, out_a, out_o):
    pick = jnp.where(
        lax.broadcasted_iota(jnp.int32, (8, LANES), 1) == GRP * lax.broadcasted_iota(jnp.int32, (8, LANES), 0), 1.0, 0.0
    ).astype(BF16)
    for ref, out in ((ref_a, out_a), (ref_o, out_o)):
        slot = (ref[...] >> 7).astype(F32).astype(BF16)
        picked = lax.dot_general(pick, slot, (((1,), (1,)), ((), ())), preferred_element_type=F32)
        out[...] = picked.astype(jnp.int32)


def group_slots(refs):
    out = (jax.ShapeDtypeStruct((8, refs[0].shape[0]), jnp.int32),) * 2
    return call(slots_body, "slots", out, [VMEM, VMEM], us=1)(*refs)


def iota_quarter():
    return lax.broadcasted_iota(jnp.int32, (8, LANES), 1) // GRP


def iota_column():
    return lax.broadcasted_iota(jnp.int32, (LANES, LANES), 0).astype(BF16)


def first_body(nrows, count, slots_a, slots_o, ref_a, ref_o, area, mask, *rest):
    pieces, (weight, lead, slab_a, slab_o, cells_a, cells_o) = rest[:5], rest[5:]
    join_slabs(y_first_rows, pieces, (slab_a, slab_o), CAP * LEAD)
    quarter = iota_quarter()

    def gather(r, _):
        for ref, slab, slots, cells in ((ref_a, slab_a, slots_a, cells_a), (ref_o, slab_o, slots_o, cells_o)):
            lanes = ref[pl.ds(r, 1), :] & (LANES - 1)
            cells[pl.ds(r, 8, stride=nrows), :] = gather_row(slab, slots, r, LEAD, 0, lanes, quarter)
        return 0

    lax.fori_loop(0, nrows, gather, 0, unroll=64)
    live = count[0]
    depth = 64

    def iterate(i, _):
        row = pl.multiple_of(i * depth, depth)
        a = [cells_a[pl.ds(pl.multiple_of(f * nrows + row, depth), depth), :] for f in range(6)]
        o = [cells_o[pl.ds(pl.multiple_of(f * nrows + row, depth), depth), :] for f in range(6)]
        here = pl.ds(row, depth)
        place = (row + lax.broadcasted_iota(jnp.int32, (depth, LANES), 0)) * LANES
        place = place + lax.broadcasted_iota(jnp.int32, (depth, LANES), 1)
        w = jnp.where((place < live) & (mask[here, :] == 1), area[here, :], 0.0)
        fluxes, transfer = bulk(a, o)
        weight[here, :] = transfer * w
        for k, flux in enumerate(fluxes):
            lead[pl.ds(row * 4 + k, depth, stride=4), :] = flux * w
        return 0

    lax.fori_loop(0, nrows // depth, iterate, 0)


def first(count, slots, refs, area, mask, pieces):
    nrows = area.shape[0]
    return call(
        functools.partial(first_body, nrows),
        "bulk",
        (shape(nrows, LANES), shape(nrows * 4 + 8, LANES)),
        [SMEM] * 3 + [VMEM] * 9,
        [pltpu.VMEM((SLOTS * LEAD + 8, LANES), F32)] * 2 + [pltpu.VMEM((8 * nrows, LANES), F32)] * 2,
        us=20,
    )(count, *slots, *refs, area, mask, *pieces)


def scatter_body(nrows, slots_a, slots_o, ref_a, ref_o, weight, lead, *rest):
    pieces, middle, outer, slabs, accs = rest[:5], rest[5:8], rest[8:11], rest[11:13], rest[13:]
    join_slabs(x_first_rows, pieces, slabs, CAP * TRACERS)
    for acc in accs:
        acc[...] = jnp.zeros_like(acc)
    quarter, column = iota_quarter(), iota_column()

    def step(r, _):
        lanes_a, lanes_o = ref_a[pl.ds(r, 1), :] & (LANES - 1), ref_o[pl.ds(r, 1), :] & (LANES - 1)
        w = jnp.broadcast_to(weight[pl.ds(r, 1), :], (8, LANES))
        values = [lead[pl.ds(r * 4, 8), :]]
        for at in (0, 8):
            a = gather_row(slabs[0], slots_a, r, TRACERS, at, lanes_a, quarter)
            o = gather_row(slabs[1], slots_o, r, TRACERS, at, lanes_o, quarter)
            values.append((a - o) * w)
        add_groups(scatter_row(values, lanes_a, lanes_o, column, quarter), slots_a, slots_o, r, *accs)
        return 0

    lax.fori_loop(0, nrows, step, 0, unroll=64)
    for n in range(9):
        p, q = n // 3, n % 3

        def split(c, _):
            for comp in range(2):
                at = pl.multiple_of((n * CAP + c) * 24, 8)
                to = pl.multiple_of(((p * 2 + comp) * CAP + c) * MIDDLE, 8)
                middle[q][pl.ds(to, MIDDLE), :] = accs[comp][pl.ds(at + 8, 8), :]
                to = ((q * 2 + comp) * CAP + c) * OUTER
                outer[p][pl.ds(to, 4), :] = accs[comp][pl.ds(at, 8), :][:4]
                outer[p][pl.ds(to + 4, 6), :] = accs[comp][pl.ds(at + 16, 8), :][:6]
            return 0

        lax.fori_loop(0, CAP, split, 0, unroll=8)


def scatter(slots, refs, weight, lead, pieces):
    nrows = weight.shape[0]
    return call(
        functools.partial(scatter_body, nrows),
        "scatter",
        (shape(3 * 2 * CAP * MIDDLE, LANES),) * 3 + (shape(3 * 2 * CAP * OUTER, LANES),) * 3,
        [SMEM] * 2 + [VMEM] * 9,
        [pltpu.VMEM((SLOTS * TRACERS + 8, LANES), F32)] * 2 + [pltpu.VMEM((SLOTS * 24, LANES), F32)] * 2,
        us=22,
    )(*slots, *refs, weight, lead, *pieces)


def add_middle_body(send_a, send_o, *rest):
    pieces, accs, (ids_a, ids_o, sems) = rest[:5], rest[5:7], rest[7:]
    copies = [pltpu.make_async_copy(s, to, sems.at[k]) for k, (s, to) in enumerate(((send_a, ids_a), (send_o, ids_o)))]
    for copy in copies:
        copy.start()
    for acc in accs:
        acc[...] = jnp.zeros_like(acc)
    for copy in copies:
        copy.wait()
    for n in range(9):

        def step(c, _):
            for comp, ids in enumerate((ids_a, ids_o)):
                at = pl.multiple_of(jnp.maximum(ids[n, 0, c], 0) * MIDDLE, 8)
                source, first = y_first_rows(pieces, n // 3, n % 3, comp, CAP)
                accs[comp][pl.ds(at, 8), :] += source[pl.ds(pl.multiple_of((first + c) * MIDDLE, 8), 8), :]
            return 0

        lax.fori_loop(0, CAP, step, 0, unroll=CAP)


def add_middle(send_a, send_o, nblocks, pieces):
    return call(
        add_middle_body,
        "add_middle",
        (shape(nblocks * MIDDLE, LANES),) * 2,
        [HBM] * 2 + [VMEM] * 5,
        [pltpu.SMEM(send_a.shape, jnp.int32)] * 2 + [pltpu.SemaphoreType.DMA((2,))],
        us=2,
    )(send_a, send_o, *pieces)


def unpack_body(nblocks, send_a, send_o, area_a, area_o, middle_a, middle_o, *rest):
    pieces, outs, accs, held, (ids_a, ids_o, sems, out_sems) = rest[:5], rest[5:7], rest[7:9], rest[9:11], rest[11:]
    copies = [pltpu.make_async_copy(s, to, sems.at[k]) for k, (s, to) in enumerate(((send_a, ids_a), (send_o, ids_o)))]
    for copy in copies:
        copy.start()
    for acc in accs:
        acc[...] = jnp.zeros_like(acc)
    for copy in copies:
        copy.wait()
    for n in range(9):

        def step(c, _):
            for comp, ids in enumerate((ids_a, ids_o)):
                at = pl.multiple_of(jnp.maximum(ids[n, 0, c], 0) * 16, 8)
                source, first = x_first_rows(pieces, n // 3, n % 3, comp, CAP)
                accs[comp][pl.ds(at, 8), :] += source[pl.ds((first + c) * OUTER, 8), :]
                accs[comp][pl.ds(at + 8, 2), :] += source[pl.ds((first + c) * OUTER + 8, 2), :]
            return 0

        lax.fori_loop(0, CAP, step, 0, unroll=CAP)
    quarters = 4
    size = nblocks // quarters
    leave = []
    for k in range(quarters):

        def finish(b, _):
            col = pl.ds(pl.multiple_of(b * LANES, LANES), LANES)
            for comp, (area, middle) in enumerate(((area_a, middle_a), (area_o, middle_o))):
                scale = 1.0 / area[pl.ds(b, 1), :]
                held[comp][0:4, col] = accs[comp][pl.ds(b * 16, 4), :] * scale
                held[comp][4:8, col] = middle[pl.ds(b * MIDDLE, 4), :] * scale
                held[comp][8:12, col] = middle[pl.ds(b * MIDDLE + 4, 4), :] * scale
                held[comp][12:16, col] = accs[comp][pl.ds(b * 16 + 4, 4), :] * scale
                held[comp][16:18, col] = accs[comp][pl.ds(b * 16 + 8, 2), :] * scale
            return 0

        lax.fori_loop(k * size, (k + 1) * size, finish, 0, unroll=8)
        here = pl.ds(k * size * LANES, size * LANES)
        for comp in range(2):
            copy = pltpu.make_async_copy(held[comp].at[:, here], outs[comp].at[:, here], out_sems.at[2 * k + comp])
            copy.start()
            leave.append(copy)
    for copy in leave:
        copy.wait()


def unpack(send_a, send_o, area_a, area_o, middle, outer):
    nblocks = area_a.shape[0]
    columns = nblocks * LANES
    return call(
        functools.partial(unpack_body, nblocks),
        "unpack",
        (shape(FLUXES, columns),) * 2,
        [HBM] * 2 + [VMEM] * 9,
        [pltpu.VMEM((nblocks * 16, LANES), F32)] * 2
        + [pltpu.VMEM((FLUXES, columns), F32)] * 2
        + [pltpu.SMEM(send_a.shape, jnp.int32)] * 2
        + [pltpu.SemaphoreType.DMA((2,)), pltpu.SemaphoreType.DMA((8,))],
        us=4,
        out_space=HBM,
    )(send_a, send_o, area_a, area_o, *add_middle(send_a, send_o, nblocks, middle), *outer)


def shards(fields_a, fields_o, area_a, area_o, send_a, send_o, atm_ref, ocn_ref, cell_area, cell_mask, cell_count):
    refs = (atm_ref.reshape(-1, LANES), ocn_ref.reshape(-1, LANES))
    send_a, send_o = send_a.transpose(1, 0, 2), send_o.transpose(1, 0, 2)
    lead_came, came = two_ways(*pack(send_a, send_o, fields_a, fields_o), 1)
    slots = group_slots(refs)
    weight, led = first(cell_count, slots, refs, cell_area.reshape(-1, LANES), cell_mask.reshape(-1, LANES), lead_came)
    sums = scatter(slots, refs, weight, led, came)
    middle, outer = two_ways(sums[:3], sums[3:], -1)
    return unpack(send_a, send_o, area_a.reshape(-1, LANES), area_o.reshape(-1, LANES), middle, outer)


def solution(mesh):
    both = ("gx", "gy")
    in_specs = (P(None, both), P(None, both), P(both), P(both), P(both, None, None), P(both, None, None)) + (P(both),) * 5
    return jax.shard_map(shards, mesh=mesh, in_specs=in_specs, out_specs=(P(None, both),) * 2, check_vma=False)
```

time: 124 us -> 116 us (0.935)
  local copies, waits for them, and re-layouts: 4.43 us -> 1.52 us
  starting transfers between devices: 40.3 us -> 37.4 us
  Pallas kernels: 48.3 us -> 46.7 us
    ppermute x8 -> x0, starting transfers between devices: 21.7 us -> none  [send(): return lax.ppermute(value, ('gx', 'gy'), pairs)]
    ppermute x8 -> x16, starting transfers between devices: 18.6 us -> 37.4 us  [hop(): lax.ppermute(value, axis, [(s, (s + steps) % count) for s in range(count)])]
    ppermute x8 -> x0, waiting for transfers between devices: 15.6 us -> none  [send(): return lax.ppermute(value, ('gx', 'gy'), pairs)]
    ppermute x8 -> x16, waiting for transfers between devices: 12.2 us -> 27.3 us  [hop(): lax.ppermute(value, axis, [(s, (s + steps) % count) for s in range(count)])]
    unnamed x24 -> x20, local copies, waits for them, and re-layouts: 4.23 us -> 0.06 us
    slice x5 -> x11, local copies, waits for them, and re-layouts: 0.2 us -> 1.46 us  [third(): return value[k * size:(k + 1) * size]]
  transfers between devices with their start and end apart: 16 -> 16, of which waited for: 6 -> 8; matrix products, arithmetic and copies ran while one was open for 0% -> 2% of each run, Pallas kernels for 13% -> 15%
where the time goes in v3:
time: 116 us; the launch traced here: 115 us
  Pallas kernels  46.7 us (40%)
  starting transfers between devices  37.4 us (32%)
  waiting for transfers between devices  27.3 us (24%)
  between operations  1.77 us (2%)
  local copies, waits for them, and re-layouts  1.52 us (1%)
    ppermute x16, starting transfers between devices, hop(): lax.ppermute(value, axis, [(s, (s + steps) % count) for s in range(count)])  37.4 us
    ppermute x16, waiting for transfers between devices, hop(): lax.ppermute(value, axis, [(s, (s + steps) % count) for s in range(count)])  27.3 us
    pallas_call x1, Pallas kernels, scatter(): call(functools.partial(scatter_body, nrows), 'scatter', (shape(3 * 2 * CA...  21.6 us
    pallas_call x1, Pallas kernels, first(): call(functools.partial(first_body, nrows), 'bulk', (shape(nrows, LANES),...  15.3 us
    pallas_call x1, Pallas kernels, pack(): call(pack_body, 'pack', outs, [HBM] * 4, [pltpu.SMEM(send_a.shape, jnp.in...  4.04 us
    pallas_call x1, Pallas kernels, unpack(): call(functools.partial(unpack_body, nblocks), 'unpack', (shape(FLUXES, co...  3.74 us
  transfers between devices with their start and end apart: 16, of which 8 were waited for; matrix products, arithmetic and copies ran while one was open for 2% of the time, Pallas kernels for 15%

profile of v3, /device:TPU:1, one launch (start us, length us, event | category | flops | bytes accessed | tf_op | source)
XLA Modules:
  0.0 115.0 jit_solution(836866330876165860)
XLA Ops:
  0.6 4.0 %pack.1 = (f32[864,128]{1,0:T(8,128)}, f32[864,128]{1,0:T(8,128)}, f32[864,128]{1,0:T(8,128)}, f32[2016,128]{1,0:T(8,128)}, f32[2016,128]{1,0:T(8,128)}, /*index=5*/f32[2016,128]{1,0:T(8,128)}) custom-call(s32[9,1,24]{2,1,0:T(1,128)} %bitcast.18, s32[9,1,24]{2,1,0:T(1,128)} %bitcast.21, f32[20,16384]{1,0:T(8,128)} %fields_a.1, f32[20,16384]{1,0:T(8,128)} %fields_o.1), custom_call_target="tpu_custom_call" | custom-call | bytes 13200000 | tf_op jit(solution)/shard_map/pack/pallas_call | solution.py:110
  4.7 1.4 %collective-permute-start = (f32[2016,128]{1,0:T(8,128)}, f32[2016,128]{1,0:T(8,128)S(1)}, u32[]{:S(2)}, u32[]{:S(2)}) collective-permute-start(f32[2016,128]{1,0:T(8,128)} %get-tuple-element.26), channel_id=1, source_target_pairs={{0,112},{16,0},{32,16},{48,32},{64,48},{80,64},{96,80},{112,96},{1... | collective-permute-start | bytes 3096584 | tf_op jit(solution)/shard_map/ppermute | solution.py:129
  6.1 1.3 %collective-permute-start.1 = (f32[2016,128]{1,0:T(8,128)}, f32[2016,128]{1,0:T(8,128)S(1)}, u32[]{:S(2)}, u32[]{:S(2)}) collective-permute-start(f32[2016,128]{1,0:T(8,128)} %get-tuple-element.28), channel_id=1, source_target_pairs={{0,16},{16,32},{32,48},{48,64},{64,80},{80,96},{96,112},{112,0},{1... | collective-permute-start | bytes 3096584 | tf_op jit(solution)/shard_map/ppermute | solution.py:129
  7.4 6.0 %collective-permute-start.2 = (f32[864,128]{1,0:T(8,128)}, f32[864,128]{1,0:T(8,128)S(1)}, u32[]{:S(2)}, u32[]{:S(2)}) collective-permute-start(f32[864,128]{1,0:T(8,128)} %get-tuple-element.29), channel_id=1, source_target_pairs={{0,15},{1,0},{2,1},{3,2},{4,3},{5,4},{6,5},{7,6},{8,7},{9,8},{10,9... | collective-permute-start | bytes 1327112 | tf_op jit(solution)/shard_map/ppermute | solution.py:129
  13.4 0.0 collective-permute-start.3
  13.4 1.1 fusion.1
  14.5 5.7 %collective-permute-done.rest_2_ = f32[2016,128]{1,0:T(8,128)S(1)} collective-permute-done((f32[2016,128]{1,0:T(8,128)}, f32[2016,128]{1,0:T(8,128)S(1)}, u32[]{:S(2)}, u32[]{:S(2)}) %collective-permute-start) | collective-permute-done | bytes 1032224 | tf_op jit(solution)/shard_map/ppermute | solution.py:129
  20.2 0.0 collective-permute-done.1.rest_4_
  20.3 0.1 pad_maximum_fusion
  20.4 6.0 %collective-permute-start.6 = (f32[2016,128]{1,0:T(8,128)S(1)}, f32[2016,128]{1,0:T(8,128)S(1)}, u32[]{:S(2)}, u32[]{:S(2)}) collective-permute-start(f32[2016,128]{1,0:T(8,128)S(1)} %pad_maximum_fusion), channel_id=1, source_target_pairs={{0,15},{1,0},{2,1},{3,2},{4,3},{5,4},{6,5},{7,6},{8,7},{9,8},{10,9... | collective-permute-start | bytes 3096584 | tf_op jit(solution)/shard_map/ppermute | solution.py:129
  26.4 0.1 pad_maximum_fusion.1
  26.5 0.1 collective-permute-start.7
  26.6 0.0 copy-start.1
  26.6 0.0 copy-start.2
  26.6 0.0 copy-start.4
  26.6 0.0 copy-start.5
  26.7 0.4 collective-permute-done.3.rest_4_
  27.1 3.8 %collective-permute-start.4 = (f32[864,128]{1,0:T(8,128)S(1)}, f32[864,128]{1,0:T(8,128)S(1)}, u32[]{:S(2)}, u32[]{:S(2)}) collective-permute-start(f32[864,128]{1,0:T(8,128)S(1)} %pad_maximum_fusion.6), channel_id=1, source_target_pairs={{0,112},{16,0},{32,16},{48,32},{64,48},{80,64},{96,80},{112,96},{1... | collective-permute-start | bytes 1327112 | tf_op jit(solution)/shard_map/ppermute | solution.py:129
  31.0 0.0 collective-permute-start.5
  31.6 0.2 slots.1
  31.8 5.2 %collective-permute-done.4.rest_0_ = f32[864,128]{1,0:T(8,128)S(1)} collective-permute-done((f32[864,128]{1,0:T(8,128)S(1)}, f32[864,128]{1,0:T(8,128)S(1)}, u32[]{:S(2)}, u32[]{:S(2)}) %collective-permute-start.4) | collective-permute-done | bytes 442400 | tf_op jit(solution)/shard_map/ppermute | solution.py:129
  37.0 0.0 collective-permute-done.5.rest_1_
  37.0 0.0 copy-start
  37.1 15.3 %bulk.1 = (f32[512,128]{1,0:T(8,128)S(1)}, f32[2056,128]{1,0:T(8,128)S(1)}) custom-call(s32[1]{0:T(128)S(6)} %copy.13.count, s32[8,512]{1,0:T(8,128)S(1)} %get-tuple-element.24.slots_a, s32[8,512]{1,0:T(8,128)S(1)} %get-tuple-element.25.slots_o, s32[512,128]{1,0:T(8,128)S(1)} %bitcast.9, s32[512,128]{1,0:T(8,128)S(1)} %bitcast.12, f32[512,128]{1,0:T(8,128)S(1)} %bitcast.14, ...), custom_call_target="tpu_custom_call" | custom-call | bytes 66000000 | tf_op jit(solution)/shard_map/bulk/pallas_call | solution.py:334
  52.4 0.0 collective-permute-done.7.rest_1_
  52.4 21.6 %scatter.1 = (f32[1152,128]{1,0:T(8,128)S(1)}, f32[1152,128]{1,0:T(8,128)S(1)}, f32[1152,128]{1,0:T(8,128)S(1)}, f32[1440,128]{1,0:T(8,128)S(1)}, f32[1440,128]{1,0:T(8,128)S(1)}, /*index=5*/f32[1440,128]{1,0:T(8,128)S(1)}) custom-call(s32[8,512]{1,0:T(8,128)S(1)} %get-tuple-element.24.slots_a, s32[8,512]{1,0:T(8,128)S(1)} %get-tuple-element.25.slots_o, ...), custom_call_target="tpu_custom_call" | custom-call | bytes 72600000 | tf_op jit(solution)/shard_map/scatter/pallas_call | solution.py:381
  74.0 3.9 %collective-permute-start.8 = (f32[1440,128]{1,0:T(8,128)S(1)}, f32[1440,128]{1,0:T(8,128)S(1)}, u32[]{:S(2)}, u32[]{:S(2)}) collective-permute-start(f32[1440,128]{1,0:T(8,128)S(1)} %get-tuple-element.36), channel_id=1, source_target_pairs={{0,16},{16,32},{32,48},{48,64},{64,80},{80,96},{96,112},{112,0},{1... | collective-permute-start | bytes 2211848 | tf_op jit(solution)/shard_map/ppermute | solution.py:129
  77.8 0.2 collective-permute-start.9
  78.0 0.0 collective-permute-start.10
  78.0 4.8 %collective-permute-start.11 = (f32[1152,128]{1,0:T(8,128)S(1)}, f32[1152,128]{1,0:T(8,128)S(1)}, u32[]{:S(2)}, u32[]{:S(2)}) collective-permute-start(f32[1152,128]{1,0:T(8,128)S(1)} %get-tuple-element.40), channel_id=1, source_target_pairs={{0,15},{1,0},{2,1},{3,2},{4,3},{5,4},{6,5},{7,6},{8,7},{9,8},{10,9... | collective-permute-start | bytes 1769480 | tf_op jit(solution)/shard_map/ppermute | solution.py:129
  82.8 3.4 %collective-permute-done.8.rest_2_ = f32[1440,128]{1,0:T(8,128)S(1)} collective-permute-done((f32[1440,128]{1,0:T(8,128)S(1)}, f32[1440,128]{1,0:T(8,128)S(1)}, u32[]{:S(2)}, u32[]{:S(2)}) %collective-permute-start.8) | collective-permute-done | bytes 737312 | tf_op jit(solution)/shard_map/ppermute | solution.py:129
  86.3 2.7 %collective-permute-done.9.rest_4_ = f32[1440,128]{1,0:T(8,128)S(1)} collective-permute-done((f32[1440,128]{1,0:T(8,128)S(1)}, f32[1440,128]{1,0:T(8,128)S(1)}, u32[]{:S(2)}, u32[]{:S(2)}) %collective-permute-start.9) | collective-permute-done | bytes 737312 | tf_op jit(solution)/shard_map/ppermute | solution.py:129
  89.1 0.1 pad_maximum_fusion.2
  89.1 0.1 collective-permute-start.14
  89.2 0.1 pad_maximum_fusion.3
  89.3 5.0 %collective-permute-start.15 = (f32[1440,128]{1,0:T(8,128)S(1)}, f32[1440,128]{1,0:T(8,128)S(1)}, u32[]{:S(2)}, u32[]{:S(2)}) collective-permute-start(f32[1440,128]{1,0:T(8,128)S(1)} %pad_maximum_fusion.3), channel_id=1, source_target_pairs={{0,15},{1,0},{2,1},{3,2},{4,3},{5,4},{6,5},{7,6},{8,7},{9,8},{10,9... | collective-permute-start | bytes 2211848 | tf_op jit(solution)/shard_map/ppermute | solution.py:129
  94.3 0.0 collective-permute-done.10.rest_2_
  94.3 0.0 copy-start.8
  94.3 0.0 copy-start.9
  94.4 4.9 %collective-permute-start.12 = (f32[1152,128]{1,0:T(8,128)S(1)}, f32[1152,128]{1,0:T(8,128)S(1)}, u32[]{:S(2)}, u32[]{:S(2)}) collective-permute-start(f32[1152,128]{1,0:T(8,128)S(1)} %pad_maximum_fusion.4), channel_id=1, source_target_pairs={{0,16},{16,32},{32,48},{48,64},{64,80},{80,96},{96,112},{112,0},{1... | collective-permute-start | bytes 1769480 | tf_op jit(solution)/shard_map/ppermute | solution.py:129
  99.3 0.0 copy-start.6
  99.3 0.0 copy-start.7
  99.3 0.0 collective-permute-start.13
  99.4 6.7 %collective-permute-done.12.rest_0_ = f32[1152,128]{1,0:T(8,128)S(1)} collective-permute-done((f32[1152,128]{1,0:T(8,128)S(1)}, f32[1152,128]{1,0:T(8,128)S(1)}, u32[]{:S(2)}, u32[]{:S(2)}) %collective-permute-start.12) | collective-permute-done | bytes 589856 | tf_op jit(solution)/shard_map/ppermute | solution.py:129
  106.1 2.9 %collective-permute-done.13.rest_1_ = f32[1152,128]{1,0:T(8,128)S(1)} collective-permute-done((f32[1152,128]{1,0:T(8,128)S(1)}, f32[1152,128]{1,0:T(8,128)S(1)}, u32[]{:S(2)}, u32[]{:S(2)}) %collective-permute-start.13) | collective-permute-done | bytes 589856 | tf_op jit(solution)/shard_map/ppermute | solution.py:129
  109.0 1.8 %add_middle.1 = (f32[1024,128]{1,0:T(8,128)S(1)}, f32[1024,128]{1,0:T(8,128)S(1)}) custom-call(s32[9,1,24]{2,1,0:T(1,128)S(1)} %bitcast.19, s32[9,1,24]{2,1,0:T(1,128)S(1)} %bitcast.22, f32[1152,128]{1,0:T(8,128)S(1)} %collective-permute-done.12.rest_0_, f32[1152,128]{1,0:T(8,128)S(1)} %collective-permute-done.13.rest_1_, ...), custom_call_target="tpu_custom_call" | custom-call | bytes 6600000 | tf_op jit(solution)/shard_map/add_middle/pallas_call | solution.py:413
  110.8 0.3 collective-permute-done.14.rest_0_
  111.1 3.7 %unpack.1 = (f32[18,16384]{1,0:T(8,128)}, f32[18,16384]{1,0:T(8,128)}) custom-call(s32[9,1,24]{2,1,0:T(1,128)S(1)} %bitcast.20, s32[9,1,24]{2,1,0:T(1,128)S(1)} %bitcast.23, f32[128,128]{1,0:T(8,128)S(1)} %bitcast.16, f32[128,128]{1,0:T(8,128)S(1)} %bitcast.17, f32[1024,128]{1,0:T(8,128)S(1)} %get-tuple-element.44.middle_a, ...), custom_call_target="tpu_custom_call" | custom-call | bytes 13200000 | tf_op jit(solution)/shard_map/unpack/pallas_call | solution.py:472
  (29 shorter events, 0.5 us)
Async XLA Ops:
  4.7 15.5 %collective-permute-start = (f32[2016,128]{1,0:T(8,128)}, f32[2016,128]{1,0:T(8,128)S(1)}, u32[]{:S(2)}, u32[]{:S(2)}) collective-permute-start(f32[2016,128]{1,0:T(8,128)} %get-tuple-element.26), channel_id=1, source_target_pairs={{0,112},{16,0},{32,16},{48,32},{64,48},{80,64},{96,80},{112,96},{1... | collective-permute-start | bytes 3096584 | tf_op jit(solution)/shard_map/ppermute | solution.py:129
  6.1 14.1 %collective-permute-start.1 = (f32[2016,128]{1,0:T(8,128)}, f32[2016,128]{1,0:T(8,128)S(1)}, u32[]{:S(2)}, u32[]{:S(2)}) collective-permute-start(f32[2016,128]{1,0:T(8,128)} %get-tuple-element.28), channel_id=1, source_target_pairs={{0,16},{16,32},{32,48},{48,64},{64,80},{80,96},{96,112},{112,0},{1... | collective-permute-start | bytes 3096584 | tf_op jit(solution)/shard_map/ppermute | solution.py:129
  7.4 19.3 %collective-permute-start.2 = (f32[864,128]{1,0:T(8,128)}, f32[864,128]{1,0:T(8,128)S(1)}, u32[]{:S(2)}, u32[]{:S(2)}) collective-permute-start(f32[864,128]{1,0:T(8,128)} %get-tuple-element.29), channel_id=1, source_target_pairs={{0,15},{1,0},{2,1},{3,2},{4,3},{5,4},{6,5},{7,6},{8,7},{9,8},{10,9... | collective-permute-start | bytes 1327112 | tf_op jit(solution)/shard_map/ppermute | solution.py:129
  13.4 13.7 %collective-permute-start.3 = (f32[864,128]{1,0:T(8,128)}, f32[864,128]{1,0:T(8,128)S(1)}, u32[]{:S(2)}, u32[]{:S(2)}) collective-permute-start(f32[864,128]{1,0:T(8,128)} %get-tuple-element.30), channel_id=1, source_target_pairs={{0,1},{1,2},{2,3},{3,4},{4,5},{5,6},{6,7},{7,8},{8,9},{9,10},{10,1... | collective-permute-start | bytes 1327112 | tf_op jit(solution)/shard_map/ppermute | solution.py:129
  20.3 6.3 %copy-start.3 = (f32[864,128]{1,0:T(8,128)S(1)}, f32[864,128]{1,0:T(8,128)}, u32[]{:S(2)}) copy-start(f32[864,128]{1,0:T(8,128)} %get-tuple-element.32.rest_3_) | copy-start | bytes 1327108
  20.4 32.0 %collective-permute-start.6 = (f32[2016,128]{1,0:T(8,128)S(1)}, f32[2016,128]{1,0:T(8,128)S(1)}, u32[]{:S(2)}, u32[]{:S(2)}) collective-permute-start(f32[2016,128]{1,0:T(8,128)S(1)} %pad_maximum_fusion), channel_id=1, source_target_pairs={{0,15},{1,0},{2,1},{3,2},{4,3},{5,4},{6,5},{7,6},{8,7},{9,8},{10,9... | collective-permute-start | bytes 3096584 | tf_op jit(solution)/shard_map/ppermute | solution.py:129
  26.5 25.9 %collective-permute-start.7 = (f32[2016,128]{1,0:T(8,128)S(1)}, f32[2016,128]{1,0:T(8,128)S(1)}, u32[]{:S(2)}, u32[]{:S(2)}) collective-permute-start(f32[2016,128]{1,0:T(8,128)S(1)} %pad_maximum_fusion.1), channel_id=1, source_target_pairs={{0,1},{1,2},{2,3},{3,4},{4,5},{5,6},{6,7},{7,8},{8,9},{9,10},{10,1... | collective-permute-start | bytes 3096584 | tf_op jit(solution)/shard_map/ppermute | solution.py:129
  26.6 5.0 %copy-start.1 = (s32[65536]{0:T(1024)S(1)}, s32[65536]{0:T(1024)}, u32[]{:S(2)}) copy-start(s32[65536]{0:T(1024)} %param.17) | copy-start | bytes 786436
  26.6 5.0 %copy-start.2 = (s32[65536]{0:T(1024)S(1)}, s32[65536]{0:T(1024)}, u32[]{:S(2)}) copy-start(s32[65536]{0:T(1024)} %param.18) | copy-start | bytes 786436
  26.6 10.4 %copy-start.4 = (f32[65536]{0:T(1024)S(1)}, f32[65536]{0:T(1024)}, u32[]{:S(2)}) copy-start(f32[65536]{0:T(1024)} %param.19) | copy-start | bytes 786436
  26.6 10.4 %copy-start.5 = (s32[65536]{0:T(1024)S(1)}, s32[65536]{0:T(1024)}, u32[]{:S(2)}) copy-start(s32[65536]{0:T(1024)} %param.20) | copy-start | bytes 786436
  27.1 9.9 %collective-permute-start.4 = (f32[864,128]{1,0:T(8,128)S(1)}, f32[864,128]{1,0:T(8,128)S(1)}, u32[]{:S(2)}, u32[]{:S(2)}) collective-permute-start(f32[864,128]{1,0:T(8,128)S(1)} %pad_maximum_fusion.6), channel_id=1, source_target_pairs={{0,112},{16,0},{32,16},{48,32},{64,48},{80,64},{96,80},{112,96},{1... | collective-permute-start | bytes 1327112 | tf_op jit(solution)/shard_map/ppermute | solution.py:129
  31.0 6.1 %collective-permute-start.5 = (f32[864,128]{1,0:T(8,128)S(1)}, f32[864,128]{1,0:T(8,128)S(1)}, u32[]{:S(2)}, u32[]{:S(2)}) collective-permute-start(f32[864,128]{1,0:T(8,128)S(1)} %pad_maximum_fusion.7), channel_id=1, source_target_pairs={{0,16},{16,32},{32,48},{48,64},{64,80},{80,96},{96,112},{112,0},{1... | collective-permute-start | bytes 1327112 | tf_op jit(solution)/shard_map/ppermute | solution.py:129
  37.0 15.4 %copy-start = (f32[2016,128]{1,0:T(8,128)S(1)}, f32[2016,128]{1,0:T(8,128)}, u32[]{:S(2)}) copy-start(f32[2016,128]{1,0:T(8,128)} %get-tuple-element.27.rest_3_) | copy-start | bytes 3096580
  74.0 12.3 %collective-permute-start.8 = (f32[1440,128]{1,0:T(8,128)S(1)}, f32[1440,128]{1,0:T(8,128)S(1)}, u32[]{:S(2)}, u32[]{:S(2)}) collective-permute-start(f32[1440,128]{1,0:T(8,128)S(1)} %get-tuple-element.36), channel_id=1, source_target_pairs={{0,16},{16,32},{32,48},{48,64},{64,80},{80,96},{96,112},{112,0},{1... | collective-permute-start | bytes 2211848 | tf_op jit(solution)/shard_map/ppermute | solution.py:129
  77.8 11.2 %collective-permute-start.9 = (f32[1440,128]{1,0:T(8,128)S(1)}, f32[1440,128]{1,0:T(8,128)S(1)}, u32[]{:S(2)}, u32[]{:S(2)}) collective-permute-start(f32[1440,128]{1,0:T(8,128)S(1)} %get-tuple-element.38), channel_id=1, source_target_pairs={{0,112},{16,0},{32,16},{48,32},{64,48},{80,64},{96,80},{112,96},{1... | collective-permute-start | bytes 2211848 | tf_op jit(solution)/shard_map/ppermute | solution.py:129
  78.0 16.3 %collective-permute-start.10 = (f32[1152,128]{1,0:T(8,128)S(1)}, f32[1152,128]{1,0:T(8,128)S(1)}, u32[]{:S(2)}, u32[]{:S(2)}) collective-permute-start(f32[1152,128]{1,0:T(8,128)S(1)} %get-tuple-element.39), channel_id=1, source_target_pairs={{0,1},{1,2},{2,3},{3,4},{4,5},{5,6},{6,7},{7,8},{8,9},{9,10},{10,1... | collective-permute-start | bytes 1769480 | tf_op jit(solution)/shard_map/ppermute | solution.py:129
  78.0 16.3 %collective-permute-start.11 = (f32[1152,128]{1,0:T(8,128)S(1)}, f32[1152,128]{1,0:T(8,128)S(1)}, u32[]{:S(2)}, u32[]{:S(2)}) collective-permute-start(f32[1152,128]{1,0:T(8,128)S(1)} %get-tuple-element.40), channel_id=1, source_target_pairs={{0,15},{1,0},{2,1},{3,2},{4,3},{5,4},{6,5},{7,6},{8,7},{9,8},{10,9... | collective-permute-start | bytes 1769480 | tf_op jit(solution)/shard_map/ppermute | solution.py:129
  89.1 22.0 %collective-permute-start.14 = (f32[1440,128]{1,0:T(8,128)S(1)}, f32[1440,128]{1,0:T(8,128)S(1)}, u32[]{:S(2)}, u32[]{:S(2)}) collective-permute-start(f32[1440,128]{1,0:T(8,128)S(1)} %pad_maximum_fusion.2), channel_id=1, source_target_pairs={{0,1},{1,2},{2,3},{3,4},{4,5},{5,6},{6,7},{7,8},{8,9},{9,10},{10,1... | collective-permute-start | bytes 2211848 | tf_op jit(solution)/shard_map/ppermute | solution.py:129
  89.3 21.8 %collective-permute-start.15 = (f32[1440,128]{1,0:T(8,128)S(1)}, f32[1440,128]{1,0:T(8,128)S(1)}, u32[]{:S(2)}, u32[]{:S(2)}) collective-permute-start(f32[1440,128]{1,0:T(8,128)S(1)} %pad_maximum_fusion.3), channel_id=1, source_target_pairs={{0,15},{1,0},{2,1},{3,2},{4,3},{5,4},{6,5},{7,6},{8,7},{9,8},{10,9... | collective-permute-start | bytes 2211848 | tf_op jit(solution)/shard_map/ppermute | solution.py:129
  94.3 14.6 %copy-start.8 = (s32[1,9,24]{2,0,1:T(1,128)S(1)}, s32[1,9,24]{2,0,1:T(1,128)}, u32[]{:S(2)}) copy-start(s32[1,9,24]{2,0,1:T(1,128)} %param.15) | copy-start | bytes 2596
  94.3 14.6 %copy-start.9 = (s32[1,9,24]{2,0,1:T(1,128)S(1)}, s32[1,9,24]{2,0,1:T(1,128)}, u32[]{:S(2)}) copy-start(s32[1,9,24]{2,0,1:T(1,128)} %param.16) | copy-start | bytes 2596
  94.4 11.7 %collective-permute-start.12 = (f32[1152,128]{1,0:T(8,128)S(1)}, f32[1152,128]{1,0:T(8,128)S(1)}, u32[]{:S(2)}, u32[]{:S(2)}) collective-permute-start(f32[1152,128]{1,0:T(8,128)S(1)} %pad_maximum_fusion.4), channel_id=1, source_target_pairs={{0,16},{16,32},{32,48},{48,64},{64,80},{80,96},{96,112},{112,0},{1... | collective-permute-start | bytes 1769480 | tf_op jit(solution)/shard_map/ppermute | solution.py:129
  99.3 11.8 %copy-start.6 = (f32[16384]{0:T(1024)S(1)}, f32[16384]{0:T(1024)}, u32[]{:S(2)}) copy-start(f32[16384]{0:T(1024)} %param.13) | copy-start | bytes 196612
  99.3 11.8 %copy-start.7 = (f32[16384]{0:T(1024)S(1)}, f32[16384]{0:T(1024)}, u32[]{:S(2)}) copy-start(f32[16384]{0:T(1024)} %param.14) | copy-start | bytes 196612
  99.3 9.6 %collective-permute-start.13 = (f32[1152,128]{1,0:T(8,128)S(1)}, f32[1152,128]{1,0:T(8,128)S(1)}, u32[]{:S(2)}, u32[]{:S(2)}) collective-permute-start(f32[1152,128]{1,0:T(8,128)S(1)} %pad_maximum_fusion.5), channel_id=1, source_target_pairs={{0,112},{16,0},{32,16},{48,32},{64,48},{80,64},{96,80},{112,96},{1... | collective-permute-start | bytes 1769480 | tf_op jit(solution)/shard_map/ppermute | solution.py:129

commit v4 on v3

--- a/solution.py
+++ b/solution.py
@@ -308,7 +308,7 @@
             cells[pl.ds(r, 8, stride=nrows), :] = gather_row(slab, slots, r, LEAD, 0, lanes, quarter)
         return 0
 
-    lax.fori_loop(0, nrows, gather, 0, unroll=64)
+    lax.fori_loop(0, nrows, gather, 0, unroll=128)
     live = count[0]
     depth = 64
 
@@ -359,7 +359,7 @@
         add_groups(scatter_row(values, lanes_a, lanes_o, column, quarter), slots_a, slots_o, r, *accs)
         return 0
 
-    lax.fori_loop(0, nrows, step, 0, unroll=64)
+    lax.fori_loop(0, nrows, step, 0, unroll=128)
     for n in range(9):
         p, q = n // 3, n % 3
 

time: 116 us -> 116 us (level)
  Pallas kernels: 46.7 us -> 45.5 us
where the time goes in v4:
time: 116 us; the launch traced here: 114 us
  Pallas kernels  45.5 us (39%)
  starting transfers between devices  38.1 us (33%)
  waiting for transfers between devices  27.1 us (23%)
  between operations  1.79 us (2%)
  local copies, waits for them, and re-layouts  1.52 us (1%)
    ppermute x16, starting transfers between devices, hop(): lax.ppermute(value, axis, [(s, (s + steps) % count) for s in range(count)])  38.1 us
    ppermute x16, waiting for transfers between devices, hop(): lax.ppermute(value, axis, [(s, (s + steps) % count) for s in range(count)])  27.1 us
    pallas_call x1, Pallas kernels, scatter(): call(functools.partial(scatter_body, nrows), 'scatter', (shape(3 * 2 * CA...  20.7 us
    pallas_call x1, Pallas kernels, first(): call(functools.partial(first_body, nrows), 'bulk', (shape(nrows, LANES),...  15 us
    pallas_call x1, Pallas kernels, pack(): call(pack_body, 'pack', outs, [HBM] * 4, [pltpu.SMEM(send_a.shape, jnp.in...  4.04 us
    pallas_call x1, Pallas kernels, unpack(): call(functools.partial(unpack_body, nblocks), 'unpack', (shape(FLUXES, co...  3.74 us
  transfers between devices with their start and end apart: 16, of which 8 were waited for; matrix products, arithmetic and copies ran while one was open for 2% of the time, Pallas kernels for 15%

profile of v4, /device:TPU:1, one launch (start us, length us, event | category | flops | bytes accessed | tf_op | source)
XLA Modules:
  0.0 114.3 jit_solution(15811189988279590978)
XLA Ops:
  0.6 4.0 %pack.1 = (f32[864,128]{1,0:T(8,128)}, f32[864,128]{1,0:T(8,128)}, f32[864,128]{1,0:T(8,128)}, f32[2016,128]{1,0:T(8,128)}, f32[2016,128]{1,0:T(8,128)}, /*index=5*/f32[2016,128]{1,0:T(8,128)}) custom-call(s32[9,1,24]{2,1,0:T(1,128)} %bitcast.18, s32[9,1,24]{2,1,0:T(1,128)} %bitcast.21, f32[20,16384]{1,0:T(8,128)} %fields_a.1, f32[20,16384]{1,0:T(8,128)} %fields_o.1), custom_call_target="tpu_custom_call" | custom-call | bytes 13200000 | tf_op jit(solution)/shard_map/pack/pallas_call | solution.py:110
  4.7 1.4 %collective-permute-start = (f32[2016,128]{1,0:T(8,128)}, f32[2016,128]{1,0:T(8,128)S(1)}, u32[]{:S(2)}, u32[]{:S(2)}) collective-permute-start(f32[2016,128]{1,0:T(8,128)} %get-tuple-element.26), channel_id=1, source_target_pairs={{0,112},{16,0},{32,16},{48,32},{64,48},{80,64},{96,80},{112,96},{1... | collective-permute-start | bytes 3096584 | tf_op jit(solution)/shard_map/ppermute | solution.py:129
  6.1 1.3 %collective-permute-start.1 = (f32[2016,128]{1,0:T(8,128)}, f32[2016,128]{1,0:T(8,128)S(1)}, u32[]{:S(2)}, u32[]{:S(2)}) collective-permute-start(f32[2016,128]{1,0:T(8,128)} %get-tuple-element.28), channel_id=1, source_target_pairs={{0,16},{16,32},{32,48},{48,64},{64,80},{80,96},{96,112},{112,0},{1... | collective-permute-start | bytes 3096584 | tf_op jit(solution)/shard_map/ppermute | solution.py:129
  7.4 6.0 %collective-permute-start.2 = (f32[864,128]{1,0:T(8,128)}, f32[864,128]{1,0:T(8,128)S(1)}, u32[]{:S(2)}, u32[]{:S(2)}) collective-permute-start(f32[864,128]{1,0:T(8,128)} %get-tuple-element.29), channel_id=1, source_target_pairs={{0,15},{1,0},{2,1},{3,2},{4,3},{5,4},{6,5},{7,6},{8,7},{9,8},{10,9... | collective-permute-start | bytes 1327112 | tf_op jit(solution)/shard_map/ppermute | solution.py:129
  13.4 0.0 collective-permute-start.3
  13.4 1.1 fusion.1
  14.5 5.7 %collective-permute-done.rest_2_ = f32[2016,128]{1,0:T(8,128)S(1)} collective-permute-done((f32[2016,128]{1,0:T(8,128)}, f32[2016,128]{1,0:T(8,128)S(1)}, u32[]{:S(2)}, u32[]{:S(2)}) %collective-permute-start) | collective-permute-done | bytes 1032224 | tf_op jit(solution)/shard_map/ppermute | solution.py:129
  20.2 0.0 collective-permute-done.1.rest_4_
  20.3 0.1 pad_maximum_fusion
  20.4 6.0 %collective-permute-start.6 = (f32[2016,128]{1,0:T(8,128)S(1)}, f32[2016,128]{1,0:T(8,128)S(1)}, u32[]{:S(2)}, u32[]{:S(2)}) collective-permute-start(f32[2016,128]{1,0:T(8,128)S(1)} %pad_maximum_fusion), channel_id=1, source_target_pairs={{0,15},{1,0},{2,1},{3,2},{4,3},{5,4},{6,5},{7,6},{8,7},{9,8},{10,9... | collective-permute-start | bytes 3096584 | tf_op jit(solution)/shard_map/ppermute | solution.py:129
  26.4 0.1 pad_maximum_fusion.1
  26.5 0.3 collective-permute-start.7
  26.8 0.0 copy-start.1
  26.8 0.0 copy-start.2
  26.8 0.0 copy-start.4
  26.8 0.0 copy-start.5
  26.8 0.0 collective-permute-done.2.rest_2_
  26.8 0.2 collective-permute-done.3.rest_4_
  27.1 4.0 %collective-permute-start.4 = (f32[864,128]{1,0:T(8,128)S(1)}, f32[864,128]{1,0:T(8,128)S(1)}, u32[]{:S(2)}, u32[]{:S(2)}) collective-permute-start(f32[864,128]{1,0:T(8,128)S(1)} %pad_maximum_fusion.6), channel_id=1, source_target_pairs={{0,112},{16,0},{32,16},{48,32},{64,48},{80,64},{96,80},{112,96},{1... | collective-permute-start | bytes 1327112 | tf_op jit(solution)/shard_map/ppermute | solution.py:129
  31.1 0.0 collective-permute-start.5
  31.8 0.2 slots.1
  32.0 5.0 %collective-permute-done.4.rest_0_ = f32[864,128]{1,0:T(8,128)S(1)} collective-permute-done((f32[864,128]{1,0:T(8,128)S(1)}, f32[864,128]{1,0:T(8,128)S(1)}, u32[]{:S(2)}, u32[]{:S(2)}) %collective-permute-start.4) | collective-permute-done | bytes 442400 | tf_op jit(solution)/shard_map/ppermute | solution.py:129
  37.0 0.0 collective-permute-done.5.rest_1_
  37.0 0.0 copy-start
  37.1 15.0 %bulk.1 = (f32[512,128]{1,0:T(8,128)S(1)}, f32[2056,128]{1,0:T(8,128)S(1)}) custom-call(s32[1]{0:T(128)S(6)} %copy.13.count, s32[8,512]{1,0:T(8,128)S(1)} %get-tuple-element.24.slots_a, s32[8,512]{1,0:T(8,128)S(1)} %get-tuple-element.25.slots_o, s32[512,128]{1,0:T(8,128)S(1)} %bitcast.9, s32[512,128]{1,0:T(8,128)S(1)} %bitcast.12, f32[512,128]{1,0:T(8,128)S(1)} %bitcast.14, ...), custom_call_target="tpu_custom_call" | custom-call | bytes 66000000 | tf_op jit(solution)/shard_map/bulk/pallas_call | solution.py:334
  52.0 0.0 collective-permute-done.6.rest_0_
  52.0 0.0 collective-permute-done.7.rest_1_
  52.1 20.7 %scatter.1 = (f32[1152,128]{1,0:T(8,128)S(1)}, f32[1152,128]{1,0:T(8,128)S(1)}, f32[1152,128]{1,0:T(8,128)S(1)}, f32[1440,128]{1,0:T(8,128)S(1)}, f32[1440,128]{1,0:T(8,128)S(1)}, /*index=5*/f32[1440,128]{1,0:T(8,128)S(1)}) custom-call(s32[8,512]{1,0:T(8,128)S(1)} %get-tuple-element.24.slots_a, s32[8,512]{1,0:T(8,128)S(1)} %get-tuple-element.25.slots_o, ...), custom_call_target="tpu_custom_call" | custom-call | bytes 72600000 | tf_op jit(solution)/shard_map/scatter/pallas_call | solution.py:381
  72.8 4.4 %collective-permute-start.8 = (f32[1440,128]{1,0:T(8,128)S(1)}, f32[1440,128]{1,0:T(8,128)S(1)}, u32[]{:S(2)}, u32[]{:S(2)}) collective-permute-start(f32[1440,128]{1,0:T(8,128)S(1)} %get-tuple-element.36), channel_id=1, source_target_pairs={{0,16},{16,32},{32,48},{48,64},{64,80},{80,96},{96,112},{112,0},{1... | collective-permute-start | bytes 2211848 | tf_op jit(solution)/shard_map/ppermute | solution.py:129
  77.2 4.8 %collective-permute-start.11 = (f32[1152,128]{1,0:T(8,128)S(1)}, f32[1152,128]{1,0:T(8,128)S(1)}, u32[]{:S(2)}, u32[]{:S(2)}) collective-permute-start(f32[1152,128]{1,0:T(8,128)S(1)} %get-tuple-element.40), channel_id=1, source_target_pairs={{0,15},{1,0},{2,1},{3,2},{4,3},{5,4},{6,5},{7,6},{8,7},{9,8},{10,9... | collective-permute-start | bytes 1769480 | tf_op jit(solution)/shard_map/ppermute | solution.py:129
  82.0 3.5 %collective-permute-done.8.rest_2_ = f32[1440,128]{1,0:T(8,128)S(1)} collective-permute-done((f32[1440,128]{1,0:T(8,128)S(1)}, f32[1440,128]{1,0:T(8,128)S(1)}, u32[]{:S(2)}, u32[]{:S(2)}) %collective-permute-start.8) | collective-permute-done | bytes 737312 | tf_op jit(solution)/shard_map/ppermute | solution.py:129
  85.6 2.7 %collective-permute-done.9.rest_4_ = f32[1440,128]{1,0:T(8,128)S(1)} collective-permute-done((f32[1440,128]{1,0:T(8,128)S(1)}, f32[1440,128]{1,0:T(8,128)S(1)}, u32[]{:S(2)}, u32[]{:S(2)}) %collective-permute-start.9) | collective-permute-done | bytes 737312 | tf_op jit(solution)/shard_map/ppermute | solution.py:129
  88.4 0.1 pad_maximum_fusion.2
  88.4 0.1 collective-permute-start.14
  88.5 0.1 pad_maximum_fusion.3
  88.6 5.1 %collective-permute-start.15 = (f32[1440,128]{1,0:T(8,128)S(1)}, f32[1440,128]{1,0:T(8,128)S(1)}, u32[]{:S(2)}, u32[]{:S(2)}) collective-permute-start(f32[1440,128]{1,0:T(8,128)S(1)} %pad_maximum_fusion.3), channel_id=1, source_target_pairs={{0,15},{1,0},{2,1},{3,2},{4,3},{5,4},{6,5},{7,6},{8,7},{9,8},{10,9... | collective-permute-start | bytes 2211848 | tf_op jit(solution)/shard_map/ppermute | solution.py:129
  93.7 0.0 copy-start.8
  93.7 0.0 copy-start.9
  93.8 4.8 %collective-permute-start.12 = (f32[1152,128]{1,0:T(8,128)S(1)}, f32[1152,128]{1,0:T(8,128)S(1)}, u32[]{:S(2)}, u32[]{:S(2)}) collective-permute-start(f32[1152,128]{1,0:T(8,128)S(1)} %pad_maximum_fusion.4), channel_id=1, source_target_pairs={{0,16},{16,32},{32,48},{48,64},{64,80},{80,96},{96,112},{112,0},{1... | collective-permute-start | bytes 1769480 | tf_op jit(solution)/shard_map/ppermute | solution.py:129
  98.6 0.0 copy-start.6
  98.7 0.0 copy-start.7
  98.7 0.0 collective-permute-start.13
  98.7 6.7 %collective-permute-done.12.rest_0_ = f32[1152,128]{1,0:T(8,128)S(1)} collective-permute-done((f32[1152,128]{1,0:T(8,128)S(1)}, f32[1152,128]{1,0:T(8,128)S(1)}, u32[]{:S(2)}, u32[]{:S(2)}) %collective-permute-start.12) | collective-permute-done | bytes 589856 | tf_op jit(solution)/shard_map/ppermute | solution.py:129
  105.4 2.9 %collective-permute-done.13.rest_1_ = f32[1152,128]{1,0:T(8,128)S(1)} collective-permute-done((f32[1152,128]{1,0:T(8,128)S(1)}, f32[1152,128]{1,0:T(8,128)S(1)}, u32[]{:S(2)}, u32[]{:S(2)}) %collective-permute-start.13) | collective-permute-done | bytes 589856 | tf_op jit(solution)/shard_map/ppermute | solution.py:129
  108.3 1.8 %add_middle.1 = (f32[1024,128]{1,0:T(8,128)S(1)}, f32[1024,128]{1,0:T(8,128)S(1)}) custom-call(s32[9,1,24]{2,1,0:T(1,128)S(1)} %bitcast.19, s32[9,1,24]{2,1,0:T(1,128)S(1)} %bitcast.22, f32[1152,128]{1,0:T(8,128)S(1)} %collective-permute-done.12.rest_0_, f32[1152,128]{1,0:T(8,128)S(1)} %collective-permute-done.13.rest_1_, ...), custom_call_target="tpu_custom_call" | custom-call | bytes 6600000 | tf_op jit(solution)/shard_map/add_middle/pallas_call | solution.py:413
  110.1 0.3 collective-permute-done.14.rest_0_
  110.4 0.0 collective-permute-done.15.rest_1_
  110.4 3.7 %unpack.1 = (f32[18,16384]{1,0:T(8,128)}, f32[18,16384]{1,0:T(8,128)}) custom-call(s32[9,1,24]{2,1,0:T(1,128)S(1)} %bitcast.20, s32[9,1,24]{2,1,0:T(1,128)S(1)} %bitcast.23, f32[128,128]{1,0:T(8,128)S(1)} %bitcast.16, f32[128,128]{1,0:T(8,128)S(1)} %bitcast.17, f32[1024,128]{1,0:T(8,128)S(1)} %get-tuple-element.44.middle_a, ...), custom_call_target="tpu_custom_call" | custom-call | bytes 13200000 | tf_op jit(solution)/shard_map/unpack/pallas_call | solution.py:472
  (29 shorter events, 0.5 us)
Async XLA Ops:
  4.7 15.5 %collective-permute-start = (f32[2016,128]{1,0:T(8,128)}, f32[2016,128]{1,0:T(8,128)S(1)}, u32[]{:S(2)}, u32[]{:S(2)}) collective-permute-start(f32[2016,128]{1,0:T(8,128)} %get-tuple-element.26), channel_id=1, source_target_pairs={{0,112},{16,0},{32,16},{48,32},{64,48},{80,64},{96,80},{112,96},{1... | collective-permute-start | bytes 3096584 | tf_op jit(solution)/shard_map/ppermute | solution.py:129
  6.1 14.1 %collective-permute-start.1 = (f32[2016,128]{1,0:T(8,128)}, f32[2016,128]{1,0:T(8,128)S(1)}, u32[]{:S(2)}, u32[]{:S(2)}) collective-permute-start(f32[2016,128]{1,0:T(8,128)} %get-tuple-element.28), channel_id=1, source_target_pairs={{0,16},{16,32},{32,48},{48,64},{64,80},{80,96},{96,112},{112,0},{1... | collective-permute-start | bytes 3096584 | tf_op jit(solution)/shard_map/ppermute | solution.py:129
  7.4 19.4 %collective-permute-start.2 = (f32[864,128]{1,0:T(8,128)}, f32[864,128]{1,0:T(8,128)S(1)}, u32[]{:S(2)}, u32[]{:S(2)}) collective-permute-start(f32[864,128]{1,0:T(8,128)} %get-tuple-element.29), channel_id=1, source_target_pairs={{0,15},{1,0},{2,1},{3,2},{4,3},{5,4},{6,5},{7,6},{8,7},{9,8},{10,9... | collective-permute-start | bytes 1327112 | tf_op jit(solution)/shard_map/ppermute | solution.py:129
  13.4 13.7 %collective-permute-start.3 = (f32[864,128]{1,0:T(8,128)}, f32[864,128]{1,0:T(8,128)S(1)}, u32[]{:S(2)}, u32[]{:S(2)}) collective-permute-start(f32[864,128]{1,0:T(8,128)} %get-tuple-element.30), channel_id=1, source_target_pairs={{0,1},{1,2},{2,3},{3,4},{4,5},{5,6},{6,7},{7,8},{8,9},{9,10},{10,1... | collective-permute-start | bytes 1327112 | tf_op jit(solution)/shard_map/ppermute | solution.py:129
  20.3 6.4 %copy-start.3 = (f32[864,128]{1,0:T(8,128)S(1)}, f32[864,128]{1,0:T(8,128)}, u32[]{:S(2)}) copy-start(f32[864,128]{1,0:T(8,128)} %get-tuple-element.32.rest_3_) | copy-start | bytes 1327108
  20.4 31.6 %collective-permute-start.6 = (f32[2016,128]{1,0:T(8,128)S(1)}, f32[2016,128]{1,0:T(8,128)S(1)}, u32[]{:S(2)}, u32[]{:S(2)}) collective-permute-start(f32[2016,128]{1,0:T(8,128)S(1)} %pad_maximum_fusion), channel_id=1, source_target_pairs={{0,15},{1,0},{2,1},{3,2},{4,3},{5,4},{6,5},{7,6},{8,7},{9,8},{10,9... | collective-permute-start | bytes 3096584 | tf_op jit(solution)/shard_map/ppermute | solution.py:129
  26.5 25.6 %collective-permute-start.7 = (f32[2016,128]{1,0:T(8,128)S(1)}, f32[2016,128]{1,0:T(8,128)S(1)}, u32[]{:S(2)}, u32[]{:S(2)}) collective-permute-start(f32[2016,128]{1,0:T(8,128)S(1)} %pad_maximum_fusion.1), channel_id=1, source_target_pairs={{0,1},{1,2},{2,3},{3,4},{4,5},{5,6},{6,7},{7,8},{8,9},{9,10},{10,1... | collective-permute-start | bytes 3096584 | tf_op jit(solution)/shard_map/ppermute | solution.py:129
  26.8 5.0 %copy-start.1 = (s32[65536]{0:T(1024)S(1)}, s32[65536]{0:T(1024)}, u32[]{:S(2)}) copy-start(s32[65536]{0:T(1024)} %param.17) | copy-start | bytes 786436
  26.8 5.0 %copy-start.2 = (s32[65536]{0:T(1024)S(1)}, s32[65536]{0:T(1024)}, u32[]{:S(2)}) copy-start(s32[65536]{0:T(1024)} %param.18) | copy-start | bytes 786436
  26.8 10.2 %copy-start.4 = (f32[65536]{0:T(1024)S(1)}, f32[65536]{0:T(1024)}, u32[]{:S(2)}) copy-start(f32[65536]{0:T(1024)} %param.19) | copy-start | bytes 786436
  26.8 10.2 %copy-start.5 = (s32[65536]{0:T(1024)S(1)}, s32[65536]{0:T(1024)}, u32[]{:S(2)}) copy-start(s32[65536]{0:T(1024)} %param.20) | copy-start | bytes 786436
  27.1 9.9 %collective-permute-start.4 = (f32[864,128]{1,0:T(8,128)S(1)}, f32[864,128]{1,0:T(8,128)S(1)}, u32[]{:S(2)}, u32[]{:S(2)}) collective-permute-start(f32[864,128]{1,0:T(8,128)S(1)} %pad_maximum_fusion.6), channel_id=1, source_target_pairs={{0,112},{16,0},{32,16},{48,32},{64,48},{80,64},{96,80},{112,96},{1... | collective-permute-start | bytes 1327112 | tf_op jit(solution)/shard_map/ppermute | solution.py:129
  31.1 5.9 %collective-permute-start.5 = (f32[864,128]{1,0:T(8,128)S(1)}, f32[864,128]{1,0:T(8,128)S(1)}, u32[]{:S(2)}, u32[]{:S(2)}) collective-permute-start(f32[864,128]{1,0:T(8,128)S(1)} %pad_maximum_fusion.7), channel_id=1, source_target_pairs={{0,16},{16,32},{32,48},{48,64},{64,80},{80,96},{96,112},{112,0},{1... | collective-permute-start | bytes 1327112 | tf_op jit(solution)/shard_map/ppermute | solution.py:129
  37.0 15.0 %copy-start = (f32[2016,128]{1,0:T(8,128)S(1)}, f32[2016,128]{1,0:T(8,128)}, u32[]{:S(2)}) copy-start(f32[2016,128]{1,0:T(8,128)} %get-tuple-element.27.rest_3_) | copy-start | bytes 3096580
  72.8 12.8 %collective-permute-start.8 = (f32[1440,128]{1,0:T(8,128)S(1)}, f32[1440,128]{1,0:T(8,128)S(1)}, u32[]{:S(2)}, u32[]{:S(2)}) collective-permute-start(f32[1440,128]{1,0:T(8,128)S(1)} %get-tuple-element.36), channel_id=1, source_target_pairs={{0,16},{16,32},{32,48},{48,64},{64,80},{80,96},{96,112},{112,0},{1... | collective-permute-start | bytes 2211848 | tf_op jit(solution)/shard_map/ppermute | solution.py:129
  77.2 11.2 %collective-permute-start.9 = (f32[1440,128]{1,0:T(8,128)S(1)}, f32[1440,128]{1,0:T(8,128)S(1)}, u32[]{:S(2)}, u32[]{:S(2)}) collective-permute-start(f32[1440,128]{1,0:T(8,128)S(1)} %get-tuple-element.38), channel_id=1, source_target_pairs={{0,112},{16,0},{32,16},{48,32},{64,48},{80,64},{96,80},{112,96},{1... | collective-permute-start | bytes 2211848 | tf_op jit(solution)/shard_map/ppermute | solution.py:129
  77.2 16.5 %collective-permute-start.10 = (f32[1152,128]{1,0:T(8,128)S(1)}, f32[1152,128]{1,0:T(8,128)S(1)}, u32[]{:S(2)}, u32[]{:S(2)}) collective-permute-start(f32[1152,128]{1,0:T(8,128)S(1)} %get-tuple-element.39), channel_id=1, source_target_pairs={{0,1},{1,2},{2,3},{3,4},{4,5},{5,6},{6,7},{7,8},{8,9},{9,10},{10,1... | collective-permute-start | bytes 1769480 | tf_op jit(solution)/shard_map/ppermute | solution.py:129
  77.2 16.5 %collective-permute-start.11 = (f32[1152,128]{1,0:T(8,128)S(1)}, f32[1152,128]{1,0:T(8,128)S(1)}, u32[]{:S(2)}, u32[]{:S(2)}) collective-permute-start(f32[1152,128]{1,0:T(8,128)S(1)} %get-tuple-element.40), channel_id=1, source_target_pairs={{0,15},{1,0},{2,1},{3,2},{4,3},{5,4},{6,5},{7,6},{8,7},{9,8},{10,9... | collective-permute-start | bytes 1769480 | tf_op jit(solution)/shard_map/ppermute | solution.py:129
  88.4 22.0 %collective-permute-start.14 = (f32[1440,128]{1,0:T(8,128)S(1)}, f32[1440,128]{1,0:T(8,128)S(1)}, u32[]{:S(2)}, u32[]{:S(2)}) collective-permute-start(f32[1440,128]{1,0:T(8,128)S(1)} %pad_maximum_fusion.2), channel_id=1, source_target_pairs={{0,1},{1,2},{2,3},{3,4},{4,5},{5,6},{6,7},{7,8},{8,9},{9,10},{10,1... | collective-permute-start | bytes 2211848 | tf_op jit(solution)/shard_map/ppermute | solution.py:129
  88.6 21.8 %collective-permute-start.15 = (f32[1440,128]{1,0:T(8,128)S(1)}, f32[1440,128]{1,0:T(8,128)S(1)}, u32[]{:S(2)}, u32[]{:S(2)}) collective-permute-start(f32[1440,128]{1,0:T(8,128)S(1)} %pad_maximum_fusion.3), channel_id=1, source_target_pairs={{0,15},{1,0},{2,1},{3,2},{4,3},{5,4},{6,5},{7,6},{8,7},{9,8},{10,9... | collective-permute-start | bytes 2211848 | tf_op jit(solution)/shard_map/ppermute | solution.py:129
  93.7 14.6 %copy-start.8 = (s32[1,9,24]{2,0,1:T(1,128)S(1)}, s32[1,9,24]{2,0,1:T(1,128)}, u32[]{:S(2)}) copy-start(s32[1,9,24]{2,0,1:T(1,128)} %param.15) | copy-start | bytes 2596
  93.7 14.6 %copy-start.9 = (s32[1,9,24]{2,0,1:T(1,128)S(1)}, s32[1,9,24]{2,0,1:T(1,128)}, u32[]{:S(2)}) copy-start(s32[1,9,24]{2,0,1:T(1,128)} %param.16) | copy-start | bytes 2596
  93.8 11.6 %collective-permute-start.12 = (f32[1152,128]{1,0:T(8,128)S(1)}, f32[1152,128]{1,0:T(8,128)S(1)}, u32[]{:S(2)}, u32[]{:S(2)}) collective-permute-start(f32[1152,128]{1,0:T(8,128)S(1)} %pad_maximum_fusion.4), channel_id=1, source_target_pairs={{0,16},{16,32},{32,48},{48,64},{64,80},{80,96},{96,112},{112,0},{1... | collective-permute-start | bytes 1769480 | tf_op jit(solution)/shard_map/ppermute | solution.py:129
  98.6 11.8 %copy-start.6 = (f32[16384]{0:T(1024)S(1)}, f32[16384]{0:T(1024)}, u32[]{:S(2)}) copy-start(f32[16384]{0:T(1024)} %param.13) | copy-start | bytes 196612
  98.7 11.8 %copy-start.7 = (f32[16384]{0:T(1024)S(1)}, f32[16384]{0:T(1024)}, u32[]{:S(2)}) copy-start(f32[16384]{0:T(1024)} %param.14) | copy-start | bytes 196612
  98.7 9.6 %collective-permute-start.13 = (f32[1152,128]{1,0:T(8,128)S(1)}, f32[1152,128]{1,0:T(8,128)S(1)}, u32[]{:S(2)}, u32[]{:S(2)}) collective-permute-start(f32[1152,128]{1,0:T(8,128)S(1)} %pad_maximum_fusion.5), channel_id=1, source_target_pairs={{0,112},{16,0},{32,16},{48,32},{64,48},{80,64},{96,80},{112,96},{1... | collective-permute-start | bytes 1769480 | tf_op jit(solution)/shard_map/ppermute | solution.py:129

commit v5 on v4

--- a/solution.py
+++ b/solution.py
@@ -359,7 +359,7 @@
         add_groups(scatter_row(values, lanes_a, lanes_o, column, quarter), slots_a, slots_o, r, *accs)
         return 0
 
-    lax.fori_loop(0, nrows, step, 0, unroll=128)
+    lax.fori_loop(0, nrows, step, 0, unroll=256)
     for n in range(9):
         p, q = n // 3, n % 3
 
@@ -373,7 +373,7 @@
                 outer[p][pl.ds(to + 4, 6), :] = accs[comp][pl.ds(at + 16, 8), :][:6]
             return 0
 
-        lax.fori_loop(0, CAP, split, 0, unroll=8)
+        lax.fori_loop(0, CAP, split, 0, unroll=CAP)
 
 
 def scatter(slots, refs, weight, lead, pieces):

time: 116 us -> 115 us (level)
  no operation moved by 1% of the time
where the time goes in v5:
time: 115 us; the launch traced here: 114 us
  Pallas kernels  45.1 us (39%)
  starting transfers between devices  37.6 us (33%)
  waiting for transfers between devices  27.4 us (24%)
  between operations  1.79 us (2%)
  local copies, waits for them, and re-layouts  1.52 us (1%)
    ppermute x16, starting transfers between devices, hop(): lax.ppermute(value, axis, [(s, (s + steps) % count) for s in range(count)])  37.6 us
    ppermute x16, waiting for transfers between devices, hop(): lax.ppermute(value, axis, [(s, (s + steps) % count) for s in range(count)])  27.4 us
    pallas_call x1, Pallas kernels, scatter(): call(functools.partial(scatter_body, nrows), 'scatter', (shape(3 * 2 * CA...  20.3 us
    pallas_call x1, Pallas kernels, first(): call(functools.partial(first_body, nrows), 'bulk', (shape(nrows, LANES),...  15 us
    pallas_call x1, Pallas kernels, pack(): call(pack_body, 'pack', outs, [HBM] * 4, [pltpu.SMEM(send_a.shape, jnp.in...  4.04 us
    pallas_call x1, Pallas kernels, unpack(): call(functools.partial(unpack_body, nblocks), 'unpack', (shape(FLUXES, co...  3.74 us
  transfers between devices with their start and end apart: 16, of which 8 were waited for; matrix products, arithmetic and copies ran while one was open for 2% of the time, Pallas kernels for 15%

profile of v5, /device:TPU:1, one launch (start us, length us, event | category | flops | bytes accessed | tf_op | source)
XLA Modules:
  0.0 113.8 jit_solution(13388025164034628603)
XLA Ops:
  0.6 4.0 %pack.1 = (f32[864,128]{1,0:T(8,128)}, f32[864,128]{1,0:T(8,128)}, f32[864,128]{1,0:T(8,128)}, f32[2016,128]{1,0:T(8,128)}, f32[2016,128]{1,0:T(8,128)}, /*index=5*/f32[2016,128]{1,0:T(8,128)}) custom-call(s32[9,1,24]{2,1,0:T(1,128)} %bitcast.18, s32[9,1,24]{2,1,0:T(1,128)} %bitcast.21, f32[20,16384]{1,0:T(8,128)} %fields_a.1, f32[20,16384]{1,0:T(8,128)} %fields_o.1), custom_call_target="tpu_custom_call" | custom-call | bytes 13200000 | tf_op jit(solution)/shard_map/pack/pallas_call | solution.py:110
  4.7 1.4 %collective-permute-start = (f32[2016,128]{1,0:T(8,128)}, f32[2016,128]{1,0:T(8,128)S(1)}, u32[]{:S(2)}, u32[]{:S(2)}) collective-permute-start(f32[2016,128]{1,0:T(8,128)} %get-tuple-element.26), channel_id=1, source_target_pairs={{0,112},{16,0},{32,16},{48,32},{64,48},{80,64},{96,80},{112,96},{1... | collective-permute-start | bytes 3096584 | tf_op jit(solution)/shard_map/ppermute | solution.py:129
  6.1 1.3 %collective-permute-start.1 = (f32[2016,128]{1,0:T(8,128)}, f32[2016,128]{1,0:T(8,128)S(1)}, u32[]{:S(2)}, u32[]{:S(2)}) collective-permute-start(f32[2016,128]{1,0:T(8,128)} %get-tuple-element.28), channel_id=1, source_target_pairs={{0,16},{16,32},{32,48},{48,64},{64,80},{80,96},{96,112},{112,0},{1... | collective-permute-start | bytes 3096584 | tf_op jit(solution)/shard_map/ppermute | solution.py:129
  7.4 6.0 %collective-permute-start.2 = (f32[864,128]{1,0:T(8,128)}, f32[864,128]{1,0:T(8,128)S(1)}, u32[]{:S(2)}, u32[]{:S(2)}) collective-permute-start(f32[864,128]{1,0:T(8,128)} %get-tuple-element.29), channel_id=1, source_target_pairs={{0,15},{1,0},{2,1},{3,2},{4,3},{5,4},{6,5},{7,6},{8,7},{9,8},{10,9... | collective-permute-start | bytes 1327112 | tf_op jit(solution)/shard_map/ppermute | solution.py:129
  13.4 0.0 collective-permute-start.3
  13.4 1.1 fusion.1
  14.5 5.7 %collective-permute-done.rest_2_ = f32[2016,128]{1,0:T(8,128)S(1)} collective-permute-done((f32[2016,128]{1,0:T(8,128)}, f32[2016,128]{1,0:T(8,128)S(1)}, u32[]{:S(2)}, u32[]{:S(2)}) %collective-permute-start) | collective-permute-done | bytes 1032224 | tf_op jit(solution)/shard_map/ppermute | solution.py:129
  20.3 0.1 pad_maximum_fusion
  20.4 6.0 %collective-permute-start.6 = (f32[2016,128]{1,0:T(8,128)S(1)}, f32[2016,128]{1,0:T(8,128)S(1)}, u32[]{:S(2)}, u32[]{:S(2)}) collective-permute-start(f32[2016,128]{1,0:T(8,128)S(1)} %pad_maximum_fusion), channel_id=1, source_target_pairs={{0,15},{1,0},{2,1},{3,2},{4,3},{5,4},{6,5},{7,6},{8,7},{9,8},{10,9... | collective-permute-start | bytes 3096584 | tf_op jit(solution)/shard_map/ppermute | solution.py:129
  26.4 0.1 pad_maximum_fusion.1
  26.5 0.1 collective-permute-start.7
  26.6 0.0 copy-start.1
  26.6 0.0 copy-start.2
  26.6 0.0 copy-start.4
  26.6 0.0 copy-start.5
  26.7 0.0 collective-permute-done.2.rest_2_
  26.7 0.4 collective-permute-done.3.rest_4_
  27.1 3.8 %collective-permute-start.4 = (f32[864,128]{1,0:T(8,128)S(1)}, f32[864,128]{1,0:T(8,128)S(1)}, u32[]{:S(2)}, u32[]{:S(2)}) collective-permute-start(f32[864,128]{1,0:T(8,128)S(1)} %pad_maximum_fusion.6), channel_id=1, source_target_pairs={{0,112},{16,0},{32,16},{48,32},{64,48},{80,64},{96,80},{112,96},{1... | collective-permute-start | bytes 1327112 | tf_op jit(solution)/shard_map/ppermute | solution.py:129
  31.0 0.0 collective-permute-start.5
  31.6 0.2 slots.1
  31.8 5.2 %collective-permute-done.4.rest_0_ = f32[864,128]{1,0:T(8,128)S(1)} collective-permute-done((f32[864,128]{1,0:T(8,128)S(1)}, f32[864,128]{1,0:T(8,128)S(1)}, u32[]{:S(2)}, u32[]{:S(2)}) %collective-permute-start.4) | collective-permute-done | bytes 442400 | tf_op jit(solution)/shard_map/ppermute | solution.py:129
  37.0 0.0 collective-permute-done.5.rest_1_
  37.0 0.0 copy-start
  37.1 15.0 %bulk.1 = (f32[512,128]{1,0:T(8,128)S(1)}, f32[2056,128]{1,0:T(8,128)S(1)}) custom-call(s32[1]{0:T(128)S(6)} %copy.13.count, s32[8,512]{1,0:T(8,128)S(1)} %get-tuple-element.24.slots_a, s32[8,512]{1,0:T(8,128)S(1)} %get-tuple-element.25.slots_o, s32[512,128]{1,0:T(8,128)S(1)} %bitcast.9, s32[512,128]{1,0:T(8,128)S(1)} %bitcast.12, f32[512,128]{1,0:T(8,128)S(1)} %bitcast.14, ...), custom_call_target="tpu_custom_call" | custom-call | bytes 66000000 | tf_op jit(solution)/shard_map/bulk/pallas_call | solution.py:334
  52.0 0.0 collective-permute-done.6.rest_0_
  52.0 0.0 collective-permute-done.7.rest_1_
  52.1 20.3 %scatter.1 = (f32[1152,128]{1,0:T(8,128)S(1)}, f32[1152,128]{1,0:T(8,128)S(1)}, f32[1152,128]{1,0:T(8,128)S(1)}, f32[1440,128]{1,0:T(8,128)S(1)}, f32[1440,128]{1,0:T(8,128)S(1)}, /*index=5*/f32[1440,128]{1,0:T(8,128)S(1)}) custom-call(s32[8,512]{1,0:T(8,128)S(1)} %get-tuple-element.24.slots_a, s32[8,512]{1,0:T(8,128)S(1)} %get-tuple-element.25.slots_o, ...), custom_call_target="tpu_custom_call" | custom-call | bytes 72600000 | tf_op jit(solution)/shard_map/scatter/pallas_call | solution.py:381
  72.4 4.2 %collective-permute-start.8 = (f32[1440,128]{1,0:T(8,128)S(1)}, f32[1440,128]{1,0:T(8,128)S(1)}, u32[]{:S(2)}, u32[]{:S(2)}) collective-permute-start(f32[1440,128]{1,0:T(8,128)S(1)} %get-tuple-element.36), channel_id=1, source_target_pairs={{0,16},{16,32},{32,48},{48,64},{64,80},{80,96},{96,112},{112,0},{1... | collective-permute-start | bytes 2211848 | tf_op jit(solution)/shard_map/ppermute | solution.py:129
  76.6 0.0 collective-permute-start.9
  76.6 0.0 collective-permute-start.10
  76.6 4.8 %collective-permute-start.11 = (f32[1152,128]{1,0:T(8,128)S(1)}, f32[1152,128]{1,0:T(8,128)S(1)}, u32[]{:S(2)}, u32[]{:S(2)}) collective-permute-start(f32[1152,128]{1,0:T(8,128)S(1)} %get-tuple-element.40), channel_id=1, source_target_pairs={{0,15},{1,0},{2,1},{3,2},{4,3},{5,4},{6,5},{7,6},{8,7},{9,8},{10,9... | collective-permute-start | bytes 1769480 | tf_op jit(solution)/shard_map/ppermute | solution.py:129
  81.5 3.5 %collective-permute-done.8.rest_2_ = f32[1440,128]{1,0:T(8,128)S(1)} collective-permute-done((f32[1440,128]{1,0:T(8,128)S(1)}, f32[1440,128]{1,0:T(8,128)S(1)}, u32[]{:S(2)}, u32[]{:S(2)}) %collective-permute-start.8) | collective-permute-done | bytes 737312 | tf_op jit(solution)/shard_map/ppermute | solution.py:129
  85.1 2.7 %collective-permute-done.9.rest_4_ = f32[1440,128]{1,0:T(8,128)S(1)} collective-permute-done((f32[1440,128]{1,0:T(8,128)S(1)}, f32[1440,128]{1,0:T(8,128)S(1)}, u32[]{:S(2)}, u32[]{:S(2)}) %collective-permute-start.9) | collective-permute-done | bytes 737312 | tf_op jit(solution)/shard_map/ppermute | solution.py:129
  87.8 0.1 pad_maximum_fusion.2
  87.9 0.1 collective-permute-start.14
  88.0 0.1 pad_maximum_fusion.3
  88.0 5.1 %collective-permute-start.15 = (f32[1440,128]{1,0:T(8,128)S(1)}, f32[1440,128]{1,0:T(8,128)S(1)}, u32[]{:S(2)}, u32[]{:S(2)}) collective-permute-start(f32[1440,128]{1,0:T(8,128)S(1)} %pad_maximum_fusion.3), channel_id=1, source_target_pairs={{0,15},{1,0},{2,1},{3,2},{4,3},{5,4},{6,5},{7,6},{8,7},{9,8},{10,9... | collective-permute-start | bytes 2211848 | tf_op jit(solution)/shard_map/ppermute | solution.py:129
  93.1 0.0 copy-start.8
  93.1 0.0 copy-start.9
  93.2 4.8 %collective-permute-start.12 = (f32[1152,128]{1,0:T(8,128)S(1)}, f32[1152,128]{1,0:T(8,128)S(1)}, u32[]{:S(2)}, u32[]{:S(2)}) collective-permute-start(f32[1152,128]{1,0:T(8,128)S(1)} %pad_maximum_fusion.4), channel_id=1, source_target_pairs={{0,16},{16,32},{32,48},{48,64},{64,80},{80,96},{96,112},{112,0},{1... | collective-permute-start | bytes 1769480 | tf_op jit(solution)/shard_map/ppermute | solution.py:129
  98.1 0.0 copy-start.6
  98.1 0.0 copy-start.7
  98.1 0.0 collective-permute-start.13
  98.1 6.7 %collective-permute-done.12.rest_0_ = f32[1152,128]{1,0:T(8,128)S(1)} collective-permute-done((f32[1152,128]{1,0:T(8,128)S(1)}, f32[1152,128]{1,0:T(8,128)S(1)}, u32[]{:S(2)}, u32[]{:S(2)}) %collective-permute-start.12) | collective-permute-done | bytes 589856 | tf_op jit(solution)/shard_map/ppermute | solution.py:129
  104.9 2.9 %collective-permute-done.13.rest_1_ = f32[1152,128]{1,0:T(8,128)S(1)} collective-permute-done((f32[1152,128]{1,0:T(8,128)S(1)}, f32[1152,128]{1,0:T(8,128)S(1)}, u32[]{:S(2)}, u32[]{:S(2)}) %collective-permute-start.13) | collective-permute-done | bytes 589856 | tf_op jit(solution)/shard_map/ppermute | solution.py:129
  107.7 1.8 %add_middle.1 = (f32[1024,128]{1,0:T(8,128)S(1)}, f32[1024,128]{1,0:T(8,128)S(1)}) custom-call(s32[9,1,24]{2,1,0:T(1,128)S(1)} %bitcast.19, s32[9,1,24]{2,1,0:T(1,128)S(1)} %bitcast.22, f32[1152,128]{1,0:T(8,128)S(1)} %collective-permute-done.12.rest_0_, f32[1152,128]{1,0:T(8,128)S(1)} %collective-permute-done.13.rest_1_, ...), custom_call_target="tpu_custom_call" | custom-call | bytes 6600000 | tf_op jit(solution)/shard_map/add_middle/pallas_call | solution.py:413
  109.6 0.3 collective-permute-done.14.rest_0_
  109.9 3.7 %unpack.1 = (f32[18,16384]{1,0:T(8,128)}, f32[18,16384]{1,0:T(8,128)}) custom-call(s32[9,1,24]{2,1,0:T(1,128)S(1)} %bitcast.20, s32[9,1,24]{2,1,0:T(1,128)S(1)} %bitcast.23, f32[128,128]{1,0:T(8,128)S(1)} %bitcast.16, f32[128,128]{1,0:T(8,128)S(1)} %bitcast.17, f32[1024,128]{1,0:T(8,128)S(1)} %get-tuple-element.44.middle_a, ...), custom_call_target="tpu_custom_call" | custom-call | bytes 13200000 | tf_op jit(solution)/shard_map/unpack/pallas_call | solution.py:472
  (29 shorter events, 0.5 us)
Async XLA Ops:
  4.7 15.5 %collective-permute-start = (f32[2016,128]{1,0:T(8,128)}, f32[2016,128]{1,0:T(8,128)S(1)}, u32[]{:S(2)}, u32[]{:S(2)}) collective-permute-start(f32[2016,128]{1,0:T(8,128)} %get-tuple-element.26), channel_id=1, source_target_pairs={{0,112},{16,0},{32,16},{48,32},{64,48},{80,64},{96,80},{112,96},{1... | collective-permute-start | bytes 3096584 | tf_op jit(solution)/shard_map/ppermute | solution.py:129
  6.1 14.1 %collective-permute-start.1 = (f32[2016,128]{1,0:T(8,128)}, f32[2016,128]{1,0:T(8,128)S(1)}, u32[]{:S(2)}, u32[]{:S(2)}) collective-permute-start(f32[2016,128]{1,0:T(8,128)} %get-tuple-element.28), channel_id=1, source_target_pairs={{0,16},{16,32},{32,48},{48,64},{64,80},{80,96},{96,112},{112,0},{1... | collective-permute-start | bytes 3096584 | tf_op jit(solution)/shard_map/ppermute | solution.py:129
  7.4 19.3 %collective-permute-start.2 = (f32[864,128]{1,0:T(8,128)}, f32[864,128]{1,0:T(8,128)S(1)}, u32[]{:S(2)}, u32[]{:S(2)}) collective-permute-start(f32[864,128]{1,0:T(8,128)} %get-tuple-element.29), channel_id=1, source_target_pairs={{0,15},{1,0},{2,1},{3,2},{4,3},{5,4},{6,5},{7,6},{8,7},{9,8},{10,9... | collective-permute-start | bytes 1327112 | tf_op jit(solution)/shard_map/ppermute | solution.py:129
  13.4 13.7 %collective-permute-start.3 = (f32[864,128]{1,0:T(8,128)}, f32[864,128]{1,0:T(8,128)S(1)}, u32[]{:S(2)}, u32[]{:S(2)}) collective-permute-start(f32[864,128]{1,0:T(8,128)} %get-tuple-element.30), channel_id=1, source_target_pairs={{0,1},{1,2},{2,3},{3,4},{4,5},{5,6},{6,7},{7,8},{8,9},{9,10},{10,1... | collective-permute-start | bytes 1327112 | tf_op jit(solution)/shard_map/ppermute | solution.py:129
  20.3 6.3 %copy-start.3 = (f32[864,128]{1,0:T(8,128)S(1)}, f32[864,128]{1,0:T(8,128)}, u32[]{:S(2)}) copy-start(f32[864,128]{1,0:T(8,128)} %get-tuple-element.32.rest_3_) | copy-start | bytes 1327108
  20.4 31.6 %collective-permute-start.6 = (f32[2016,128]{1,0:T(8,128)S(1)}, f32[2016,128]{1,0:T(8,128)S(1)}, u32[]{:S(2)}, u32[]{:S(2)}) collective-permute-start(f32[2016,128]{1,0:T(8,128)S(1)} %pad_maximum_fusion), channel_id=1, source_target_pairs={{0,15},{1,0},{2,1},{3,2},{4,3},{5,4},{6,5},{7,6},{8,7},{9,8},{10,9... | collective-permute-start | bytes 3096584 | tf_op jit(solution)/shard_map/ppermute | solution.py:129
  26.5 25.6 %collective-permute-start.7 = (f32[2016,128]{1,0:T(8,128)S(1)}, f32[2016,128]{1,0:T(8,128)S(1)}, u32[]{:S(2)}, u32[]{:S(2)}) collective-permute-start(f32[2016,128]{1,0:T(8,128)S(1)} %pad_maximum_fusion.1), channel_id=1, source_target_pairs={{0,1},{1,2},{2,3},{3,4},{4,5},{5,6},{6,7},{7,8},{8,9},{9,10},{10,1... | collective-permute-start | bytes 3096584 | tf_op jit(solution)/shard_map/ppermute | solution.py:129
  26.6 5.0 %copy-start.1 = (s32[65536]{0:T(1024)S(1)}, s32[65536]{0:T(1024)}, u32[]{:S(2)}) copy-start(s32[65536]{0:T(1024)} %param.17) | copy-start | bytes 786436
  26.6 5.0 %copy-start.2 = (s32[65536]{0:T(1024)S(1)}, s32[65536]{0:T(1024)}, u32[]{:S(2)}) copy-start(s32[65536]{0:T(1024)} %param.18) | copy-start | bytes 786436
  26.6 10.4 %copy-start.4 = (f32[65536]{0:T(1024)S(1)}, f32[65536]{0:T(1024)}, u32[]{:S(2)}) copy-start(f32[65536]{0:T(1024)} %param.19) | copy-start | bytes 786436
  26.6 10.4 %copy-start.5 = (s32[65536]{0:T(1024)S(1)}, s32[65536]{0:T(1024)}, u32[]{:S(2)}) copy-start(s32[65536]{0:T(1024)} %param.20) | copy-start | bytes 786436
  27.1 9.9 %collective-permute-start.4 = (f32[864,128]{1,0:T(8,128)S(1)}, f32[864,128]{1,0:T(8,128)S(1)}, u32[]{:S(2)}, u32[]{:S(2)}) collective-permute-start(f32[864,128]{1,0:T(8,128)S(1)} %pad_maximum_fusion.6), channel_id=1, source_target_pairs={{0,112},{16,0},{32,16},{48,32},{64,48},{80,64},{96,80},{112,96},{1... | collective-permute-start | bytes 1327112 | tf_op jit(solution)/shard_map/ppermute | solution.py:129
  31.0 6.1 %collective-permute-start.5 = (f32[864,128]{1,0:T(8,128)S(1)}, f32[864,128]{1,0:T(8,128)S(1)}, u32[]{:S(2)}, u32[]{:S(2)}) collective-permute-start(f32[864,128]{1,0:T(8,128)S(1)} %pad_maximum_fusion.7), channel_id=1, source_target_pairs={{0,16},{16,32},{32,48},{48,64},{64,80},{80,96},{96,112},{112,0},{1... | collective-permute-start | bytes 1327112 | tf_op jit(solution)/shard_map/ppermute | solution.py:129
  37.0 15.0 %copy-start = (f32[2016,128]{1,0:T(8,128)S(1)}, f32[2016,128]{1,0:T(8,128)}, u32[]{:S(2)}) copy-start(f32[2016,128]{1,0:T(8,128)} %get-tuple-element.27.rest_3_) | copy-start | bytes 3096580
  72.4 12.6 %collective-permute-start.8 = (f32[1440,128]{1,0:T(8,128)S(1)}, f32[1440,128]{1,0:T(8,128)S(1)}, u32[]{:S(2)}, u32[]{:S(2)}) collective-permute-start(f32[1440,128]{1,0:T(8,128)S(1)} %get-tuple-element.36), channel_id=1, source_target_pairs={{0,16},{16,32},{32,48},{48,64},{64,80},{80,96},{96,112},{112,0},{1... | collective-permute-start | bytes 2211848 | tf_op jit(solution)/shard_map/ppermute | solution.py:129
  76.6 11.2 %collective-permute-start.9 = (f32[1440,128]{1,0:T(8,128)S(1)}, f32[1440,128]{1,0:T(8,128)S(1)}, u32[]{:S(2)}, u32[]{:S(2)}) collective-permute-start(f32[1440,128]{1,0:T(8,128)S(1)} %get-tuple-element.38), channel_id=1, source_target_pairs={{0,112},{16,0},{32,16},{48,32},{64,48},{80,64},{96,80},{112,96},{1... | collective-permute-start | bytes 2211848 | tf_op jit(solution)/shard_map/ppermute | solution.py:129
  76.6 16.5 %collective-permute-start.10 = (f32[1152,128]{1,0:T(8,128)S(1)}, f32[1152,128]{1,0:T(8,128)S(1)}, u32[]{:S(2)}, u32[]{:S(2)}) collective-permute-start(f32[1152,128]{1,0:T(8,128)S(1)} %get-tuple-element.39), channel_id=1, source_target_pairs={{0,1},{1,2},{2,3},{3,4},{4,5},{5,6},{6,7},{7,8},{8,9},{9,10},{10,1... | collective-permute-start | bytes 1769480 | tf_op jit(solution)/shard_map/ppermute | solution.py:129
  76.6 16.5 %collective-permute-start.11 = (f32[1152,128]{1,0:T(8,128)S(1)}, f32[1152,128]{1,0:T(8,128)S(1)}, u32[]{:S(2)}, u32[]{:S(2)}) collective-permute-start(f32[1152,128]{1,0:T(8,128)S(1)} %get-tuple-element.40), channel_id=1, source_target_pairs={{0,15},{1,0},{2,1},{3,2},{4,3},{5,4},{6,5},{7,6},{8,7},{9,8},{10,9... | collective-permute-start | bytes 1769480 | tf_op jit(solution)/shard_map/ppermute | solution.py:129
  87.9 22.0 %collective-permute-start.14 = (f32[1440,128]{1,0:T(8,128)S(1)}, f32[1440,128]{1,0:T(8,128)S(1)}, u32[]{:S(2)}, u32[]{:S(2)}) collective-permute-start(f32[1440,128]{1,0:T(8,128)S(1)} %pad_maximum_fusion.2), channel_id=1, source_target_pairs={{0,1},{1,2},{2,3},{3,4},{4,5},{5,6},{6,7},{7,8},{8,9},{9,10},{10,1... | collective-permute-start | bytes 2211848 | tf_op jit(solution)/shard_map/ppermute | solution.py:129
  88.0 21.8 %collective-permute-start.15 = (f32[1440,128]{1,0:T(8,128)S(1)}, f32[1440,128]{1,0:T(8,128)S(1)}, u32[]{:S(2)}, u32[]{:S(2)}) collective-permute-start(f32[1440,128]{1,0:T(8,128)S(1)} %pad_maximum_fusion.3), channel_id=1, source_target_pairs={{0,15},{1,0},{2,1},{3,2},{4,3},{5,4},{6,5},{7,6},{8,7},{9,8},{10,9... | collective-permute-start | bytes 2211848 | tf_op jit(solution)/shard_map/ppermute | solution.py:129
  93.1 14.6 %copy-start.8 = (s32[1,9,24]{2,0,1:T(1,128)S(1)}, s32[1,9,24]{2,0,1:T(1,128)}, u32[]{:S(2)}) copy-start(s32[1,9,24]{2,0,1:T(1,128)} %param.15) | copy-start | bytes 2596
  93.1 14.6 %copy-start.9 = (s32[1,9,24]{2,0,1:T(1,128)S(1)}, s32[1,9,24]{2,0,1:T(1,128)}, u32[]{:S(2)}) copy-start(s32[1,9,24]{2,0,1:T(1,128)} %param.16) | copy-start | bytes 2596
  93.2 11.6 %collective-permute-start.12 = (f32[1152,128]{1,0:T(8,128)S(1)}, f32[1152,128]{1,0:T(8,128)S(1)}, u32[]{:S(2)}, u32[]{:S(2)}) collective-permute-start(f32[1152,128]{1,0:T(8,128)S(1)} %pad_maximum_fusion.4), channel_id=1, source_target_pairs={{0,16},{16,32},{32,48},{48,64},{64,80},{80,96},{96,112},{112,0},{1... | collective-permute-start | bytes 1769480 | tf_op jit(solution)/shard_map/ppermute | solution.py:129
  98.1 11.8 %copy-start.6 = (f32[16384]{0:T(1024)S(1)}, f32[16384]{0:T(1024)}, u32[]{:S(2)}) copy-start(f32[16384]{0:T(1024)} %param.13) | copy-start | bytes 196612
  98.1 11.7 %copy-start.7 = (f32[16384]{0:T(1024)S(1)}, f32[16384]{0:T(1024)}, u32[]{:S(2)}) copy-start(f32[16384]{0:T(1024)} %param.14) | copy-start | bytes 196612
  98.1 9.6 %collective-permute-start.13 = (f32[1152,128]{1,0:T(8,128)S(1)}, f32[1152,128]{1,0:T(8,128)S(1)}, u32[]{:S(2)}, u32[]{:S(2)}) collective-permute-start(f32[1152,128]{1,0:T(8,128)S(1)} %pad_maximum_fusion.5), channel_id=1, source_target_pairs={{0,112},{16,0},{32,16},{48,32},{64,48},{80,64},{96,80},{112,96},{1... | collective-permute-start | bytes 1769480 | tf_op jit(solution)/shard_map/ppermute | solution.py:129
